TPU v7x, 128 devices: a whole 4x4x4 slice. The times are simulated.
128 devices in a mesh: row: 8 (over y, z_hi), col: 16 (over x, z_lo, core).
Axes of the slice: x: 4, y: 4, z: 4 (z_hi: 2, z_lo: 2; z = z_hi * 2 + z_lo), core: 2. Of those that a mesh axis runs over, the one named last changes fastest.
Arguments:
- tokens: bfloat16 [16448, 1024], P('row', 'col'), may hold values from -6 to 6
- qkv_weight: bfloat16 [1024, 3072], P('col', 'row'), may hold values from -2 to 2
- persistent: bfloat16 [16, 2, 1024], P(None, None, 'row'), may hold values from -6 to 6
- cache_pages: bfloat16 [1024, 256, 2, 1024], P('col', None, None, 'row'), may hold values from -48 to 48
- page_table: int32 [64, 16], P('col'), may hold values from 0 to 63, as said below
- cache_len: int32 [64], P('col'), may hold values from 1 to 4096, as said below
- destination: int32 [16], P('col'), may hold values from 0 to 15, each once
- memory_in: float32 [16, 8, 128, 128], P('col', 'row'), may hold values from -6 to 6
- momentum_in: float32 [16, 8, 128, 128], P('col', 'row'), may hold values from -3 to 3
- forget_rate: float32 [16, 8, 16], P('col', 'row'), may hold values from 0.02 to 0.5
- keep_rate: float32 [16, 8, 16], P('col', 'row'), may hold values from 0.3 to 0.95
- learn_rate: float32 [16, 8, 16], P('col', 'row'), may hold values from 0.05 to 1
- decode_memory: float32 [64, 8, 128, 128], P('col', 'row'), may hold values from -6 to 6
Outputs:
- heads_out: bfloat16 [16448, 1024], P('col', 'row')
- memory_out: float32 [16, 8, 128, 128], P('col', 'row')
- momentum_out: float32 [16, 8, 128, 128], P('col', 'row')
Inputs may be any that keep to these rules, and one draw needn't show every extreme that they name: `page_table`: the 4 decode requests of one index of col together name every page of that index's pool once. `cache_len`: some request has exactly 4096. `destination`: each request block once.
All inputs are finite; a program needn't handle non-finite values.
Results may differ from a plain program's by a relative error of at most 0.012.
The roundings to bfloat16 on the way count: a program that leaves them out, or rounds other values in their place, can miss the bound.
Values may be sent and summed in bfloat16 or wider, within the bound.
No kernel may reach another device: no remote copies, remote signals or barrier semaphores. Data moves between devices by JAX's collectives and lax.ppermute only.
A program may use at most 128 MiB of HBM per device.

v0:
```python
import jax
import jax.numpy as jnp
from jax import lax
from jax.sharding import PartitionSpec as P

HD = 128
PERS = 16
MCH = 64
PCH = 1024
DEC_DEV = 4
CACHE = 4096


epsilon = 1e-06
highest = lax.Precision.HIGHEST


def unit_rows(values):
    return values / jnp.sqrt(jnp.sum(values * values, axis=-1, keepdims=True) + epsilon)


def memory_spans(
    query_unit, key_unit, value_rows, memory, momentum, forget_rate, keep_rate, learn_rate
):

    def advance(carry, inputs):
        memory_now, momentum_now = carry
        query_now, key_now, value_now, forget_now, keep_now, learn_now = inputs
        readout = jnp.dot(query_now, memory_now, precision=highest)
        errors = jnp.dot(key_now, memory_now, precision=highest) - value_now
        gradient = jnp.dot(key_now.T, errors, precision=highest) * (2.0 / MCH)
        momentum_now = keep_now * momentum_now - learn_now * gradient
        memory_now = (1.0 - forget_now) * memory_now + momentum_now
        return ((memory_now, momentum_now), readout)

    (memory, momentum), readouts = lax.scan(
        advance,
        (memory, momentum),
        (query_unit, key_unit, value_rows, forget_rate, keep_rate, learn_rate),
    )
    return (readouts, memory, momentum)


def window_attention(query_rows, key_rows, value_rows, persist_key, persist_value):
    scale_factor = query_rows.shape[-1] ** (-0.5)
    inner_score = (
        jnp.einsum("nqd,nkd->nqk", query_rows, key_rows, preferred_element_type=jnp.float32)
        * scale_factor
    )
    length_q = query_rows.shape[1]
    causal = jnp.arange(length_q)[:, None] >= jnp.arange(length_q)[None, :]
    inner_score = jnp.where(causal[None], inner_score, -jnp.inf)
    outer_score = (
        jnp.einsum("nqd,pd->nqp", query_rows, persist_key, preferred_element_type=jnp.float32)
        * scale_factor
    )
    highest_score = jnp.maximum(jnp.max(inner_score, axis=-1), jnp.max(outer_score, axis=-1))[
        ..., None
    ]
    inner_exp = jnp.exp(inner_score - highest_score)
    outer_exp = jnp.exp(outer_score - highest_score)
    totals = jnp.sum(inner_exp, axis=-1, keepdims=True) + jnp.sum(outer_exp, axis=-1, keepdims=True)
    inner_weight = (inner_exp / totals).astype(jnp.bfloat16)
    outer_weight = (outer_exp / totals).astype(jnp.bfloat16)
    attended = jnp.einsum(
        "nqk,nkd->nqd", inner_weight, value_rows, preferred_element_type=jnp.float32
    )
    return attended + jnp.einsum(
        "nqp,pd->nqd", outer_weight, persist_value, preferred_element_type=jnp.float32
    )


def prefill_head(
    token_block, persist_key, persist_value, memory, momentum, forget_rate, keep_rate, learn_rate
):
    spans = token_block.shape[0] // MCH
    query_rows = token_block[:, 0].reshape(spans, MCH, -1)
    key_rows = token_block[:, 1].reshape(spans, MCH, -1)
    value_rows = token_block[:, 2].reshape(spans, MCH, -1)
    readouts, memory, momentum = memory_spans(
        unit_rows(query_rows.astype(jnp.float32)),
        unit_rows(key_rows.astype(jnp.float32)),
        value_rows.astype(jnp.float32),
        memory,
        momentum,
        forget_rate,
        keep_rate,
        learn_rate,
    )
    attended = window_attention(query_rows, key_rows, value_rows, persist_key, persist_value)
    return (
        (attended + readouts).reshape(-1, token_block.shape[-1]).astype(jnp.bfloat16),
        memory,
        momentum,
    )


def decode_block(row_block, cache_block, persist_key, persist_value, memory_now, length_now):
    scale_factor = row_block.shape[-1] ** (-0.5)
    query_row = row_block[:, 0]
    key_row = row_block[:, 1]
    value_row = row_block[:, 2]
    cache_score = (
        jnp.einsum("chd,hd->hc", cache_block[:, 0], query_row, preferred_element_type=jnp.float32)
        * scale_factor
    )
    live_mask = jnp.arange(cache_block.shape[0]) < length_now
    cache_score = jnp.where(live_mask[None, :], cache_score, -jnp.inf)
    own_score = (
        jnp.sum(query_row.astype(jnp.float32) * key_row.astype(jnp.float32), axis=-1) * scale_factor
    )
    persist_score = (
        jnp.einsum("phd,hd->hp", persist_key, query_row, preferred_element_type=jnp.float32)
        * scale_factor
    )
    highest_score = jnp.maximum(
        jnp.maximum(jnp.max(cache_score, axis=-1), own_score), jnp.max(persist_score, axis=-1)
    )
    cache_exp = jnp.exp(cache_score - highest_score[:, None])
    own_exp = jnp.exp(own_score - highest_score)
    persist_exp = jnp.exp(persist_score - highest_score[:, None])
    totals = jnp.sum(cache_exp, axis=-1) + own_exp + jnp.sum(persist_exp, axis=-1)
    cache_weight = (cache_exp / totals[:, None]).astype(jnp.bfloat16)
    own_weight = (own_exp / totals).astype(jnp.bfloat16)
    persist_weight = (persist_exp / totals[:, None]).astype(jnp.bfloat16)
    attended = jnp.einsum(
        "hc,chd->hd", cache_weight, cache_block[:, 1], preferred_element_type=jnp.float32
    )
    attended = attended + own_weight.astype(jnp.float32)[:, None] * value_row.astype(jnp.float32)
    attended = attended + jnp.einsum(
        "hp,phd->hd", persist_weight, persist_value, preferred_element_type=jnp.float32
    )
    readout = jnp.einsum(
        "hd,hde->he", unit_rows(query_row.astype(jnp.float32)), memory_now, precision=highest
    )
    return (attended + readout).astype(jnp.bfloat16)


def shards(
    tokens,
    qkv_weight,
    persistent,
    cache_pages,
    page_table,
    cache_len,
    destination,
    memory_in,
    momentum_in,
    forget_rate,
    keep_rate,
    learn_rate,
    decode_memory,
):
    block_rows = PCH + DEC_DEV
    heads_dev = qkv_weight.shape[1] // (3 * HD)
    gathered = lax.all_gather(tokens, "row", axis=0, tiled=True)
    projected = lax.psum_scatter(
        jnp.dot(gathered, qkv_weight, preferred_element_type=jnp.float32),
        "col",
        scatter_dimension=0,
        tiled=True,
    )
    projected = projected.astype(jnp.bfloat16).reshape(block_rows, heads_dev, 3, HD)
    slot_count = lax.axis_size("col")
    target = (jnp.arange(slot_count, dtype=jnp.int32) == destination[0]).astype(jnp.float32)
    states = jnp.stack([memory_in[0], momentum_in[0]], axis=0)
    outgoing = target[:, None, None, None, None] * states[None]
    arrived = jnp.sum(
        lax.all_to_all(outgoing, "col", split_axis=0, concat_axis=0, tiled=True), axis=0
    )
    persist = persistent.reshape(PERS, 2, heads_dev, HD)
    out_rows, memory_next, momentum_next = prefill_head(
        projected[:PCH, 0],
        persist[:, 0, 0],
        persist[:, 1, 0],
        arrived[0, 0],
        arrived[1, 0],
        forget_rate[0, 0],
        keep_rate[0, 0],
        learn_rate[0, 0],
    )
    prefill_list = [out_rows]
    memory_list = [memory_next]
    momentum_list = [momentum_next]
    caches = cache_pages[page_table.reshape(-1)].reshape(DEC_DEV, CACHE, 2, heads_dev, HD)
    decode_map = jax.vmap(decode_block, in_axes=(0, 0, None, None, 0, 0))
    decode_out = decode_map(
        projected[PCH:], caches, persist[:, 0], persist[:, 1], decode_memory, cache_len
    )
    prefill_out = jnp.stack(prefill_list, axis=1)
    heads_out = jnp.concatenate([prefill_out, decode_out], axis=0).reshape(
        block_rows, heads_dev * HD
    )
    return (heads_out, jnp.stack(memory_list, axis=0)[None], jnp.stack(momentum_list, axis=0)[None])


def solution(mesh):
    placed = (
        P("row", "col"),
        P("col", "row"),
        P(None, None, "row"),
        P("col", None, None, "row"),
        P("col", None),
        P("col"),
        P("col"),
        P("col", "row", None, None),
        P("col", "row", None, None),
        P("col", "row", None),
        P("col", "row", None),
        P("col", "row", None),
        P("col", "row", None, None),
    )
    return jax.shard_map(
        shards,
        mesh=mesh,
        in_specs=placed,
        out_specs=(P("col", "row"), P("col", "row", None, None), P("col", "row", None, None)),
        check_vma=False,
    )
```

profile of v0, /device:TPU:1, one launch (start us, length us, event | category | flops | bytes accessed | tf_op | source)
XLA Modules:
  0.0 477.1 jit_solution(6140073066499957147)
XLA Ops:
  9.5 1.6 broadcast_multiply_fusion
  11.1 7.2 %all-to-all-start = ((f32[16,2,1,128,128]{4,3,2,1,0:T(8,128)}), f32[16,2,1,128,128]{4,3,2,1,0:T(8,128)S(1)}, u32[]{:S(2)}, u32[]{:S(2)}) async-start(f32[16,2,1,128,128]{4,3,2,1,0:T(8,128)} %broadcast_multiply_fusion), calls=%async_computation | async-start | bytes 4194304 | tf_op jit(solution)/shard_map/all_to_all | solution.py:169
  18.4 22.1 %gather_fusion = bf16[64,256,2,128]{3,2,1,0:T(2,128)(2,1)} fusion(bf16[64,256,2,128]{3,2,1,0:T(2,128)(2,1)} %param.18, s32[1024]{0:T(1024)S(1)} %pad_clamp_fusion), kind=kCustom, calls=%fused_computation | custom fusion | bytes 16777472 | tf_op jit(solution)/shard_map/gather | solution.py:185
  40.5 8.8 %copy.43 = bf16[64,256,2,128]{3,1,0,2:T(8,128)(2,1)} copy(bf16[64,256,2,128]{3,2,1,0:T(2,128)(2,1)} %gather_fusion) | data formatting | bytes 16777216 | tf_op jit(solution)/shard_map/gather | solution.py:185
  50.7 34.3 %all-gather.3.cloned.1.call-done = bf16[8,2056,64]{1,2,0:T(8,128)(2,1)} async-done(((bf16[1,2056,64]{1,2,0:T(8,128)(2,1)}), bf16[8,2056,64]{1,2,0:T(8,128)(2,1)}) %all-gather.3.cloned.1.call-update) | async-done | bytes 2105360 | tf_op jit(solution)/shard_map/all_gather | solution.py:156
  85.0 2.9 copy.36
  87.9 3.0 reshape.345
  90.9 13.4 %fusion.56 = f32[16448,384]{1,0:T(8,128)} fusion(bf16[16448,64]{0,1:T(8,128)(2,1)} %reshape.345, bf16[64,384]{1,0:T(8,128)(2,1)S(1)} %copy-done.4), kind=kOutput, calls=%fused_computation.104 | convolution fusion | flops 808452096 | bytes 27418624 | tf_op jit(solution)/shard_map/dot_general | solution.py:158
  104.3 271.0 %fusion = f32[1040,384]{1,0:T(8,128)S(1)} fusion(f32[16448,384]{1,0:T(8,128)} %fusion.56), kind=kCustom, calls=%all-reduce-scatter | all-reduce-scatter fusion | flops 6389761 | bytes 26862080
  375.3 4.6 collective-permute-start
  379.9 1.8 collective-permute-done
  381.7 2.1 concatenate.4
  386.8 1.1 fusion.23
  388.5 73.0 %while.14 = (s32[]{:T(128)}, f32[128,128]{1,0:T(8,128)S(1)}, f32[128,128]{1,0:T(8,128)S(1)}, f32[16,64,128]{2,1,0:T(8,128)S(1)}, f32[16]{0:T(128)S(1)}, /*index=...) while((s32[]{:T(128)}, f32[128,128]{1,0:T(8,128)S(1)}, ...), condition=%wide.region_9.10_spmd, body=%wide.region_8.9_spmd.sunk | while | flops 37838852 | bytes 624841 | solution.py:36
  392.1 1.0 multiply_add_fusion.2
  396.7 1.0 multiply_add_fusion.2
  405.8 1.0 multiply_add_fusion.2
  414.9 1.0 multiply_add_fusion.2
  428.6 1.0 multiply_add_fusion.2
  433.2 1.0 multiply_add_fusion.2
  451.4 1.0 multiply_add_fusion.2
  456.0 1.0 multiply_add_fusion.2
  461.6 3.4 fusion.13
  465.8 2.8 fusion.12
  (164 shorter events, 51.8 us)
Async XLA Ops:
  7.2 461.9 %copy-start = (f32[4,1,128,128]{3,2,1,0:T(8,128)S(1)}, f32[4,1,128,128]{3,2,1,0:T(8,128)}, u32[]{:S(2)}) copy-start(f32[4,1,128,128]{3,2,1,0:T(8,128)} %param.27) | copy-start | bytes 786436
  7.2 11.1 %copy-start.5 = (bf16[16,2,128]{2,1,0:T(2,128)(2,1)S(1)}, bf16[16,2,128]{2,1,0:T(2,128)(2,1)}, u32[]{:S(2)}) copy-start(bf16[16,2,128]{2,1,0:T(2,128)(2,1)} %param.17) | copy-start | bytes 24580
  7.2 11.1 %copy-start.6 = (s32[4,16]{1,0:T(4,128)S(1)}, s32[4,16]{1,0:T(4,128)}, u32[]{:S(2)}) copy-start(s32[4,16]{1,0:T(4,128)} %param.19) | copy-start | bytes 772
  7.2 77.8 %all-gather.3.cloned.1.call-start = ((), (), s32[]{:S(2)}) async-start(), calls=%async_computation.1 | async-start | bytes 2506752 | tf_op jit(solution)/shard_map/all_gather | solution.py:156
  11.1 39.5 %all-to-all-start = ((f32[16,2,1,128,128]{4,3,2,1,0:T(8,128)}), f32[16,2,1,128,128]{4,3,2,1,0:T(8,128)S(1)}, u32[]{:S(2)}, u32[]{:S(2)}) async-start(f32[16,2,1,128,128]{4,3,2,1,0:T(8,128)} %broadcast_multiply_fusion), calls=%async_computation | async-start | bytes 4194304 | tf_op jit(solution)/shard_map/all_to_all | solution.py:169
  40.5 8.8 %copy-start.8 = (u32[128]{0:T(128)S(1)}, u32[128]{0:T(128)}, u32[]{:S(2)}) copy-start(u32[128]{0:T(128)} %constant.47) | copy-start | bytes 1540
  50.7 40.2 %copy-start.4 = (bf16[64,384]{1,0:T(8,128)(2,1)S(1)}, bf16[64,384]{1,0:T(8,128)(2,1)}, u32[]{:S(2)}) copy-start(bf16[64,384]{1,0:T(8,128)(2,1)} %param.16) | copy-start | bytes 147460
  375.3 6.4 %collective-permute-start = (bf16[180,384]{1,0:T(8,128)(2,1)S(1)}, bf16[180,384]{1,0:T(8,128)(2,1)}, u32[]{:S(2)}, u32[]{:S(2)}) collective-permute-start(bf16[180,384]{1,0:T(8,128)(2,1)S(1)} %slice.81), channel_id=1, source_target_pairs={{0,1},{1,2},{2,3},{3,4},{4,5},{5,6},{6,7},{7,8},{8,9},{9,10},{10,1... | collective-permute-start | bytes 414728
  385.2 3.3 copy-start.9
  385.2 3.3 copy-start.10
  385.2 3.3 copy-start.11
  388.5 76.5 %copy-start.7 = (s32[4]{0:T(128)S(1)}, s32[4]{0:T(128)}, u32[]{:S(2)}) copy-start(s32[4]{0:T(128)} %param.20) | copy-start | bytes 52
  461.5 7.1 %copy-start.1 = (f32[128,128]{1,0:T(8,128)}, f32[128,128]{1,0:T(8,128)S(1)}, u32[]{:S(2)}) copy-start(f32[128,128]{1,0:T(8,128)S(1)} %get-tuple-element.58) | copy-start | bytes 196612
  461.6 7.1 %copy-start.2 = (f32[128,128]{1,0:T(8,128)}, f32[128,128]{1,0:T(8,128)S(1)}, u32[]{:S(2)}) copy-start(f32[128,128]{1,0:T(8,128)S(1)} %get-tuple-element.59) | copy-start | bytes 196612
  461.6 7.1 %copy-start.3 = (f32[16,64,128]{2,1,0:T(8,128)S(1)}, f32[16,64,128]{2,1,0:T(8,128)}, u32[]{:S(2)}) copy-start(f32[16,64,128]{2,1,0:T(8,128)} %fusion.23) | copy-start | bytes 1572868
Sparse Core Ops, SparseCore 0:
  10.3 74.6 all-gather.2
where the time goes:
time: 478 us; the launch traced here: 477 us
  blocking collectives  271 us (57%)
  local copies, waits for them, and re-layouts  70.9 us (15%)
  matrix products  44.4 us (9%)
  waiting for transfers between devices  36.8 us (8%)
  loops' own time  21.4 us (4%)
  between operations  15.7 us (3%)
  starting transfers between devices  11.8 us (2%)
  other arithmetic  5.13 us (1%)
    unnamed x1, blocking collectives  271 us
    all_gather x1, waiting for transfers between devices, shards(): gathered = lax.all_gather(tokens, 'row', axis=0, tiled=True)  34.3 us
    gather x2, local copies, waits for them, and re-layouts, shards(): cache_pages[page_table.reshape(-1)]  30.9 us
    dynamic_slice x48, local copies, waits for them, and re-layouts, memory_spans(): lax.scan(advance, (memory, momentum), (query_unit, key_unit, value_rows,...  29.6 us
    another operation x1, loops' own time, memory_spans(): lax.scan(advance, (memory, momentum), (query_unit, key_unit, value_rows,...  21.4 us
    dot_general x16, matrix products, advance(): gradient = jnp.dot(key_now.T, errors, precision=highest) * (2.0 / MCH)  16 us
    dot_general x1, matrix products, shards(): jnp.dot(gathered, qkv_weight, preferred_element_type=jnp.float32)  13.4 us
  transfers between devices with their start and end apart: 3, of which 2 were waited for; matrix products, arithmetic and copies ran while one was open for 7% of the time, Pallas kernels for 0%

commit v1 on v0

v1 whole, which is shorter than its diff:
```python
import jax
import jax.numpy as jnp
from jax import lax
from jax.experimental import pallas as pl
from jax.experimental.pallas import tpu as pltpu
from jax.sharding import PartitionSpec as P

HD = 128
PERS = 16
MCH = 64
PCH = 1024
DEC_DEV = 4
CACHE = 4096
PAGE = 256
PAGES = CACHE // PAGE
ROWS = PCH + DEC_DEV
PADDED = PCH + 16

F32 = jnp.float32
BF16 = jnp.bfloat16
EPSILON = 1e-6
SCALE = HD**-0.5


def device_at(x, y, z_hi, z_lo, core):
    return (2 * y + z_hi) * 16 + 4 * x + 2 * z_lo + core


def moves(target):
    pairs = []
    for x in range(4):
        for y in range(4):
            for z_hi in range(2):
                for z_lo in range(2):
                    for core in range(2):
                        here = (x, y, z_hi, z_lo, core)
                        pairs.append((device_at(*here), device_at(*target(*here))))
    return pairs


def permute(values, target):
    return lax.ppermute(values, ("row", "col"), moves(target))


def dot_f32(left, right):
    return lax.dot_general(left, right, (((1,), (0,)), ((), ())), preferred_element_type=F32)


def dot_rows(left, right):
    return lax.dot_general(left, right, (((1,), (1,)), ((), ())), preferred_element_type=F32)


def dot_turned(left, right):
    return lax.dot_general(left, right, (((0,), (0,)), ((), ())), preferred_element_type=F32)


def two_parts(values):
    high = values.astype(BF16)
    return jnp.concatenate([high, (values - high.astype(F32)).astype(BF16)], axis=0)


def inverse_norm(rows):
    wide = rows.astype(F32)
    return lax.rsqrt(jnp.sum(wide * wide, axis=-1, keepdims=True) + EPSILON)


def layer_kernel(
    table_ref,
    length_ref,
    forget_ref,
    keep_ref,
    learn_ref,
    token_ref,
    weight_ref,
    persist_key_ref,
    persist_value_ref,
    state_ref,
    decode_memory_ref,
    page_ref,
    out_ref,
    memory_ref,
    momentum_ref,
    projected,
    cache,
    score,
    arrival,
):
    for request in range(DEC_DEV):
        for place in range(PAGES):
            pltpu.make_async_copy(
                page_ref.at[table_ref[request * PAGES + place]],
                cache.at[request, pl.ds(place * 2 * PAGE, 2 * PAGE)],
                arrival.at[request],
            ).start()

    total = None
    for chunk in range(4):
        rows = jnp.concatenate([token_ref[2 * chunk], token_ref[2 * chunk + 1]], axis=1)
        part = dot_f32(rows, weight_ref[256 * chunk : 256 * chunk + 256, :])
        total = part if total is None else total + part
    projected[...] = total.astype(BF16)

    persist_key = persist_key_ref[...]
    persist_value = persist_value_ref[...]
    blank = jnp.zeros((HD - MCH - PERS, HD), BF16)
    row_at = lax.broadcasted_iota(jnp.int32, (MCH, HD), 0)
    column_at = lax.broadcasted_iota(jnp.int32, (MCH, HD), 1)
    visible = (column_at <= row_at) | ((column_at >= MCH) & (column_at < MCH + PERS))

    memory = jnp.concatenate([state_ref[s, 0:8, :] for s in range(16)], axis=0)
    momentum = jnp.concatenate([state_ref[s, 8:16, :] for s in range(16)], axis=0)
    for block in range(PCH // MCH):
        here = slice(block * MCH, block * MCH + MCH)
        query = projected[here, 0:HD]
        key = projected[here, HD : 2 * HD]
        value = projected[here, 2 * HD : 3 * HD]
        query_scale = inverse_norm(query)
        key_scale = inverse_norm(key)
        left = jnp.concatenate(
            [jnp.concatenate([query, query], axis=1), jnp.concatenate([key, key], axis=1)], axis=0
        )
        reads = dot_f32(left, two_parts(memory))
        errors = reads[MCH:] * key_scale - value.astype(F32)
        errors = errors * (key_scale * (2.0 / MCH))
        gradient = dot_turned(jnp.concatenate([key, key], axis=0), two_parts(errors))
        momentum = keep_ref[block] * momentum - learn_ref[block] * gradient
        memory = (1.0 - forget_ref[block]) * memory + momentum

        keys = jnp.concatenate([key, persist_key, blank], axis=0)
        values = jnp.concatenate([value, persist_value, blank], axis=0)
        scores = jnp.where(visible, dot_rows(query, keys) * SCALE, -jnp.inf)
        powers = jnp.exp(scores - jnp.max(scores, axis=-1, keepdims=True))
        weights = (powers / jnp.sum(powers, axis=-1, keepdims=True)).astype(BF16)
        out_ref[here, :] = (dot_f32(weights, values) + reads[:MCH] * query_scale).astype(BF16)
    memory_ref[...] = memory
    momentum_ref[...] = momentum

    query = projected[PCH:PADDED, 0:HD]
    key = projected[PCH:PADDED, HD : 2 * HD]
    value = projected[PCH:PADDED, 2 * HD : 3 * HD]
    row = lax.broadcasted_iota(jnp.int32, (16, 1), 0)
    length = jnp.zeros((16, 1), jnp.int32)
    for request in range(DEC_DEV):
        pltpu.make_async_copy(cache.at[request], cache.at[request], arrival.at[request]).wait()
        length = jnp.where(row == request, length_ref[request], length)
    for place in range(PAGES):
        span = slice(place * 2 * PAGE, place * 2 * PAGE + 2 * PAGE)
        found = dot_rows(query, cache[0, span, :])
        for request in range(1, DEC_DEV):
            found = jnp.where(row == request, dot_rows(query, cache[request, span, :]), found)
        column = lax.broadcasted_iota(jnp.int32, (16, 2 * PAGE), 1)
        live = ((column & 1) == 0) & ((column >> 1) + place * PAGE < length)
        score[:, span] = jnp.where(live, found * SCALE, -jnp.inf)
    own_score = jnp.sum(query.astype(F32) * key.astype(F32), axis=-1, keepdims=True) * SCALE
    persist_score = dot_rows(query, persist_key) * SCALE
    cache_score = score[...]
    largest = jnp.maximum(
        jnp.maximum(jnp.max(cache_score, axis=-1, keepdims=True), own_score),
        jnp.max(persist_score, axis=-1, keepdims=True),
    )
    cache_power = jnp.exp(cache_score - largest)
    own_power = jnp.exp(own_score - largest)
    persist_power = jnp.exp(persist_score - largest)
    totals = (
        jnp.sum(cache_power, axis=-1, keepdims=True)
        + own_power
        + jnp.sum(persist_power, axis=-1, keepdims=True)
    )
    share = 1.0 / totals
    cache_weight = pltpu.roll(cache_power * share, 1, 1).astype(BF16)
    attended = jnp.zeros((16, HD), F32)
    for request in range(DEC_DEV):
        attended = jnp.where(row == request, dot_f32(cache_weight, cache[request]), attended)
    own_weight = (own_power * share).astype(BF16).astype(F32)
    attended = attended + own_weight * value.astype(F32)
    attended = attended + dot_f32((persist_power * share).astype(BF16), persist_value)
    twice = jnp.concatenate([query, query], axis=1)
    readout = jnp.zeros((16, HD), F32)
    for request in range(DEC_DEV):
        readout = jnp.where(row == request, dot_f32(twice, two_parts(decode_memory_ref[request])), readout)
    result = (attended + readout * inverse_norm(query)).astype(BF16)
    out_ref[PCH:ROWS, :] = result[:DEC_DEV]


def layer(table, length, forget, keep, learn, chunks, weight, persist, state, decode_memory, pages):
    in_smem = pl.BlockSpec(memory_space=pltpu.SMEM)
    in_vmem = pl.BlockSpec(memory_space=pltpu.VMEM)
    return pl.pallas_call(
        layer_kernel,
        out_shape=(
            jax.ShapeDtypeStruct((ROWS, HD), BF16),
            jax.ShapeDtypeStruct((HD, HD), F32),
            jax.ShapeDtypeStruct((HD, HD), F32),
        ),
        in_specs=[in_smem] * 5 + [in_vmem] * 6 + [pl.BlockSpec(memory_space=pl.ANY)],
        out_specs=(in_vmem, in_vmem, in_vmem),
        scratch_shapes=[
            pltpu.VMEM((PADDED, 3 * HD), BF16),
            pltpu.VMEM((DEC_DEV, 2 * CACHE, HD), BF16),
            pltpu.VMEM((16, 2 * CACHE), F32),
            pltpu.SemaphoreType.DMA((DEC_DEV,)),
        ],
        compiler_params=pltpu.CompilerParams(vmem_limit_bytes=40 * 2**20),
    )(
        table.reshape(-1),
        length,
        forget.reshape(-1),
        keep.reshape(-1),
        learn.reshape(-1),
        chunks,
        weight,
        persist[:, 0],
        persist[:, 1],
        state,
        decode_memory.reshape(DEC_DEV, HD, HD),
        pages.reshape(DEC_DEV * PAGES, 2 * PAGE, HD),
    )


def route_states(memory_in, momentum_in, destination):
    slots = 16
    mark = jnp.broadcast_to(destination.astype(F32).reshape(1, 1, 1), (slots, 8, HD))
    pieces = jnp.concatenate(
        [memory_in.reshape(slots, 8, HD), momentum_in.reshape(slots, 8, HD), mark], axis=1
    )
    spread = lax.all_to_all(pieces, "col", split_axis=0, concat_axis=0, tiled=True)
    target = spread[:, 16, 0].astype(jnp.int32)
    chosen = target[None, :] == jnp.arange(slots, dtype=jnp.int32)[:, None]
    ordered = jnp.sum(
        jnp.where(chosen[:, :, None, None], spread[None, :, :16, :], 0.0), axis=1
    )
    return lax.all_to_all(ordered, "col", split_axis=0, concat_axis=0, tiled=True)


def shards(
    tokens,
    qkv_weight,
    persistent,
    cache_pages,
    page_table,
    cache_len,
    destination,
    memory_in,
    momentum_in,
    forget_rate,
    keep_rate,
    learn_rate,
    decode_memory,
):
    core = lax.axis_index("col") % 2
    halves = tokens.reshape(2, ROWS, tokens.shape[1])
    kept = lax.dynamic_index_in_dim(halves, core, 0, keepdims=False)
    sent = lax.dynamic_index_in_dim(halves, 1 - core, 0, keepdims=False)
    came = permute(sent, lambda x, y, z_hi, z_lo, core: (x, y, z_hi, z_lo, 1 - core))
    own = jnp.concatenate(
        [jnp.where(core == 0, kept, came), jnp.where(core == 0, came, kept)], axis=1
    )
    own = jnp.pad(own, ((0, PADDED - ROWS), (0, 0)))
    turned = permute(own, lambda x, y, z_hi, z_lo, core: (y, x, z_lo, z_hi, core))
    chunks = lax.all_to_all(
        jnp.broadcast_to(turned[None], (8, PADDED, HD)),
        "row",
        split_axis=0,
        concat_axis=0,
        tiled=True,
    )
    weight = lax.all_gather(qkv_weight, "col", axis=0, tiled=True)
    state = route_states(memory_in, momentum_in, destination)
    heads_out, memory, momentum = layer(
        page_table,
        cache_len,
        forget_rate,
        keep_rate,
        learn_rate,
        chunks,
        weight,
        persistent,
        state,
        decode_memory,
        cache_pages,
    )
    return heads_out, memory[None, None], momentum[None, None]


def solution(mesh):
    placed = (
        P("row", "col"),
        P("col", "row"),
        P(None, None, "row"),
        P("col", None, None, "row"),
        P("col", None),
        P("col"),
        P("col"),
        P("col", "row", None, None),
        P("col", "row", None, None),
        P("col", "row", None),
        P("col", "row", None),
        P("col", "row", None),
        P("col", "row", None, None),
    )
    return jax.shard_map(
        shards,
        mesh=mesh,
        in_specs=placed,
        out_specs=(P("col", "row"), P("col", "row", None, None), P("col", "row", None, None)),
        check_vma=False,
    )
```

time: 478 us -> 110 us (0.23)
  blocking collectives: 271 us -> 57.4 us
  local copies, waits for them, and re-layouts: 70.9 us -> 7.65 us
  matrix products: 44.4 us -> 0 us
  waiting for transfers between devices: 36.8 us -> 5.56 us
  Pallas kernels: 0 us -> 22.7 us
  loops' own time: 21.4 us -> 0 us
  between operations: 15.7 us -> 1.51 us
    unnamed x1 -> x0, blocking collectives: 271 us -> none
    dot_general x58 -> x0, matrix products: 44.4 us -> none  [the longest x16 16 us: advance(): gradient = jnp.dot(key_now.T, errors, precision=highest) * (2.0 / MCH)]
    all_gather x0 -> x1, blocking collectives: none -> 41.4 us  [shards(): weight = lax.all_gather(qkv_weight, 'col', axis=0, tiled=True)]
    all_gather x1 -> x0, waiting for transfers between devices: 34.3 us -> none  [shards(): gathered = lax.all_gather(tokens, 'row', axis=0, tiled=True)]
    gather x2 -> x0, local copies, waits for them, and re-layouts: 30.9 us -> none  [shards(): cache_pages[page_table.reshape(-1)]]
    dynamic_slice x48 -> x3, local copies, waits for them, and re-layouts: 29.6 us -> 1.13 us  [the longest x2 0.87 us: shards(): kept = lax.dynamic_index_in_dim(halves, core, 0, keepdims=False)]
    pallas_call x0 -> x1, Pallas kernels: none -> 22.7 us  [layer(): pl.pallas_call(layer_kernel, out_shape=(jax.ShapeDtypeStruct((ROWS, HD),...]
    another operation x1 -> x0, loops' own time: 21.4 us -> none  [memory_spans(): lax.scan(advance, (memory, momentum), (query_unit, key_unit, value_rows,...]
  transfers between devices with their start and end apart: 3 -> 4, of which waited for: 2 -> 1; matrix products, arithmetic and copies ran while one was open for 7% -> 2% of each run, Pallas kernels for 0% -> 0%
where the time goes in v1:
time: 110 us; the launch traced here: 109 us
  blocking collectives  57.4 us (52%)
  Pallas kernels  22.7 us (21%)
  starting transfers between devices  12.7 us (12%)
  local copies, waits for them, and re-layouts  7.65 us (7%)
  waiting for transfers between devices  5.56 us (5%)
  other arithmetic  1.74 us (2%)
  between operations  1.51 us (1%)
    all_gather x1, blocking collectives, shards(): weight = lax.all_gather(qkv_weight, 'col', axis=0, tiled=True)  41.4 us
    pallas_call x1, Pallas kernels, layer(): pl.pallas_call(layer_kernel, out_shape=(jax.ShapeDtypeStruct((ROWS, HD),...  22.7 us
    all_to_all x1, blocking collectives, route_states(): lax.all_to_all(ordered, 'col', split_axis=0, concat_axis=0, tiled=True)  16.1 us
    all_to_all x1, starting transfers between devices, route_states(): lax.all_to_all(pieces, 'col', split_axis=0, concat_axis=0, tiled=True)  5.86 us
    all_to_all x1, waiting for transfers between devices, route_states(): lax.all_to_all(pieces, 'col', split_axis=0, concat_axis=0, tiled=True)  5.55 us
    all_to_all x1, starting transfers between devices, shards(): lax.all_to_all(jnp.broadcast_to(turned[None], (8, PADDED, HD)), 'row', sp...  4.61 us
    unnamed x22, local copies, waits for them, and re-layouts  3.43 us
  transfers between devices with their start and end apart: 4, of which 1 were waited for; matrix products, arithmetic and copies ran while one was open for 2% of the time, Pallas kernels for 0%

profile of v1, /device:TPU:1, one launch (start us, length us, event | category | flops | bytes accessed | tf_op | source)
XLA Modules:
  0.0 109.3 jit_solution(16410245928480468129)
XLA Ops:
  0.7 1.3 %reshape.66 = bf16[2,1028,64]{1,0,2:T(2,128)(2,1)S(1)} reshape(bf16[2056,64]{0,1:T(8,128)(2,1)} %param.13) | data formatting | bytes 526336 | tf_op jit(solution)/shard_map/reshape | solution.py:251
  2.0 0.6 constant_dynamic-slice_fusion.1
  2.6 0.3 copy.32
  2.9 1.5 %collective-permute-start = (bf16[1028,64]{1,0:T(8,128)(2,1)S(1)}, bf16[1028,64]{1,0:T(8,128)(2,1)S(1)}, u32[]{:S(2)}, u32[]{:S(2)}) collective-permute-start(bf16[1028,64]{1,0:T(8,128)(2,1)S(1)} %bitcast.25), channel_id=1, source_target_pairs={{0,1},{1,0},{2,3},{3,2},{16,17},{17,16},{18,19},{19,18},{32,33},{3... | collective-permute-start | bytes 394760 | tf_op jit(solution)/shard_map/ppermute | solution.py:42
  5.0 0.1 pad.7.clone
  5.1 0.8 maximum_maximum_fusion
  5.9 5.9 %all-to-all-start.1 = ((f32[16,24,128]{2,1,0:T(8,128)}), f32[16,24,128]{2,1,0:T(8,128)S(1)}, u32[]{:S(2)}, u32[]{:S(2)}) async-start(f32[16,24,128]{2,1,0:T(8,128)} %maximum_maximum_fusion), calls=%async_computation.1 | async-start | bytes 393216 | tf_op jit(solution)/shard_map/all_to_all | solution.py:226
  11.7 0.3 copy.31
  12.0 0.1 bitcast_select_fusion.1
  12.1 0.2 fusion.2
  12.3 0.7 collective-permute-start.1
  13.0 5.6 %all-to-all-done.1 = f32[16,24,128]{2,1,0:T(8,128)S(1)} async-done(((f32[16,24,128]{2,1,0:T(8,128)}), f32[16,24,128]{2,1,0:T(8,128)S(1)}, u32[]{:S(2)}, u32[]{:S(2)}) %all-to-all-start.1) | async-done | bytes 196640 | tf_op jit(solution)/shard_map/all_to_all | solution.py:226
  18.5 0.4 fusion.3
  18.9 0.3 select_reduce_fusion
  19.3 16.1 %all_to_all.15.state_ref = f32[16,16,128]{2,1,0:T(8,128)S(1)} all-to-all(f32[16,16,128]{2,1,0:T(8,128)S(1)} %select_reduce_fusion), channel_id=1, replica_groups=mesh['row'=8,'col'=16] {'col'}, dimensions={0} | all-to-all | bytes 262144 | tf_op jit(solution)/shard_map/all_to_all | solution.py:232
  35.3 1.6 %broadcast_in_dim.43 = bf16[8,1040,128]{2,1,0:T(8,128)(2,1)} broadcast(bf16[1040,128]{1,0:T(8,128)(2,1)S(1)} %collective-permute-done.1), dimensions={1,2} | broadcast | bytes 2396160 | tf_op jit(solution)/shard_map/broadcast_in_dim | solution.py:261
  37.0 0.0 copy-start.2
  37.0 0.0 copy-start.5
  37.0 4.6 %all-to-all-start = ((bf16[8,1040,128]{2,1,0:T(8,128)(2,1)}), bf16[8,1040,128]{2,1,0:T(8,128)(2,1)S(1)}, u32[]{:S(2)}, u32[]{:S(2)}) async-start(bf16[8,1040,128]{2,1,0:T(8,128)(2,1)} %broadcast_in_dim.43), calls=%async_computation | async-start | bytes 4259840 | tf_op jit(solution)/shard_map/all_to_all | solution.py:260
  41.6 0.1 reshape.62.table_ref
  41.8 41.4 %all_gather.3.weight_ref = bf16[1024,384]{1,0:T(8,128)(2,1)S(1)} all-gather(bf16[64,384]{1,0:T(8,128)(2,1)S(1)} %copy-done.8), channel_id=1, replica_groups=mesh['row'=8,'col'=16] {'col'}, dimensions={0}, use_global_device_ids=true | all-gather | bytes 835584 | tf_op jit(solution)/shard_map/all_gather | solution.py:267
  83.2 0.0 copy-start
  83.2 3.4 %copy-done = bf16[64,256,2,128]{3,2,1,0:T(2,128)(2,1)S(1)} copy-done((bf16[64,256,2,128]{3,2,1,0:T(2,128)(2,1)S(1)}, bf16[64,256,2,128]{3,2,1,0:T(2,128)(2,1)}, u32[]{:S(2)}) %copy-start) | copy-done | bytes 8388632
  86.6 22.7 %shard_map.148 = (bf16[1028,128]{1,0:T(8,128)(2,1)}, f32[128,128]{1,0:T(8,128)}, f32[128,128]{1,0:T(8,128)}) custom-call(s32[64]{0:T(128)S(1)} %reshape.62.table_ref, s32[4]{0:T(128)S(1)} %copy-done.2, f32[16]{0:T(128)S(1)} %bitcast.22, f32[16]{0:T(128)S(1)} %bitcast.23, f32[16]{0:T(128)S(1)} %bitcast.24, bf16[8,1040,128]{2,1,0:T(8,128)(2,1)S(1)} %all-to-all-done.token_ref, ...), custom_call_target="tpu_custom_call" | custom-call | tf_op jit(solution)/shard_map/pallas_call | solution.py:188
  (26 shorter events, 0.1 us)
Async XLA Ops:
  0.6 4.5 %copy-start.7 = (f32[1,1,128,128]{3,2,1,0:T(8,128)S(1)}, f32[1,1,128,128]{3,2,1,0:T(8,128)}, u32[]{:S(2)}) copy-start(f32[1,1,128,128]{3,2,1,0:T(8,128)} %param.20) | copy-start | bytes 196612
  0.6 4.5 %copy-start.6 = (f32[1,1,128,128]{3,2,1,0:T(8,128)S(1)}, f32[1,1,128,128]{3,2,1,0:T(8,128)}, u32[]{:S(2)}) copy-start(f32[1,1,128,128]{3,2,1,0:T(8,128)} %param.21) | copy-start | bytes 196612
  2.9 9.1 %collective-permute-start = (bf16[1028,64]{1,0:T(8,128)(2,1)S(1)}, bf16[1028,64]{1,0:T(8,128)(2,1)S(1)}, u32[]{:S(2)}, u32[]{:S(2)}) collective-permute-start(bf16[1028,64]{1,0:T(8,128)(2,1)S(1)} %bitcast.25), channel_id=1, source_target_pairs={{0,1},{1,0},{2,3},{3,2},{16,17},{17,16},{18,19},{19,18},{32,33},{3... | collective-permute-start | bytes 394760 | tf_op jit(solution)/shard_map/ppermute | solution.py:42
  5.9 12.7 %all-to-all-start.1 = ((f32[16,24,128]{2,1,0:T(8,128)}), f32[16,24,128]{2,1,0:T(8,128)S(1)}, u32[]{:S(2)}, u32[]{:S(2)}) async-start(f32[16,24,128]{2,1,0:T(8,128)} %maximum_maximum_fusion), calls=%async_computation.1 | async-start | bytes 393216 | tf_op jit(solution)/shard_map/all_to_all | solution.py:226
  12.3 23.1 %collective-permute-start.1 = (bf16[1040,128]{1,0:T(8,128)(2,1)S(1)}, bf16[1040,128]{1,0:T(8,128)(2,1)S(1)}, u32[]{:S(2)}, u32[]{:S(2)}) collective-permute-start(bf16[1040,128]{1,0:T(8,128)(2,1)S(1)} %fusion.2), channel_id=1, source_target_pairs={{0,0},{1,1},{2,16},{3,17},{16,2},{17,3},{18,18},{19,19},{32,4},{33... | collective-permute-start | bytes 798728 | tf_op jit(solution)/shard_map/ppermute | solution.py:42
  36.9 4.7 %copy-start.10 = (s32[4,16]{1,0:T(4,128)S(1)}, s32[4,16]{1,0:T(4,128)}, u32[]{:S(2)}) copy-start(s32[4,16]{1,0:T(4,128)} %param.17) | copy-start | bytes 772
  36.9 4.8 %copy-start.9 = (bf16[16,2,128]{2,1,0:T(2,128)(2,1)S(1)}, bf16[16,2,128]{2,1,0:T(2,128)(2,1)}, u32[]{:S(2)}) copy-start(bf16[16,2,128]{2,1,0:T(2,128)(2,1)} %param.15) | copy-start | bytes 24580
  36.9 4.8 %copy-start.8 = (bf16[64,384]{1,0:T(8,128)(2,1)S(1)}, bf16[64,384]{1,0:T(8,128)(2,1)}, u32[]{:S(2)}) copy-start(bf16[64,384]{1,0:T(8,128)(2,1)} %param.14) | copy-start | bytes 147460
  37.0 46.2 %copy-start.1 = (f32[4,1,128,128]{3,2,1,0:T(8,128)S(1)}, f32[4,1,128,128]{3,2,1,0:T(8,128)}, u32[]{:S(2)}) copy-start(f32[4,1,128,128]{3,2,1,0:T(8,128)} %param.25) | copy-start | bytes 786436
  37.0 46.2 %copy-start.2 = (s32[4]{0:T(128)S(1)}, s32[4]{0:T(128)}, u32[]{:S(2)}) copy-start(s32[4]{0:T(128)} %length_ref.1) | copy-start | bytes 52
  37.0 46.2 %copy-start.3 = (f32[1,1,16]{2,1,0:T(1,128)S(1)}, f32[1,1,16]{2,1,0:T(1,128)}, u32[]{:S(2)}) copy-start(f32[1,1,16]{2,1,0:T(1,128)} %param.22) | copy-start | bytes 196
  37.0 46.2 %copy-start.4 = (f32[1,1,16]{2,1,0:T(1,128)S(1)}, f32[1,1,16]{2,1,0:T(1,128)}, u32[]{:S(2)}) copy-start(f32[1,1,16]{2,1,0:T(1,128)} %param.23) | copy-start | bytes 196
  37.0 46.2 %copy-start.5 = (f32[1,1,16]{2,1,0:T(1,128)S(1)}, f32[1,1,16]{2,1,0:T(1,128)}, u32[]{:S(2)}) copy-start(f32[1,1,16]{2,1,0:T(1,128)} %param.24) | copy-start | bytes 196
  37.0 46.1 %all-to-all-start = ((bf16[8,1040,128]{2,1,0:T(8,128)(2,1)}), bf16[8,1040,128]{2,1,0:T(8,128)(2,1)S(1)}, u32[]{:S(2)}, u32[]{:S(2)}) async-start(bf16[8,1040,128]{2,1,0:T(8,128)(2,1)} %broadcast_in_dim.43), calls=%async_computation | async-start | bytes 4259840 | tf_op jit(solution)/shard_map/all_to_all | solution.py:260
  83.2 3.4 %copy-start = (bf16[64,256,2,128]{3,2,1,0:T(2,128)(2,1)S(1)}, bf16[64,256,2,128]{3,2,1,0:T(2,128)(2,1)}, u32[]{:S(2)}) copy-start(bf16[64,256,2,128]{3,2,1,0:T(2,128)(2,1)} %param.16) | copy-start | bytes 25165828

commit v2 on v1

v2 whole, which is shorter than its diff:
```python
import jax
import jax.numpy as jnp
from jax import lax
from jax.experimental import pallas as pl
from jax.experimental.pallas import tpu as pltpu
from jax.sharding import PartitionSpec as P

HD = 128
PERS = 16
MCH = 64
PCH = 1024
DEC_DEV = 4
CACHE = 4096
PAGE = 256
PAGES = CACHE // PAGE
ROWS = PCH + DEC_DEV
PADDED = PCH + 16

F32 = jnp.float32
BF16 = jnp.bfloat16
EPSILON = 1e-6
SCALE = HD**-0.5


def device_at(x, y, z_hi, z_lo, core):
    return (2 * y + z_hi) * 16 + 4 * x + 2 * z_lo + core


def moves(target):
    pairs = []
    for x in range(4):
        for y in range(4):
            for z_hi in range(2):
                for z_lo in range(2):
                    for core in range(2):
                        here = (x, y, z_hi, z_lo, core)
                        pairs.append((device_at(*here), device_at(*target(*here))))
    return pairs


def permute(values, target):
    return lax.ppermute(values, ("row", "col"), moves(target))


def dot_f32(left, right):
    return lax.dot_general(left, right, (((1,), (0,)), ((), ())), preferred_element_type=F32)


def dot_rows(left, right):
    return lax.dot_general(left, right, (((1,), (1,)), ((), ())), preferred_element_type=F32)


def dot_turned(left, right):
    return lax.dot_general(left, right, (((0,), (0,)), ((), ())), preferred_element_type=F32)


def two_parts(values):
    high = values.astype(BF16)
    return jnp.concatenate([high, (values - high.astype(F32)).astype(BF16)], axis=0)


def inverse_norm(rows):
    wide = rows.astype(F32)
    return lax.rsqrt(jnp.sum(wide * wide, axis=-1, keepdims=True) + EPSILON)


HALF = PCH // 2
EXTRA = PADDED - PCH


def project(token_refs, weight_ref):
    total = None
    for step, token_ref in enumerate(token_refs):
        part = dot_f32(token_ref[...], weight_ref[256 * step : 256 * step + 256, :])
        total = part if total is None else total + part
    return total.astype(BF16)


def prefill(
    first, projected, persist_key, persist_value, memory, momentum, rates, out_ref, out_at
):
    forget_ref, keep_ref, learn_ref = rates
    blank = jnp.zeros((HD - MCH - PERS, HD), BF16)
    row_at = lax.broadcasted_iota(jnp.int32, (MCH, HD), 0)
    column_at = lax.broadcasted_iota(jnp.int32, (MCH, HD), 1)
    visible = (column_at <= row_at) | ((column_at >= MCH) & (column_at < MCH + PERS))
    for step in range(HALF // MCH):
        block = first + step
        here = slice(step * MCH, step * MCH + MCH)
        query = projected[here, 0:HD]
        key = projected[here, HD : 2 * HD]
        value = projected[here, 2 * HD : 3 * HD]
        query_scale = inverse_norm(query)
        key_scale = inverse_norm(key)
        left = jnp.concatenate(
            [jnp.concatenate([query, query], axis=1), jnp.concatenate([key, key], axis=1)], axis=0
        )
        reads = dot_f32(left, two_parts(memory))
        errors = reads[MCH:] * key_scale - value.astype(F32)
        errors = errors * (key_scale * (2.0 / MCH))
        gradient = dot_turned(jnp.concatenate([key, key], axis=0), two_parts(errors))
        momentum = keep_ref[block] * momentum - learn_ref[block] * gradient
        memory = (1.0 - forget_ref[block]) * memory + momentum

        keys = jnp.concatenate([key, persist_key, blank], axis=0)
        values = jnp.concatenate([value, persist_value, blank], axis=0)
        scores = jnp.where(visible, dot_rows(query, keys) * SCALE, -jnp.inf)
        powers = jnp.exp(scores - jnp.max(scores, axis=-1, keepdims=True))
        weights = (powers / jnp.sum(powers, axis=-1, keepdims=True)).astype(BF16)
        result = dot_f32(weights, values) + reads[:MCH] * query_scale
        out_ref[out_at + step * MCH : out_at + step * MCH + MCH, :] = result.astype(BF16)
    return memory, momentum


def decode(
    length_ref, projected, persist_key, persist_value, decode_memory_ref, cache, score, arrival
):
    query = projected[HALF : HALF + EXTRA, 0:HD]
    key = projected[HALF : HALF + EXTRA, HD : 2 * HD]
    value = projected[HALF : HALF + EXTRA, 2 * HD : 3 * HD]
    row = lax.broadcasted_iota(jnp.int32, (EXTRA, 1), 0)
    length = jnp.zeros((EXTRA, 1), jnp.int32)
    for request in range(DEC_DEV):
        pltpu.make_async_copy(cache.at[request], cache.at[request], arrival.at[request]).wait()
        length = jnp.where(row == request, length_ref[request], length)
    for place in range(PAGES):
        span = slice(place * 2 * PAGE, place * 2 * PAGE + 2 * PAGE)
        found = dot_rows(query, cache[0, span, :])
        for request in range(1, DEC_DEV):
            found = jnp.where(row == request, dot_rows(query, cache[request, span, :]), found)
        column = lax.broadcasted_iota(jnp.int32, (EXTRA, 2 * PAGE), 1)
        live = ((column & 1) == 0) & ((column >> 1) + place * PAGE < length)
        score[:, span] = jnp.where(live, found * SCALE, -jnp.inf)
    own_score = jnp.sum(query.astype(F32) * key.astype(F32), axis=-1, keepdims=True) * SCALE
    persist_score = dot_rows(query, persist_key) * SCALE
    cache_score = score[...]
    largest = jnp.maximum(
        jnp.maximum(jnp.max(cache_score, axis=-1, keepdims=True), own_score),
        jnp.max(persist_score, axis=-1, keepdims=True),
    )
    cache_power = jnp.exp(cache_score - largest)
    own_power = jnp.exp(own_score - largest)
    persist_power = jnp.exp(persist_score - largest)
    totals = (
        jnp.sum(cache_power, axis=-1, keepdims=True)
        + own_power
        + jnp.sum(persist_power, axis=-1, keepdims=True)
    )
    share = 1.0 / totals
    cache_weight = pltpu.roll(cache_power * share, 1, 1).astype(BF16)
    attended = jnp.zeros((EXTRA, HD), F32)
    for request in range(DEC_DEV):
        attended = jnp.where(row == request, dot_f32(cache_weight, cache[request]), attended)
    own_weight = (own_power * share).astype(BF16).astype(F32)
    attended = attended + own_weight * value.astype(F32)
    attended = attended + dot_f32((persist_power * share).astype(BF16), persist_value)
    twice = jnp.concatenate([query, query], axis=1)
    readout = jnp.zeros((EXTRA, HD), F32)
    for request in range(DEC_DEV):
        read = dot_f32(twice, two_parts(decode_memory_ref[request]))
        readout = jnp.where(row == request, read, readout)
    return (attended + readout * inverse_norm(query)).astype(BF16)


def first_kernel(
    table_ref,
    length_ref,
    forget_ref,
    keep_ref,
    learn_ref,
    token_0_ref,
    token_1_ref,
    token_2_ref,
    token_3_ref,
    weight_ref,
    persist_key_ref,
    persist_value_ref,
    state_ref,
    decode_memory_ref,
    page_ref,
    out_ref,
    tail_ref,
    memory_ref,
    momentum_ref,
    projected,
    cache,
    score,
    arrival,
):
    for request in range(DEC_DEV):
        for place in range(PAGES):
            pltpu.make_async_copy(
                page_ref.at[table_ref[request * PAGES + place]],
                cache.at[request, pl.ds(place * 2 * PAGE, 2 * PAGE)],
                arrival.at[request],
            ).start()
    projected[...] = project((token_0_ref, token_1_ref, token_2_ref, token_3_ref), weight_ref)
    memory = jnp.concatenate([state_ref[s, 0:8, :] for s in range(16)], axis=0)
    momentum = jnp.concatenate([state_ref[s, 8:16, :] for s in range(16)], axis=0)
    persist_key, persist_value = persist_key_ref[...], persist_value_ref[...]
    rates = (forget_ref, keep_ref, learn_ref)
    memory, momentum = prefill(
        0, projected, persist_key, persist_value, memory, momentum, rates, out_ref, 0
    )
    memory_ref[...] = memory
    momentum_ref[...] = momentum
    tail_ref[...] = decode(
        length_ref, projected, persist_key, persist_value, decode_memory_ref, cache, score, arrival
    )


def second_kernel(
    forget_ref,
    keep_ref,
    learn_ref,
    token_0_ref,
    token_1_ref,
    token_2_ref,
    token_3_ref,
    weight_ref,
    persist_key_ref,
    persist_value_ref,
    memory_in_ref,
    momentum_in_ref,
    first_ref,
    tail_ref,
    out_ref,
    memory_ref,
    momentum_ref,
    projected,
):
    projected[...] = project((token_0_ref, token_1_ref, token_2_ref, token_3_ref), weight_ref)
    memory, momentum = prefill(
        HALF // MCH,
        projected,
        persist_key_ref[...],
        persist_value_ref[...],
        memory_in_ref[...],
        momentum_in_ref[...],
        (forget_ref, keep_ref, learn_ref),
        out_ref,
        HALF,
    )
    memory_ref[...] = memory
    momentum_ref[...] = momentum
    out_ref[0:HALF, :] = first_ref[...]
    out_ref[PCH:ROWS, :] = tail_ref[0:DEC_DEV, :]


IN_SMEM = pl.BlockSpec(memory_space=pltpu.SMEM)
IN_VMEM = pl.BlockSpec(memory_space=pltpu.VMEM)


def first_part(table, length, rates, chunks, weight, keys, values, state, decode_memory, pages):
    return pl.pallas_call(
        first_kernel,
        out_shape=(
            jax.ShapeDtypeStruct((HALF, HD), BF16),
            jax.ShapeDtypeStruct((EXTRA, HD), BF16),
            jax.ShapeDtypeStruct((HD, HD), F32),
            jax.ShapeDtypeStruct((HD, HD), F32),
        ),
        in_specs=[IN_SMEM] * 5 + [IN_VMEM] * 9 + [pl.BlockSpec(memory_space=pltpu.HBM)],
        out_specs=(IN_VMEM,) * 4,
        scratch_shapes=[
            pltpu.VMEM((HALF + EXTRA, 3 * HD), BF16),
            pltpu.VMEM((DEC_DEV, 2 * CACHE, HD), BF16),
            pltpu.VMEM((EXTRA, 2 * CACHE), F32),
            pltpu.SemaphoreType.DMA((DEC_DEV,)),
        ],
        compiler_params=pltpu.CompilerParams(vmem_limit_bytes=48 * 2**20),
    )(
        table.reshape(-1),
        length,
        *rates,
        *chunks,
        weight,
        keys,
        values,
        state,
        decode_memory.reshape(DEC_DEV, HD, HD),
        pages.reshape(DEC_DEV * PAGES, 2 * PAGE, HD),
    )


def second_part(rates, chunks, weight, keys, values, memory, momentum, first, tail):
    return pl.pallas_call(
        second_kernel,
        out_shape=(
            jax.ShapeDtypeStruct((ROWS, HD), BF16),
            jax.ShapeDtypeStruct((HD, HD), F32),
            jax.ShapeDtypeStruct((HD, HD), F32),
        ),
        in_specs=[IN_SMEM] * 3 + [IN_VMEM] * 11,
        out_specs=(IN_VMEM,) * 3,
        scratch_shapes=[pltpu.VMEM((HALF, 3 * HD), BF16)],
        compiler_params=pltpu.CompilerParams(vmem_limit_bytes=16 * 2**20),
    )(*rates, *chunks, weight, keys, values, memory, momentum, first, tail)


def pair_up(piece):
    z_hi = lax.axis_index("row") % 2
    other = permute(piece, lambda x, y, z_hi, z_lo, core: (x, y, 1 - z_hi, z_lo, core))
    return jnp.concatenate(
        [jnp.where(z_hi == 0, piece, other), jnp.where(z_hi == 0, other, piece)], axis=1
    )


def spread_rows(pair):
    came = [
        permute(
            pair,
            lambda x, y, z_hi, z_lo, core, step=step: (x, (y + step) % 4, z_hi, z_lo, core),
        )
        for step in (1, 2, 3)
    ]
    return [pair, *came]


def gather_weight(block):
    y = lax.axis_index("row") // 2
    x = lax.axis_index("col") // 4
    z_lo = lax.axis_index("col") // 2 % 2
    core = lax.axis_index("col") % 2
    other = permute(block, lambda x, y, z_hi, z_lo, core: (x, y, z_hi, 1 - z_lo, core))
    pair = jnp.stack(
        [jnp.where(z_lo == 0, block, other), jnp.where(z_lo == 0, other, block)], axis=0
    )
    shifted = [pair]
    for step in (1, 2, 3):
        shifted.append(
            permute(
                pair,
                lambda x, y, z_hi, z_lo, core, step=step: ((x + step) % 4, y, z_hi, z_lo, core),
            )
        )
    ordered = []
    for place in range(4):
        chosen = shifted[3]
        for step in (0, 1, 2):
            chosen = jnp.where((2 * x - y + place) % 4 == step, shifted[step], chosen)
        ordered.append(chosen)
    mine = jnp.stack(ordered, axis=0)
    theirs = permute(mine, lambda x, y, z_hi, z_lo, core: (x, y, z_hi, z_lo, 1 - core))
    both = jnp.stack(
        [jnp.where(core == 0, mine, theirs), jnp.where(core == 0, theirs, mine)], axis=2
    )
    return both.reshape(-1, block.shape[1])


def deal_states(memory_in, momentum_in, destination):
    slots = 16
    mark = jnp.broadcast_to(destination.astype(F32).reshape(1, 1, 1), (slots, 8, HD))
    pieces = jnp.concatenate(
        [memory_in.reshape(slots, 8, HD), momentum_in.reshape(slots, 8, HD), mark], axis=1
    )
    spread = lax.all_to_all(pieces, "col", split_axis=0, concat_axis=0, tiled=True)
    target = spread[:, 16, 0].astype(jnp.int32)
    chosen = target[None, :] == jnp.arange(slots, dtype=jnp.int32)[:, None]
    return jnp.sum(jnp.where(chosen[:, :, None, None], spread[None, :, :16, :], 0.0), axis=1)


def shards(
    tokens,
    qkv_weight,
    persistent,
    cache_pages,
    page_table,
    cache_len,
    destination,
    memory_in,
    momentum_in,
    forget_rate,
    keep_rate,
    learn_rate,
    decode_memory,
):
    core = lax.axis_index("col") % 2
    lower, upper = tokens[:ROWS], tokens[ROWS:]
    kept = jnp.where(core == 0, lower, upper)
    sent = jnp.where(core == 0, upper, lower)
    came = permute(sent, lambda x, y, z_hi, z_lo, core: (x, y, z_hi, z_lo, 1 - core))
    came, memory_in, momentum_in, qkv_weight = lax.optimization_barrier(
        (came, memory_in, momentum_in, qkv_weight)
    )
    own = jnp.concatenate(
        [jnp.where(core == 0, kept, came), jnp.where(core == 0, came, kept)], axis=1
    )
    parts = [
        jnp.concatenate([own[:HALF], jnp.pad(own[PCH:], ((0, PADDED - ROWS), (0, 0)))], axis=0),
        own[HALF:PCH],
    ]
    turned = [
        permute(part, lambda x, y, z_hi, z_lo, core: (y, (x + y) % 4, z_lo, z_hi, core))
        for part in parts
    ]
    pairs = [pair_up(part) for part in turned]
    weight = gather_weight(qkv_weight)
    chunks = [spread_rows(pair) for pair in pairs]
    dealt = deal_states(memory_in, momentum_in, destination)
    dealt, chunks[0][1] = lax.optimization_barrier((dealt, chunks[0][1]))
    state = lax.all_to_all(dealt, "col", split_axis=0, concat_axis=0, tiled=True)
    rates = [rate.reshape(-1) for rate in (forget_rate, keep_rate, learn_rate)]
    keys, values = persistent[:, 0], persistent[:, 1]
    first, tail, memory, momentum = first_part(
        page_table,
        cache_len,
        rates,
        chunks[0],
        weight,
        keys,
        values,
        state,
        decode_memory,
        cache_pages,
    )
    heads_out, memory, momentum = second_part(
        rates, chunks[1], weight, keys, values, memory, momentum, first, tail
    )
    return heads_out, memory[None, None], momentum[None, None]


def solution(mesh):
    placed = (
        P("row", "col"),
        P("col", "row"),
        P(None, None, "row"),
        P("col", None, None, "row"),
        P("col", None),
        P("col"),
        P("col"),
        P("col", "row", None, None),
        P("col", "row", None, None),
        P("col", "row", None),
        P("col", "row", None),
        P("col", "row", None),
        P("col", "row", None, None),
    )
    return jax.shard_map(
        shards,
        mesh=mesh,
        in_specs=placed,
        out_specs=(P("col", "row"), P("col", "row", None, None), P("col", "row", None, None)),
        check_vma=False,
    )
```

time: 110 us -> 84.2 us (0.77)
  blocking collectives: 57.4 us -> 0 us
  starting transfers between devices: 12.7 us -> 41.5 us
  waiting for transfers between devices: 5.56 us -> 18.3 us
  Pallas kernels: 22.7 us -> 15.5 us
  local copies, waits for them, and re-layouts: 7.65 us -> 1.82 us
  other arithmetic: 1.74 us -> 4.85 us
    all_gather x1 -> x0, blocking collectives: 41.4 us -> none  [shards(): weight = lax.all_gather(qkv_weight, 'col', axis=0, tiled=True)]
    ppermute x2 -> x16, starting transfers between devices: 2.18 us -> 28.5 us  [permute(): return lax.ppermute(values, ('row', 'col'), moves(target))]
    ppermute x2 -> x16, waiting for transfers between devices: 0.01 us -> 17.3 us  [permute(): return lax.ppermute(values, ('row', 'col'), moves(target))]
    all_to_all x1 -> x0, blocking collectives: 16.1 us -> none  [route_states(): lax.all_to_all(ordered, 'col', split_axis=0, concat_axis=0, tiled=True)]
    pallas_call x1 -> x2, Pallas kernels: 22.7 us -> 15.5 us  [the longest x1 10.9 us: first_part(): pl.pallas_call(first_kernel, out_shape=(jax.ShapeDtypeStruct((HALF, HD),...]
    all_to_all x2, waiting for transfers between devices: 5.56 us -> 1.03 us  [the longest x1 1.03 us: deal_states(): lax.all_to_all(pieces, 'col', split_axis=0, concat_axis=0, tiled=True)]
    unnamed x22, local copies, waits for them, and re-layouts: 3.43 us -> 0.44 us
    all_to_all x2, starting transfers between devices: 10.5 us -> 13 us  [the longest x1 7.65 us: shards(): lax.all_to_all(dealt, 'col', split_axis=0, concat_axis=0, tiled=True)]
  transfers between devices with their start and end apart: 4 -> 18, of which waited for: 1 -> 7; matrix products, arithmetic and copies ran while one was open for 2% -> 6% of each run, Pallas kernels for 0% -> 13%
where the time goes in v2:
time: 84.2 us; the launch traced here: 83.6 us
  starting transfers between devices  41.5 us (49%)
  waiting for transfers between devices  18.3 us (22%)
  Pallas kernels  15.5 us (18%)
  other arithmetic  4.85 us (6%)
  local copies, waits for them, and re-layouts  1.82 us (2%)
  between operations  1.65 us (2%)
    ppermute x16, starting transfers between devices, permute(): return lax.ppermute(values, ('row', 'col'), moves(target))  28.5 us
    ppermute x16, waiting for transfers between devices, permute(): return lax.ppermute(values, ('row', 'col'), moves(target))  17.3 us
    pallas_call x1, Pallas kernels, first_part(): pl.pallas_call(first_kernel, out_shape=(jax.ShapeDtypeStruct((HALF, HD),...  10.9 us
    all_to_all x1, starting transfers between devices, shards(): lax.all_to_all(dealt, 'col', split_axis=0, concat_axis=0, tiled=True)  7.65 us
    all_to_all x1, starting transfers between devices, deal_states(): lax.all_to_all(pieces, 'col', split_axis=0, concat_axis=0, tiled=True)  5.36 us
    pallas_call x1, Pallas kernels, second_part(): pl.pallas_call(second_kernel, out_shape=(jax.ShapeDtypeStruct((ROWS, HD),...  4.62 us
  transfers between devices with their start and end apart: 18, of which 7 were waited for; matrix products, arithmetic and copies ran while one was open for 6% of the time, Pallas kernels for 13%

profile of v2, /device:TPU:1, one launch (start us, length us, event | category | flops | bytes accessed | tf_op | source)
XLA Modules:
  0.0 83.6 jit_solution(2150335408279325903)
XLA Ops:
  0.7 1.1 %fusion.6 = (bf16[1028,64]{0,1:T(8,128)(2,1)S(1)}, bf16[1028,64]{0,1:T(8,128)(2,1)S(1)}) fusion(bf16[2056,64]{0,1:T(8,128)(2,1)} %param.13), kind=kLoop, calls=%fused_computation.39 | loop fusion | bytes 526336 | tf_op jit(solution)/shard_map/slice | solution.py:379
  2.3 1.5 %collective-permute-start = (bf16[1028,64]{1,0:T(8,128)(2,1)S(1)}, bf16[1028,64]{1,0:T(8,128)(2,1)S(1)}, u32[]{:S(2)}, u32[]{:S(2)}) collective-permute-start(bf16[1028,64]{1,0:T(8,128)(2,1)S(1)} %broadcast_select_fusion.2), channel_id=1, source_target_pairs={{0,1},{1,0},{2,3},{3,2},{16,17},{17,16},{18,19},{19,18},{32,33},{3... | collective-permute-start | bytes 394760 | tf_op jit(solution)/shard_map/ppermute | solution.py:42
  5.3 1.8 %collective-permute-start.6 = (bf16[64,384]{1,0:T(8,128)(2,1)S(1)}, bf16[64,384]{1,0:T(8,128)(2,1)S(1)}, u32[]{:S(2)}, u32[]{:S(2)}) collective-permute-start(bf16[64,384]{1,0:T(8,128)(2,1)S(1)} %copy-done.7), channel_id=1, source_target_pairs={{0,2},{1,3},{2,0},{3,1},{16,18},{17,19},{18,16},{19,17},{32,34},{3... | collective-permute-start | bytes 147464 | tf_op jit(solution)/shard_map/ppermute | solution.py:42
  7.1 0.7 collective-permute-start.11
  7.8 0.7 collective-permute-start.1
  8.7 10.8 %collective-permute-start.7 = (bf16[2,64,384]{2,1,0:T(8,128)(2,1)S(1)}, bf16[2,64,384]{2,1,0:T(8,128)(2,1)S(1)}, u32[]{:S(2)}, u32[]{:S(2)}) collective-permute-start(bf16[2,64,384]{2,1,0:T(8,128)(2,1)S(1)} %pad_maximum_fusion.5), channel_id=1, source_target_pairs={{0,8},{1,9},{2,10},{3,11},{16,24},{17,25},{18,26},{19,27},{32,40},... | collective-permute-start | bytes 294920 | tf_op jit(solution)/shard_map/ppermute | solution.py:42
  19.5 2.7 %collective-permute-start.9 = (bf16[2,64,384]{2,1,0:T(8,128)(2,1)S(1)}, bf16[2,64,384]{2,1,0:T(8,128)(2,1)S(1)}, u32[]{:S(2)}, u32[]{:S(2)}) collective-permute-start(bf16[2,64,384]{2,1,0:T(8,128)(2,1)S(1)} %pad_maximum_fusion.5), channel_id=1, source_target_pairs={{0,12},{1,13},{2,14},{3,15},{16,28},{17,29},{18,30},{19,31},{32,44... | collective-permute-start | bytes 294920 | tf_op jit(solution)/shard_map/ppermute | solution.py:42
  22.1 0.8 maximum_maximum_fusion
  22.9 5.4 %all-to-all-start = ((f32[16,24,128]{2,1,0:T(8,128)}), f32[16,24,128]{2,1,0:T(8,128)S(1)}, u32[]{:S(2)}, u32[]{:S(2)}) async-start(f32[16,24,128]{2,1,0:T(8,128)} %maximum_maximum_fusion), calls=%async_computation | async-start | bytes 393216 | tf_op jit(solution)/shard_map/all_to_all | solution.py:357
  28.3 4.3 %collective-permute-start.2 = (bf16[512,128]{1,0:T(8,128)(2,1)S(1)}, bf16[512,128]{1,0:T(8,128)(2,1)S(1)}, u32[]{:S(2)}, u32[]{:S(2)}) collective-permute-start(bf16[512,128]{1,0:T(8,128)(2,1)S(1)} %collective-permute-done.1), channel_id=1, source_target_pairs={{0,16},{1,17},{2,18},{3,19},{16,0},{17,1},{18,2},{19,3},{32,48},{3... | collective-permute-start | bytes 393224 | tf_op jit(solution)/shard_map/ppermute | solution.py:42
  32.8 0.8 pad_maximum_fusion.1
  33.6 0.5 collective-permute-start.10
  34.1 1.0 %all-to-all-done = f32[16,24,128]{2,1,0:T(8,128)S(1)} async-done(((f32[16,24,128]{2,1,0:T(8,128)}), f32[16,24,128]{2,1,0:T(8,128)S(1)}, u32[]{:S(2)}, u32[]{:S(2)}) %all-to-all-start) | async-done | bytes 196640 | tf_op jit(solution)/shard_map/all_to_all | solution.py:357
  35.5 1.0 %select_reduce_fusion = f32[16,16,128]{2,1,0:T(8,128)} fusion(f32[16,16,128]{2,1,0:T(8,128)S(1)} %slice.41, pred[16,16]{1,0:T(8,128)(4,1)S(1)} %iota_compare_fusion.1), kind=kLoop, calls=%fused_computation | loop fusion | flops 1015808 | bytes 262400 | tf_op jit(solution)/shard_map/reduce_sum | solution.py:360
  36.5 4.9 %collective-permute-done.12 = bf16[528,128]{1,0:T(8,128)(2,1)S(1)} collective-permute-done((bf16[528,128]{1,0:T(8,128)(2,1)S(1)}, bf16[528,128]{1,0:T(8,128)(2,1)S(1)}, u32[]{:S(2)}, u32[]{:S(2)}) %collective-permute-start.12) | collective-permute-done | bytes 135200 | tf_op jit(solution)/shard_map/ppermute | solution.py:42
  41.7 3.8 %collective-permute-start.4 = (bf16[512,256]{1,0:T(8,128)(2,1)S(1)}, bf16[512,256]{1,0:T(8,128)(2,1)S(1)}, u32[]{:S(2)}, u32[]{:S(2)}) collective-permute-start(bf16[512,256]{1,0:T(8,128)(2,1)S(1)} %pad_maximum_fusion.3.token_0_ref), channel_id=1, source_target_pairs={{0,64},{1,65},{2,66},{3,67},{16,80},{17,81},{18,82},{19,83},{32,96... | collective-permute-start | bytes 786440 | tf_op jit(solution)/shard_map/ppermute | solution.py:42
  45.6 4.4 %collective-permute-done.13.token_1_ref = bf16[528,256]{1,0:T(8,128)(2,1)S(1)} collective-permute-done((bf16[528,256]{1,0:T(8,128)(2,1)S(1)}, bf16[528,256]{1,0:T(8,128)(2,1)S(1)}, u32[]{:S(2)}, u32[]{:S(2)}) %collective-permute-start.13) | collective-permute-done | bytes 270368 | tf_op jit(solution)/shard_map/ppermute | solution.py:42
  50.0 7.6 %all-to-all-start.1 = ((f32[16,16,128]{2,1,0:T(8,128)}), f32[16,16,128]{2,1,0:T(8,128)S(1)}, u32[]{:S(2)}, u32[]{:S(2)}) async-start(f32[16,16,128]{2,1,0:T(8,128)} %select_reduce_fusion), calls=%async_computation.1 | async-start | bytes 262144 | tf_op jit(solution)/shard_map/all_to_all | solution.py:402
  57.7 1.4 %collective-permute-start.15 = (bf16[528,256]{1,0:T(8,128)(2,1)S(1)}, bf16[528,256]{1,0:T(8,128)(2,1)S(1)}, u32[]{:S(2)}, u32[]{:S(2)}) collective-permute-start(bf16[528,256]{1,0:T(8,128)(2,1)S(1)} %pad_maximum_fusion.2.token_0_ref), channel_id=1, source_target_pairs={{0,96},{1,97},{2,98},{3,99},{16,112},{17,113},{18,114},{19,115},{3... | collective-permute-start | bytes 811016 | tf_op jit(solution)/shard_map/ppermute | solution.py:42
  59.1 1.1 %select_bitcast_fusion.1 = (bf16[4,2,1,64,384]{4,3,1,0,2:T(8,128)(2,1)S(1)}, bf16[4,2,1,64,384]{4,3,1,0,2:T(8,128)(2,1)S(1)}) fusion(bf16[4,2,64,384]{3,2,1,0:T(8,128)(2,1)} %collective-permute-done.10, pred[]{:T(512)S(6)} %eq.90, bf16[1,2,64,384]{3,2,1,0:T(8,128)(2,1)S(1)} %get-tuple-element.36, bf16[1,2,64,384]{3,2,1,0:T(8,128)(2,1)S(1)} %get-tuple-element.37, ...), kind=kLoop, calls=%fused_computation.4 | loop fusion | flops 983040 | bytes 1572865 | tf_op jit(solution)/shard_map/stack | solution.py:345
  60.5 4.9 %collective-permute-done.14.token_2_ref = bf16[528,256]{1,0:T(8,128)(2,1)S(1)} collective-permute-done((bf16[528,256]{1,0:T(8,128)(2,1)S(1)}, bf16[528,256]{1,0:T(8,128)(2,1)S(1)}, u32[]{:S(2)}, u32[]{:S(2)}) %collective-permute-start.14) | collective-permute-done | bytes 270368 | tf_op jit(solution)/shard_map/ppermute | solution.py:42
  65.4 2.7 %collective-permute-done.15.token_3_ref = bf16[528,256]{1,0:T(8,128)(2,1)S(1)} collective-permute-done((bf16[528,256]{1,0:T(8,128)(2,1)S(1)}, bf16[528,256]{1,0:T(8,128)(2,1)S(1)}, u32[]{:S(2)}, u32[]{:S(2)}) %collective-permute-start.15) | collective-permute-done | bytes 270368 | tf_op jit(solution)/shard_map/ppermute | solution.py:42
  68.1 10.9 %shard_map.148 = (bf16[512,128]{1,0:T(8,128)(2,1)S(1)}, bf16[16,128]{1,0:T(8,128)(2,1)S(1)}, f32[128,128]{1,0:T(8,128)S(1)}, f32[128,128]{1,0:T(8,128)S(1)}) custom-call(s32[64]{0:T(128)S(1)} %reshape.65.table_ref, s32[4]{0:T(128)S(1)} %copy-done.4, f32[16]{0:T(128)S(1)} %bitcast.34, f32[16]{0:T(128)S(1)} %bitcast.36, f32[16]{0:T(128)S(1)} %bitcast.38, ...), custom_call_target="tpu_custom_call" | custom-call | tf_op jit(solution)/shard_map/pallas_call | solution.py:255
  79.0 4.6 %shard_map.149 = (bf16[1028,128]{1,0:T(8,128)(2,1)}, f32[128,128]{1,0:T(8,128)}, f32[128,128]{1,0:T(8,128)}) custom-call(f32[16]{0:T(128)S(1)} %bitcast.35, f32[16]{0:T(128)S(1)} %bitcast.37, f32[16]{0:T(128)S(1)} %bitcast.39, bf16[512,256]{1,0:T(8,128)(2,1)S(1)} %pad_maximum_fusion.3.token_0_ref, bf16[512,256]{1,0:T(8,128)(2,1)S(1)} %collective-permute-done.3.token_1_ref, ...), custom_call_target="tpu_custom_call" | custom-call | tf_op jit(solution)/shard_map/pallas_call | solution.py:287
  (64 shorter events, 2.7 us)
Async XLA Ops:
  2.2 20.0 %copy-start.5 = (f32[1,1,128,128]{3,2,1,0:T(8,128)S(1)}, f32[1,1,128,128]{3,2,1,0:T(8,128)}, u32[]{:S(2)}) copy-start(f32[1,1,128,128]{3,2,1,0:T(8,128)} %param.21) | copy-start | bytes 196612
  2.2 20.0 %copy-start.6 = (f32[1,1,128,128]{3,2,1,0:T(8,128)S(1)}, f32[1,1,128,128]{3,2,1,0:T(8,128)}, u32[]{:S(2)}) copy-start(f32[1,1,128,128]{3,2,1,0:T(8,128)} %param.20) | copy-start | bytes 196612
  2.3 2.7 %collective-permute-start = (bf16[1028,64]{1,0:T(8,128)(2,1)S(1)}, bf16[1028,64]{1,0:T(8,128)(2,1)S(1)}, u32[]{:S(2)}, u32[]{:S(2)}) collective-permute-start(bf16[1028,64]{1,0:T(8,128)(2,1)S(1)} %broadcast_select_fusion.2), channel_id=1, source_target_pairs={{0,1},{1,0},{2,3},{3,2},{16,17},{17,16},{18,19},{19,18},{32,33},{3... | collective-permute-start | bytes 394760 | tf_op jit(solution)/shard_map/ppermute | solution.py:42
  5.3 3.3 %collective-permute-start.6 = (bf16[64,384]{1,0:T(8,128)(2,1)S(1)}, bf16[64,384]{1,0:T(8,128)(2,1)S(1)}, u32[]{:S(2)}, u32[]{:S(2)}) collective-permute-start(bf16[64,384]{1,0:T(8,128)(2,1)S(1)} %copy-done.7), channel_id=1, source_target_pairs={{0,2},{1,3},{2,0},{3,1},{16,18},{17,19},{18,16},{19,17},{32,34},{3... | collective-permute-start | bytes 147464 | tf_op jit(solution)/shard_map/ppermute | solution.py:42
  7.1 25.4 %collective-permute-start.11 = (bf16[528,128]{1,0:T(8,128)(2,1)S(1)}, bf16[528,128]{1,0:T(8,128)(2,1)S(1)}, u32[]{:S(2)}, u32[]{:S(2)}) collective-permute-start(bf16[528,128]{1,0:T(8,128)(2,1)S(1)} %pad_maximum_fusion.4), channel_id=1, source_target_pairs={{0,0},{1,1},{2,16},{3,17},{16,2},{17,3},{18,18},{19,19},{32,36},{3... | collective-permute-start | bytes 405512 | tf_op jit(solution)/shard_map/ppermute | solution.py:42
  7.8 20.4 %collective-permute-start.1 = (bf16[512,128]{1,0:T(8,128)(2,1)S(1)}, bf16[512,128]{1,0:T(8,128)(2,1)S(1)}, u32[]{:S(2)}, u32[]{:S(2)}) collective-permute-start(bf16[512,128]{1,0:T(8,128)(2,1)S(1)} %get-tuple-element.34), channel_id=1, source_target_pairs={{0,0},{1,1},{2,16},{3,17},{16,2},{17,3},{18,18},{19,19},{32,36},{3... | collective-permute-start | bytes 393224 | tf_op jit(solution)/shard_map/ppermute | solution.py:42
  8.7 24.0 %collective-permute-start.7 = (bf16[2,64,384]{2,1,0:T(8,128)(2,1)S(1)}, bf16[2,64,384]{2,1,0:T(8,128)(2,1)S(1)}, u32[]{:S(2)}, u32[]{:S(2)}) collective-permute-start(bf16[2,64,384]{2,1,0:T(8,128)(2,1)S(1)} %pad_maximum_fusion.5), channel_id=1, source_target_pairs={{0,8},{1,9},{2,10},{3,11},{16,24},{17,25},{18,26},{19,27},{32,40},... | collective-permute-start | bytes 294920 | tf_op jit(solution)/shard_map/ppermute | solution.py:42
  19.5 13.2 %collective-permute-start.8 = (bf16[2,64,384]{2,1,0:T(8,128)(2,1)S(1)}, bf16[2,64,384]{2,1,0:T(8,128)(2,1)S(1)}, u32[]{:S(2)}, u32[]{:S(2)}) collective-permute-start(bf16[2,64,384]{2,1,0:T(8,128)(2,1)S(1)} %pad_maximum_fusion.5), channel_id=1, source_target_pairs={{0,4},{1,5},{2,6},{3,7},{16,20},{17,21},{18,22},{19,23},{32,36},{3... | collective-permute-start | bytes 294920 | tf_op jit(solution)/shard_map/ppermute | solution.py:42
  19.5 13.2 %collective-permute-start.9 = (bf16[2,64,384]{2,1,0:T(8,128)(2,1)S(1)}, bf16[2,64,384]{2,1,0:T(8,128)(2,1)S(1)}, u32[]{:S(2)}, u32[]{:S(2)}) collective-permute-start(bf16[2,64,384]{2,1,0:T(8,128)(2,1)S(1)} %pad_maximum_fusion.5), channel_id=1, source_target_pairs={{0,12},{1,13},{2,14},{3,15},{16,28},{17,29},{18,30},{19,31},{32,44... | collective-permute-start | bytes 294920 | tf_op jit(solution)/shard_map/ppermute | solution.py:42
  22.9 12.2 %all-to-all-start = ((f32[16,24,128]{2,1,0:T(8,128)}), f32[16,24,128]{2,1,0:T(8,128)S(1)}, u32[]{:S(2)}, u32[]{:S(2)}) async-start(f32[16,24,128]{2,1,0:T(8,128)} %maximum_maximum_fusion), calls=%async_computation | async-start | bytes 393216 | tf_op jit(solution)/shard_map/all_to_all | solution.py:357
  28.3 13.3 %collective-permute-start.2 = (bf16[512,128]{1,0:T(8,128)(2,1)S(1)}, bf16[512,128]{1,0:T(8,128)(2,1)S(1)}, u32[]{:S(2)}, u32[]{:S(2)}) collective-permute-start(bf16[512,128]{1,0:T(8,128)(2,1)S(1)} %collective-permute-done.1), channel_id=1, source_target_pairs={{0,16},{1,17},{2,18},{3,19},{16,0},{17,1},{18,2},{19,3},{32,48},{3... | collective-permute-start | bytes 393224 | tf_op jit(solution)/shard_map/ppermute | solution.py:42
  32.6 8.8 %collective-permute-start.12 = (bf16[528,128]{1,0:T(8,128)(2,1)S(1)}, bf16[528,128]{1,0:T(8,128)(2,1)S(1)}, u32[]{:S(2)}, u32[]{:S(2)}) collective-permute-start(bf16[528,128]{1,0:T(8,128)(2,1)S(1)} %collective-permute-done.11), channel_id=1, source_target_pairs={{0,16},{1,17},{2,18},{3,19},{16,0},{17,1},{18,2},{19,3},{32,48},{3... | collective-permute-start | bytes 405512 | tf_op jit(solution)/shard_map/ppermute | solution.py:42
  33.6 24.1 %collective-permute-start.10 = (bf16[4,2,64,384]{3,2,1,0:T(8,128)(2,1)}, bf16[4,2,64,384]{3,2,1,0:T(8,128)(2,1)}, u32[]{:S(2)}, u32[]{:S(2)}) collective-permute-start(bf16[4,2,64,384]{3,2,1,0:T(8,128)(2,1)} %pad_maximum_fusion.1), channel_id=1, source_target_pairs={{0,1},{1,0},{2,3},{3,2},{16,17},{17,16},{18,19},{19,18},{32,33},{3... | collective-permute-start | bytes 1179656 | tf_op jit(solution)/shard_map/ppermute | solution.py:42
  41.5 8.6 %collective-permute-start.13 = (bf16[528,256]{1,0:T(8,128)(2,1)S(1)}, bf16[528,256]{1,0:T(8,128)(2,1)S(1)}, u32[]{:S(2)}, u32[]{:S(2)}) collective-permute-start(bf16[528,256]{1,0:T(8,128)(2,1)S(1)} %pad_maximum_fusion.2.token_0_ref), channel_id=1, source_target_pairs={{0,32},{1,33},{2,34},{3,35},{16,48},{17,49},{18,50},{19,51},{32,64... | collective-permute-start | bytes 811016 | tf_op jit(solution)/shard_map/ppermute | solution.py:42
  41.6 37.4 %collective-permute-start.3 = (bf16[512,256]{1,0:T(8,128)(2,1)S(1)}, bf16[512,256]{1,0:T(8,128)(2,1)S(1)}, u32[]{:S(2)}, u32[]{:S(2)}) collective-permute-start(bf16[512,256]{1,0:T(8,128)(2,1)S(1)} %pad_maximum_fusion.3.token_0_ref), channel_id=1, source_target_pairs={{0,32},{1,33},{2,34},{3,35},{16,48},{17,49},{18,50},{19,51},{32,64... | collective-permute-start | bytes 786440 | tf_op jit(solution)/shard_map/ppermute | solution.py:42
  41.7 37.3 %collective-permute-start.4 = (bf16[512,256]{1,0:T(8,128)(2,1)S(1)}, bf16[512,256]{1,0:T(8,128)(2,1)S(1)}, u32[]{:S(2)}, u32[]{:S(2)}) collective-permute-start(bf16[512,256]{1,0:T(8,128)(2,1)S(1)} %pad_maximum_fusion.3.token_0_ref), channel_id=1, source_target_pairs={{0,64},{1,65},{2,66},{3,67},{16,80},{17,81},{18,82},{19,83},{32,96... | collective-permute-start | bytes 786440 | tf_op jit(solution)/shard_map/ppermute | solution.py:42
  45.5 33.5 %collective-permute-start.5 = (bf16[512,256]{1,0:T(8,128)(2,1)S(1)}, bf16[512,256]{1,0:T(8,128)(2,1)S(1)}, u32[]{:S(2)}, u32[]{:S(2)}) collective-permute-start(bf16[512,256]{1,0:T(8,128)(2,1)S(1)} %pad_maximum_fusion.3.token_0_ref), channel_id=1, source_target_pairs={{0,96},{1,97},{2,98},{3,99},{16,112},{17,113},{18,114},{19,115},{3... | collective-permute-start | bytes 786440 | tf_op jit(solution)/shard_map/ppermute | solution.py:42
  50.0 15.4 %collective-permute-start.14 = (bf16[528,256]{1,0:T(8,128)(2,1)S(1)}, bf16[528,256]{1,0:T(8,128)(2,1)S(1)}, u32[]{:S(2)}, u32[]{:S(2)}) collective-permute-start(bf16[528,256]{1,0:T(8,128)(2,1)S(1)} %pad_maximum_fusion.2.token_0_ref), channel_id=1, source_target_pairs={{0,64},{1,65},{2,66},{3,67},{16,80},{17,81},{18,82},{19,83},{32,96... | collective-permute-start | bytes 811016 | tf_op jit(solution)/shard_map/ppermute | solution.py:42
  50.0 18.0 %all-to-all-start.1 = ((f32[16,16,128]{2,1,0:T(8,128)}), f32[16,16,128]{2,1,0:T(8,128)S(1)}, u32[]{:S(2)}, u32[]{:S(2)}) async-start(f32[16,16,128]{2,1,0:T(8,128)} %select_reduce_fusion), calls=%async_computation.1 | async-start | bytes 262144 | tf_op jit(solution)/shard_map/all_to_all | solution.py:402
  57.7 10.4 %copy-start = (f32[4,1,128,128]{3,2,1,0:T(8,128)S(1)}, f32[4,1,128,128]{3,2,1,0:T(8,128)}, u32[]{:S(2)}) copy-start(f32[4,1,128,128]{3,2,1,0:T(8,128)} %param.25) | copy-start | bytes 786436
  57.7 10.4 %copy-start.1 = (f32[1,1,16]{2,1,0:T(1,128)S(1)}, f32[1,1,16]{2,1,0:T(1,128)}, u32[]{:S(2)}) copy-start(f32[1,1,16]{2,1,0:T(1,128)} %param.22) | copy-start | bytes 196
  57.7 10.4 %copy-start.2 = (f32[1,1,16]{2,1,0:T(1,128)S(1)}, f32[1,1,16]{2,1,0:T(1,128)}, u32[]{:S(2)}) copy-start(f32[1,1,16]{2,1,0:T(1,128)} %param.23) | copy-start | bytes 196
  57.7 10.4 %copy-start.3 = (f32[1,1,16]{2,1,0:T(1,128)S(1)}, f32[1,1,16]{2,1,0:T(1,128)}, u32[]{:S(2)}) copy-start(f32[1,1,16]{2,1,0:T(1,128)} %param.24) | copy-start | bytes 196
  57.7 10.3 %collective-permute-start.15 = (bf16[528,256]{1,0:T(8,128)(2,1)S(1)}, bf16[528,256]{1,0:T(8,128)(2,1)S(1)}, u32[]{:S(2)}, u32[]{:S(2)}) collective-permute-start(bf16[528,256]{1,0:T(8,128)(2,1)S(1)} %pad_maximum_fusion.2.token_0_ref), channel_id=1, source_target_pairs={{0,96},{1,97},{2,98},{3,99},{16,112},{17,113},{18,114},{19,115},{3... | collective-permute-start | bytes 811016 | tf_op jit(solution)/shard_map/ppermute | solution.py:42
  (4 other events, 21.4 us)

commit v3 on v2

--- a/solution.py
+++ b/solution.py
@@ -66,14 +66,39 @@
 
 HALF = PCH // 2
 EXTRA = PADDED - PCH
-
-
-def project(token_refs, weight_ref):
+STATE = 3 * MCH
+MARK = STATE + 2 * HD
+PACKET = MARK + 16
+
+
+def step_weight(step, near_ref, far_ref):
+    tiles = []
+    for tile in range(3):
+        rows = slice(tile * MCH, tile * MCH + MCH)
+        parts = [ref[step, place, rows, :] for place in range(2) for ref in (near_ref, far_ref)]
+        tiles.append(jnp.concatenate(parts, axis=0))
+    return jnp.concatenate(tiles, axis=1)
+
+
+def project(token_refs, near_ref, far_ref):
     total = None
+    x, y = lax.axis_index("col") // 4, lax.axis_index("row") // 2
     for step, token_ref in enumerate(token_refs):
-        part = dot_f32(token_ref[...], weight_ref[256 * step : 256 * step + 256, :])
+        moved = lax.rem(2 * x + step + 4 - y, 4)
+        part = dot_f32(token_ref[...], step_weight(moved, near_ref, far_ref))
         total = part if total is None else total + part
     return total.astype(BF16)
+
+
+def own_states(column, packet_refs):
+    total = jnp.zeros((2 * HD, HD), F32)
+    for packet_ref in packet_refs:
+        for step in range(4):
+            for place in range(2):
+                mark = packet_ref[step, place, MARK : MARK + 16, :].astype(F32)[0:1]
+                state = packet_ref[step, place, STATE : STATE + 2 * HD, :].astype(F32)
+                total = total + jnp.where(mark == column, state, 0.0)
+    return total[:HD], total[HD:]
 
 
 def prefill(
@@ -113,7 +138,7 @@
 
 
 def decode(
-    length_ref, projected, persist_key, persist_value, decode_memory_ref, cache, score, arrival
+    whole_ref, projected, persist_key, persist_value, decode_memory_ref, cache, score, arrival
 ):
     query = projected[HALF : HALF + EXTRA, 0:HD]
     key = projected[HALF : HALF + EXTRA, HD : 2 * HD]
@@ -122,7 +147,7 @@
     length = jnp.zeros((EXTRA, 1), jnp.int32)
     for request in range(DEC_DEV):
         pltpu.make_async_copy(cache.at[request], cache.at[request], arrival.at[request]).wait()
-        length = jnp.where(row == request, length_ref[request], length)
+        length = jnp.where(row == request, whole_ref[DEC_DEV * PAGES + request], length)
     for place in range(PAGES):
         span = slice(place * 2 * PAGE, place * 2 * PAGE + 2 * PAGE)
         found = dot_rows(query, cache[0, span, :])
@@ -157,87 +182,58 @@
     twice = jnp.concatenate([query, query], axis=1)
     readout = jnp.zeros((EXTRA, HD), F32)
     for request in range(DEC_DEV):
-        read = dot_f32(twice, two_parts(decode_memory_ref[request]))
+        read = dot_f32(twice, decode_memory_ref[request])
         readout = jnp.where(row == request, read, readout)
     return (attended + readout * inverse_norm(query)).astype(BF16)
 
 
-def first_kernel(
-    table_ref,
-    length_ref,
-    forget_ref,
-    keep_ref,
-    learn_ref,
-    token_0_ref,
-    token_1_ref,
-    token_2_ref,
-    token_3_ref,
-    weight_ref,
-    persist_key_ref,
-    persist_value_ref,
-    state_ref,
-    decode_memory_ref,
-    page_ref,
-    out_ref,
-    tail_ref,
-    memory_ref,
-    momentum_ref,
-    projected,
-    cache,
-    score,
-    arrival,
-):
+class Rate:
+    def __init__(self, rates_ref, kind):
+        self.rates_ref, self.start = rates_ref, kind * (PCH // MCH)
+
+    def __getitem__(self, block):
+        return self.rates_ref[self.start + block]
+
+
+def first_kernel(*refs):
+    token_refs, packet_refs = refs[0:4], refs[4:6]
+    whole_ref, rates_ref, persist_ref, decode_memory_ref, page_ref = refs[6:11]
+    out_ref, tail_ref, memory_ref, momentum_ref = refs[11:15]
+    projected, cache, score, arrival = refs[15:]
     for request in range(DEC_DEV):
         for place in range(PAGES):
             pltpu.make_async_copy(
-                page_ref.at[table_ref[request * PAGES + place]],
+                page_ref.at[whole_ref[request * PAGES + place]],
                 cache.at[request, pl.ds(place * 2 * PAGE, 2 * PAGE)],
                 arrival.at[request],
             ).start()
-    projected[...] = project((token_0_ref, token_1_ref, token_2_ref, token_3_ref), weight_ref)
-    memory = jnp.concatenate([state_ref[s, 0:8, :] for s in range(16)], axis=0)
-    momentum = jnp.concatenate([state_ref[s, 8:16, :] for s in range(16)], axis=0)
-    persist_key, persist_value = persist_key_ref[...], persist_value_ref[...]
-    rates = (forget_ref, keep_ref, learn_ref)
+    projected[...] = project(token_refs, *packet_refs)
+    memory, momentum = own_states(lax.axis_index("col").astype(F32), packet_refs)
+    persist_key, persist_value = persist_ref[0:PERS, :], persist_ref[PERS:, :]
+    rates = [Rate(rates_ref, kind) for kind in range(3)]
     memory, momentum = prefill(
         0, projected, persist_key, persist_value, memory, momentum, rates, out_ref, 0
     )
     memory_ref[...] = memory
     momentum_ref[...] = momentum
     tail_ref[...] = decode(
-        length_ref, projected, persist_key, persist_value, decode_memory_ref, cache, score, arrival
-    )
-
-
-def second_kernel(
-    forget_ref,
-    keep_ref,
-    learn_ref,
-    token_0_ref,
-    token_1_ref,
-    token_2_ref,
-    token_3_ref,
-    weight_ref,
-    persist_key_ref,
-    persist_value_ref,
-    memory_in_ref,
-    momentum_in_ref,
-    first_ref,
-    tail_ref,
-    out_ref,
-    memory_ref,
-    momentum_ref,
-    projected,
-):
-    projected[...] = project((token_0_ref, token_1_ref, token_2_ref, token_3_ref), weight_ref)
+        whole_ref, projected, persist_key, persist_value, decode_memory_ref, cache, score, arrival
+    )
+
+
+def second_kernel(*refs):
+    token_refs, packet_refs, rates_ref, persist_ref = refs[0:4], refs[4:6], refs[6], refs[7]
+    memory_in_ref, momentum_in_ref, first_ref, tail_ref = refs[8:12]
+    out_ref, memory_ref, momentum_ref, projected = refs[12:]
+    projected[...] = project(token_refs, *packet_refs)
     memory, momentum = prefill(
         HALF // MCH,
         projected,
-        persist_key_ref[...],
-        persist_value_ref[...],
+        persist_ref[0:PERS, :],
+        persist_ref[PERS:, :],
         memory_in_ref[...],
         momentum_in_ref[...],
-        (forget_ref, keep_ref, learn_ref),
+        [Rate(rates_ref, kind) for kind in range(3)],
         out_ref,
         HALF,
     )
@@ -251,7 +247,10 @@
 IN_VMEM = pl.BlockSpec(memory_space=pltpu.VMEM)
 
 
-def first_part(table, length, rates, chunks, weight, keys, values, state, decode_memory, pages):
+IN_HBM = pl.BlockSpec(memory_space=pltpu.HBM)
+
+
+def first_part(whole, rates, chunks, packets, persist, decode_memory, pages):
     return pl.pallas_call(
         first_kernel,
         out_shape=(
@@ -260,7 +259,7 @@
             jax.ShapeDtypeStruct((HD, HD), F32),
             jax.ShapeDtypeStruct((HD, HD), F32),
         ),
-        in_specs=[IN_SMEM] * 5 + [IN_VMEM] * 9 + [pl.BlockSpec(memory_space=pltpu.HBM)],
+        in_specs=[IN_VMEM] * 6 + [IN_SMEM] * 2 + [IN_VMEM] * 2 + [IN_HBM],
         out_specs=(IN_VMEM,) * 4,
         scratch_shapes=[
             pltpu.VMEM((HALF + EXTRA, 3 * HD), BF16),
@@ -268,22 +267,19 @@
             pltpu.VMEM((EXTRA, 2 * CACHE), F32),
             pltpu.SemaphoreType.DMA((DEC_DEV,)),
         ],
-        compiler_params=pltpu.CompilerParams(vmem_limit_bytes=48 * 2**20),
+        compiler_params=pltpu.CompilerParams(vmem_limit_bytes=46 * 2**20),
     )(
-        table.reshape(-1),
-        length,
-        *rates,
         *chunks,
-        weight,
-        keys,
-        values,
-        state,
-        decode_memory.reshape(DEC_DEV, HD, HD),
+        *packets,
+        whole,
+        rates,
+        persist,
+        decode_memory,
         pages.reshape(DEC_DEV * PAGES, 2 * PAGE, HD),
     )
 
 
-def second_part(rates, chunks, weight, keys, values, memory, momentum, first, tail):
+def second_part(rates, chunks, packets, persist, memory, momentum, first, tail):
     return pl.pallas_call(
         second_kernel,
         out_shape=(
@@ -291,19 +287,16 @@
             jax.ShapeDtypeStruct((HD, HD), F32),
             jax.ShapeDtypeStruct((HD, HD), F32),
         ),
-        in_specs=[IN_SMEM] * 3 + [IN_VMEM] * 11,
+        in_specs=[IN_VMEM] * 6 + [IN_SMEM] + [IN_VMEM] * 5,
         out_specs=(IN_VMEM,) * 3,
         scratch_shapes=[pltpu.VMEM((HALF, 3 * HD), BF16)],
         compiler_params=pltpu.CompilerParams(vmem_limit_bytes=16 * 2**20),
-    )(*rates, *chunks, weight, keys, values, memory, momentum, first, tail)
+    )(*chunks, *packets, rates, persist, memory, momentum, first, tail)
 
 
 def pair_up(piece):
-    z_hi = lax.axis_index("row") % 2
     other = permute(piece, lambda x, y, z_hi, z_lo, core: (x, y, 1 - z_hi, z_lo, core))
-    return jnp.concatenate(
-        [jnp.where(z_hi == 0, piece, other), jnp.where(z_hi == 0, other, piece)], axis=1
-    )
+    return jnp.concatenate([piece, other], axis=1)
 
 
 def spread_rows(pair):
@@ -317,47 +310,40 @@
     return [pair, *came]
 
 
-def gather_weight(block):
-    y = lax.axis_index("row") // 2
-    x = lax.axis_index("col") // 4
-    z_lo = lax.axis_index("col") // 2 % 2
-    core = lax.axis_index("col") % 2
-    other = permute(block, lambda x, y, z_hi, z_lo, core: (x, y, z_hi, 1 - z_lo, core))
-    pair = jnp.stack(
-        [jnp.where(z_lo == 0, block, other), jnp.where(z_lo == 0, other, block)], axis=0
-    )
-    shifted = [pair]
+def packet_kernel(destination_ref, weight_ref, memory_ref, momentum_ref, packet_ref):
+    for tile in range(3):
+        packet_ref[tile * MCH : tile * MCH + MCH, :] = weight_ref[:, tile * HD : tile * HD + HD]
+    states = jnp.concatenate([memory_ref[...], momentum_ref[...]], axis=0)
+    high = states.astype(BF16)
+    packet_ref[STATE : STATE + 2 * HD, :] = high
+    packet_ref[MARK:PACKET, :] = jnp.full((16, HD), destination_ref[0].astype(F32)).astype(BF16)
+
+
+def make_packet(weight, memory_in, momentum_in, destination):
+    return pl.pallas_call(
+        packet_kernel,
+        out_shape=jax.ShapeDtypeStruct((PACKET, HD), BF16),
+        in_specs=[IN_SMEM] + [IN_VMEM] * 3,
+        out_specs=IN_VMEM,
+    )(destination, weight, memory_in.reshape(HD, HD), momentum_in.reshape(HD, HD))
+
+
+def gather_packets(packet, turned):
+    same = lax.axis_index("row") % 2 == lax.axis_index("col") // 2 % 2
+    other = permute(packet, lambda x, y, z_hi, z_lo, core: (x, y, z_hi, 1 - z_lo, core))
+    pair = jnp.stack([jnp.where(same, packet, other), jnp.where(same, other, packet)], axis=0)
+    pair, turned = lax.optimization_barrier((pair, turned))
+    near = [pair]
     for step in (1, 2, 3):
-        shifted.append(
+        near.append(
             permute(
                 pair,
                 lambda x, y, z_hi, z_lo, core, step=step: ((x + step) % 4, y, z_hi, z_lo, core),
             )
         )
-    ordered = []
-    for place in range(4):
-        chosen = shifted[3]
-        for step in (0, 1, 2):
-            chosen = jnp.where((2 * x - y + place) % 4 == step, shifted[step], chosen)
-        ordered.append(chosen)
-    mine = jnp.stack(ordered, axis=0)
-    theirs = permute(mine, lambda x, y, z_hi, z_lo, core: (x, y, z_hi, z_lo, 1 - core))
-    both = jnp.stack(
-        [jnp.where(core == 0, mine, theirs), jnp.where(core == 0, theirs, mine)], axis=2
-    )
-    return both.reshape(-1, block.shape[1])
-
-
-def deal_states(memory_in, momentum_in, destination):
-    slots = 16
-    mark = jnp.broadcast_to(destination.astype(F32).reshape(1, 1, 1), (slots, 8, HD))
-    pieces = jnp.concatenate(
-        [memory_in.reshape(slots, 8, HD), momentum_in.reshape(slots, 8, HD), mark], axis=1
-    )
-    spread = lax.all_to_all(pieces, "col", split_axis=0, concat_axis=0, tiled=True)
-    target = spread[:, 16, 0].astype(jnp.int32)
-    chosen = target[None, :] == jnp.arange(slots, dtype=jnp.int32)[:, None]
-    return jnp.sum(jnp.where(chosen[:, :, None, None], spread[None, :, :16, :], 0.0), axis=1)
+    near = jnp.stack(near, axis=0)
+    far = permute(near, lambda x, y, z_hi, z_lo, core: (x, y, z_hi, z_lo, 1 - core))
+    return (near, far), turned
 
 
 def shards(
@@ -380,42 +366,63 @@
     kept = jnp.where(core == 0, lower, upper)
     sent = jnp.where(core == 0, upper, lower)
     came = permute(sent, lambda x, y, z_hi, z_lo, core: (x, y, z_hi, z_lo, 1 - core))
-    came, memory_in, momentum_in, qkv_weight = lax.optimization_barrier(
-        (came, memory_in, momentum_in, qkv_weight)
-    )
-    own = jnp.concatenate(
-        [jnp.where(core == 0, kept, came), jnp.where(core == 0, came, kept)], axis=1
+    own = jnp.concatenate([kept, came], axis=1)
+    (
+        own,
+        persistent,
+        page_table,
+        cache_len,
+        forget_rate,
+        keep_rate,
+        learn_rate,
+        decode_memory,
+    ) = lax.optimization_barrier(
+        (
+            own,
+            persistent,
+            page_table,
+            cache_len,
+            forget_rate,
+            keep_rate,
+            learn_rate,
+            decode_memory,
+        )
     )
     parts = [
         jnp.concatenate([own[:HALF], jnp.pad(own[PCH:], ((0, PADDED - ROWS), (0, 0)))], axis=0),
         own[HALF:PCH],
     ]
-    turned = [
-        permute(part, lambda x, y, z_hi, z_lo, core: (y, (x + y) % 4, z_lo, z_hi, core))
-        for part in parts
-    ]
-    pairs = [pair_up(part) for part in turned]
-    weight = gather_weight(qkv_weight)
+    turned = permute(
+        jnp.concatenate(parts, axis=0),
+        lambda x, y, z_hi, z_lo, core: (y, (x + y) % 4, z_lo, z_hi, core),
+    )
+    packets, turned = gather_packets(
+        make_packet(qkv_weight, memory_in, momentum_in, destination), turned
+    )
+    pair = pair_up(turned)
+    pairs = [pair[: HALF + EXTRA], pair[HALF + EXTRA :]]
     chunks = [spread_rows(pair) for pair in pairs]
-    dealt = deal_states(memory_in, momentum_in, destination)
-    dealt, chunks[0][1] = lax.optimization_barrier((dealt, chunks[0][1]))
-    state = lax.all_to_all(dealt, "col", split_axis=0, concat_axis=0, tiled=True)
-    rates = [rate.reshape(-1) for rate in (forget_rate, keep_rate, learn_rate)]
-    keys, values = persistent[:, 0], persistent[:, 1]
+    rates = jnp.concatenate(
+        [rate.reshape(-1) for rate in (forget_rate, keep_rate, learn_rate)], axis=0
+    )
+    whole = jnp.concatenate([page_table.reshape(-1), cache_len], axis=0)
+    persist = jnp.concatenate([persistent[:, 0], persistent[:, 1]], axis=0)
+    decode_memory = decode_memory.reshape(DEC_DEV, HD, HD)
+    high = decode_memory.astype(BF16)
+    decode_parts = jnp.concatenate(
+        [high, (decode_memory - high.astype(F32)).astype(BF16)], axis=1
+    )
     first, tail, memory, momentum = first_part(
-        page_table,
-        cache_len,
+        whole,
         rates,
         chunks[0],
-        weight,
-        keys,
-        values,
-        state,
-        decode_memory,
+        packets,
+        persist,
+        decode_parts,
         cache_pages,
     )
     heads_out, memory, momentum = second_part(
-        rates, chunks[1], weight, keys, values, memory, momentum, first, tail
+        rates, chunks[1], packets, persist, memory, momentum, first, tail
     )
     return heads_out, memory[None, None], momentum[None, None]
 

time: 84.2 us -> 75.8 us (0.900); the launches traced: 83.6 us -> 74.3 us
  starting transfers between devices: 41.5 us -> 30.7 us
  other arithmetic: 4.85 us -> 1.55 us
  Pallas kernels: 15.5 us -> 17.4 us
  waiting for transfers between devices: 18.3 us -> 19.9 us
  local copies, waits for them, and re-layouts: 1.82 us -> 3.17 us
    all_to_all x2 -> x0, starting transfers between devices: 13 us -> none  [the longest x1 7.65 us: shards(): lax.all_to_all(dealt, 'col', split_axis=0, concat_axis=0, tiled=True)]
    ppermute x16 -> x14, waiting for transfers between devices: 17.3 us -> 19.9 us  [permute(): return lax.ppermute(values, ('row', 'col'), moves(target))]
    ppermute x16 -> x14, starting transfers between devices: 28.5 us -> 30.7 us  [permute(): return lax.ppermute(values, ('row', 'col'), moves(target))]
    pallas_call x0 -> x1, Pallas kernels: none -> 1.56 us  [make_packet(): pl.pallas_call(packet_kernel, out_shape=jax.ShapeDtypeStruct((PACKET, HD)...]
    another operation x7 -> x3, other arithmetic: 2.13 us -> 1.07 us  [the longest x2 0.95 us: gather_packets(): jnp.stack([jnp.where(same, packet, other), jnp.where(same, other, packet)...]
    all_to_all x2 -> x0, waiting for transfers between devices: 1.03 us -> none  [the longest x1 1.03 us: deal_states(): lax.all_to_all(pieces, 'col', split_axis=0, concat_axis=0, tiled=True)]
    reduce_sum x1 -> x0, other arithmetic: 1 us -> none  [deal_states(): jnp.sum(jnp.where(chosen[:, :, None, None], spread[None, :, :16, :], 0.0)...]
  transfers between devices with their start and end apart: 18 -> 14, of which waited for: 7 -> 5; matrix products, arithmetic and copies ran while one was open for 6% -> 4% of each run, Pallas kernels for 13% -> 17%
where the time goes in v3:
time: 75.8 us; the launch traced here: 74.3 us
  starting transfers between devices  30.7 us (41%)
  waiting for transfers between devices  19.9 us (26%)
  Pallas kernels  17.4 us (23%)
  local copies, waits for them, and re-layouts  3.17 us (4%)
  between operations  1.56 us (2%)
  other arithmetic  1.55 us (2%)
    ppermute x14, starting transfers between devices, permute(): return lax.ppermute(values, ('row', 'col'), moves(target))  30.7 us
    ppermute x14, waiting for transfers between devices, permute(): return lax.ppermute(values, ('row', 'col'), moves(target))  19.9 us
    pallas_call x1, Pallas kernels, first_part(): pl.pallas_call(first_kernel, out_shape=(jax.ShapeDtypeStruct((HALF, HD),...  11.2 us
    pallas_call x1, Pallas kernels, second_part(): pl.pallas_call(second_kernel, out_shape=(jax.ShapeDtypeStruct((ROWS, HD),...  4.64 us
    pallas_call x1, Pallas kernels, make_packet(): pl.pallas_call(packet_kernel, out_shape=jax.ShapeDtypeStruct((PACKET, HD)...  1.56 us
  transfers between devices with their start and end apart: 14, of which 5 were waited for; matrix products, arithmetic and copies ran while one was open for 4% of the time, Pallas kernels for 17%

profile of v3, /device:TPU:1, one launch (start us, length us, event | category | flops | bytes accessed | tf_op | source)
XLA Modules:
  0.0 74.3 jit_solution(13424195984419201011)
XLA Ops:
  0.7 1.1 %fusion.5 = (bf16[1028,64]{0,1:T(8,128)(2,1)S(1)}, bf16[1028,64]{0,1:T(8,128)(2,1)S(1)}) fusion(bf16[2056,64]{0,1:T(8,128)(2,1)} %param.13), kind=kLoop, calls=%fused_computation.24 | loop fusion | bytes 526336 | tf_op jit(solution)/shard_map/slice | solution.py:365
  1.8 0.2 copy.20
  2.0 0.2 copy.21
  2.4 1.5 %collective-permute-start.1 = (bf16[1028,64]{1,0:T(8,128)(2,1)S(1)}, bf16[1028,64]{1,0:T(8,128)(2,1)S(1)}, u32[]{:S(2)}, u32[]{:S(2)}) collective-permute-start(bf16[1028,64]{1,0:T(8,128)(2,1)S(1)} %get-tuple-element.40), channel_id=1, source_target_pairs={{0,1},{1,0},{2,3},{3,2},{16,17},{17,16},{18,19},{19,18},{32,33},{3... | collective-permute-start | bytes 394760 | tf_op jit(solution)/shard_map/ppermute | solution.py:42
  4.5 1.6 %shard_map.148 = bf16[464,128]{1,0:T(8,128)(2,1)} custom-call(s32[1]{0:T(128)S(6)} %copy.23.destination_ref, bf16[64,384]{1,0:T(8,128)(2,1)} %weight_ref.1, f32[128,128]{1,0:T(8,128)} %bitcast.31, f32[128,128]{1,0:T(8,128)} %bitcast.32), custom_call_target="tpu_custom_call" | custom-call | tf_op jit(solution)/shard_map/pallas_call | solution.py:323
  6.1 1.7 %collective-permute-start = (bf16[464,128]{1,0:T(8,128)(2,1)}, bf16[464,128]{1,0:T(8,128)(2,1)S(1)}, u32[]{:S(2)}, u32[]{:S(2)}) collective-permute-start(bf16[464,128]{1,0:T(8,128)(2,1)} %shard_map.148), channel_id=1, source_target_pairs={{0,2},{1,3},{2,0},{3,1},{16,18},{17,19},{18,16},{19,17},{32,34},{3... | collective-permute-start | bytes 356360 | tf_op jit(solution)/shard_map/ppermute | solution.py:42
  7.8 0.2 pad_maximum_fusion.1
  8.0 0.7 collective-permute-start.2
  8.7 2.9 %collective-permute-done = bf16[464,128]{1,0:T(8,128)(2,1)S(1)} collective-permute-done((bf16[464,128]{1,0:T(8,128)(2,1)}, bf16[464,128]{1,0:T(8,128)(2,1)S(1)}, u32[]{:S(2)}, u32[]{:S(2)}) %collective-permute-start) | collective-permute-done | bytes 118816 | tf_op jit(solution)/shard_map/ppermute | solution.py:42
  11.6 0.9 %select_bitcast_fusion.1 = (bf16[1,464,128]{2,1,0:T(8,128)(2,1)S(1)}, bf16[1,464,128]{2,1,0:T(8,128)(2,1)S(1)}) fusion(bf16[464,128]{1,0:T(8,128)(2,1)} %shard_map.148, bf16[464,128]{1,0:T(8,128)(2,1)S(1)} %collective-permute-done, pred[]{:T(512)S(6)} %eq.11), kind=kLoop, calls=%fused_computation.16 | loop fusion | flops 118784 | bytes 475137 | tf_op jit(solution)/shard_map/stack | solution.py:334
  12.5 8.7 %collective-permute-start.7 = (bf16[2,464,128]{2,1,0:T(8,128)(2,1)S(1)}, bf16[2,464,128]{2,1,0:T(8,128)(2,1)S(1)}, u32[]{:S(2)}, u32[]{:S(2)}) collective-permute-start(bf16[2,464,128]{2,1,0:T(8,128)(2,1)S(1)} %pad_maximum_fusion.3), channel_id=1, source_target_pairs={{0,4},{1,5},{2,6},{3,7},{16,20},{17,21},{18,22},{19,23},{32,36},{3... | collective-permute-start | bytes 712712 | tf_op jit(solution)/shard_map/ppermute | solution.py:42
  21.3 6.3 %collective-permute-start.8 = (bf16[2,464,128]{2,1,0:T(8,128)(2,1)S(1)}, bf16[2,464,128]{2,1,0:T(8,128)(2,1)S(1)}, u32[]{:S(2)}, u32[]{:S(2)}) collective-permute-start(bf16[2,464,128]{2,1,0:T(8,128)(2,1)S(1)} %pad_maximum_fusion.3), channel_id=1, source_target_pairs={{0,8},{1,9},{2,10},{3,11},{16,24},{17,25},{18,26},{19,27},{32,40},... | collective-permute-start | bytes 712712 | tf_op jit(solution)/shard_map/ppermute | solution.py:42
  27.6 0.7 copy.18
  28.3 0.8 %reshape.35 = s32[64]{0:T(128)S(1)} reshape(s32[4,16]{1,0:T(4,128)} %param.17) | data formatting | bytes 512 | tf_op jit(solution)/shard_map/reshape | solution.py:408
  29.1 1.6 %collective-permute-start.3 = (bf16[1040,128]{1,0:T(8,128)(2,1)S(1)}, bf16[1040,128]{1,0:T(8,128)(2,1)S(1)}, u32[]{:S(2)}, u32[]{:S(2)}) collective-permute-start(bf16[1040,128]{1,0:T(8,128)(2,1)S(1)} %collective-permute-done.2), channel_id=1, source_target_pairs={{0,16},{1,17},{2,18},{3,19},{16,0},{17,1},{18,2},{19,3},{32,48},{3... | collective-permute-start | bytes 798728 | tf_op jit(solution)/shard_map/ppermute | solution.py:42
  30.7 1.0 %collective-permute-done.7 = bf16[2,464,128]{2,1,0:T(8,128)(2,1)S(1)} collective-permute-done((bf16[2,464,128]{2,1,0:T(8,128)(2,1)S(1)}, bf16[2,464,128]{2,1,0:T(8,128)(2,1)S(1)}, u32[]{:S(2)}, u32[]{:S(2)}) %collective-permute-start.7) | collective-permute-done | bytes 237600 | tf_op jit(solution)/shard_map/ppermute | solution.py:42
  31.7 5.9 %collective-permute-done.8 = bf16[2,464,128]{2,1,0:T(8,128)(2,1)S(1)} collective-permute-done((bf16[2,464,128]{2,1,0:T(8,128)(2,1)S(1)}, bf16[2,464,128]{2,1,0:T(8,128)(2,1)S(1)}, u32[]{:S(2)}, u32[]{:S(2)}) %collective-permute-start.8) | collective-permute-done | bytes 237600 | tf_op jit(solution)/shard_map/ppermute | solution.py:42
  37.7 1.9 %collective-permute-start.10 = (bf16[4,2,464,128]{3,2,1,0:T(8,128)(2,1)S(1)}, bf16[4,2,464,128]{3,2,1,0:T(8,128)(2,1)S(1)}, u32[]{:S(2)}, u32[]{:S(2)}) collective-permute-start(bf16[4,2,464,128]{3,2,1,0:T(8,128)(2,1)S(1)} %pad_maximum_fusion.refs_4_), channel_id=1, source_target_pairs={{0,1},{1,0},{2,3},{3,2},{16,17},{17,16},{18,19},{19,18},{32,33},{3... | collective-permute-start | bytes 2850824 | tf_op jit(solution)/shard_map/ppermute | solution.py:42
  39.9 6.4 %collective-permute-start.12 = (bf16[528,256]{1,0:T(8,128)(2,1)S(1)}, bf16[528,256]{1,0:T(8,128)(2,1)S(1)}, u32[]{:S(2)}, u32[]{:S(2)}) collective-permute-start(bf16[528,256]{1,0:T(8,128)(2,1)S(1)} %slice.39.refs_0_), channel_id=1, source_target_pairs={{0,64},{1,65},{2,66},{3,67},{16,80},{17,81},{18,82},{19,83},{32,96... | collective-permute-start | bytes 811016 | tf_op jit(solution)/shard_map/ppermute | solution.py:42
  46.5 1.5 %collective-permute-start.4 = (bf16[512,256]{1,0:T(8,128)(2,1)S(1)}, bf16[512,256]{1,0:T(8,128)(2,1)S(1)}, u32[]{:S(2)}, u32[]{:S(2)}) collective-permute-start(bf16[512,256]{1,0:T(8,128)(2,1)S(1)} %slice.36.refs_0_), channel_id=1, source_target_pairs={{0,32},{1,33},{2,34},{3,35},{16,48},{17,49},{18,50},{19,51},{32,64... | collective-permute-start | bytes 786440 | tf_op jit(solution)/shard_map/ppermute | solution.py:42
  48.0 3.5 %collective-permute-done.11.refs_1_ = bf16[528,256]{1,0:T(8,128)(2,1)S(1)} collective-permute-done((bf16[528,256]{1,0:T(8,128)(2,1)S(1)}, bf16[528,256]{1,0:T(8,128)(2,1)S(1)}, u32[]{:S(2)}, u32[]{:S(2)}) %collective-permute-start.11) | collective-permute-done | bytes 270368 | tf_op jit(solution)/shard_map/ppermute | solution.py:42
  51.7 6.6 %collective-permute-done.12.refs_2_ = bf16[528,256]{1,0:T(8,128)(2,1)S(1)} collective-permute-done((bf16[528,256]{1,0:T(8,128)(2,1)S(1)}, bf16[528,256]{1,0:T(8,128)(2,1)S(1)}, u32[]{:S(2)}, u32[]{:S(2)}) %collective-permute-start.12) | collective-permute-done | bytes 270368 | tf_op jit(solution)/shard_map/ppermute | solution.py:42
  58.4 11.2 %shard_map.149 = (bf16[512,128]{1,0:T(8,128)(2,1)S(1)}, bf16[16,128]{1,0:T(8,128)(2,1)S(1)}, f32[128,128]{1,0:T(8,128)S(1)}, f32[128,128]{1,0:T(8,128)S(1)}) custom-call(bf16[528,256]{1,0:T(8,128)(2,1)S(1)} %slice.39.refs_0_, bf16[528,256]{1,0:T(8,128)(2,1)S(1)} %collective-permute-done.11.refs_1_, bf16[528,256]{1,0:T(8,128)(2,1)S(1)} %collective-permute-done.12.refs_2_, ...), custom_call_target="tpu_custom_call" | custom-call | tf_op jit(solution)/shard_map/pallas_call | solution.py:254
  69.6 4.6 %shard_map.150 = (bf16[1028,128]{1,0:T(8,128)(2,1)}, f32[128,128]{1,0:T(8,128)}, f32[128,128]{1,0:T(8,128)}) custom-call(bf16[512,256]{1,0:T(8,128)(2,1)S(1)} %slice.36.refs_0_, bf16[512,256]{1,0:T(8,128)(2,1)S(1)} %collective-permute-done.4.refs_1_, bf16[512,256]{1,0:T(8,128)(2,1)S(1)} %collective-permute-done.5.refs_2_, ...), custom_call_target="tpu_custom_call" | custom-call | tf_op jit(solution)/shard_map/pallas_call | solution.py:283
  (40 shorter events, 1.0 us)
Async XLA Ops:
  0.6 45.7 %copy-start.4 = (s32[4]{0:T(128)S(1)}, s32[4]{0:T(128)}, u32[]{:S(2)}) copy-start(s32[4]{0:T(128)} %param.18) | copy-start | bytes 52
  0.6 57.6 %copy-start.3 = (f32[1,1,16]{2,1,0:T(1,128)S(1)}, f32[1,1,16]{2,1,0:T(1,128)}, u32[]{:S(2)}) copy-start(f32[1,1,16]{2,1,0:T(1,128)} %param.22) | copy-start | bytes 196
  0.7 57.6 %copy-start.2 = (f32[1,1,16]{2,1,0:T(1,128)S(1)}, f32[1,1,16]{2,1,0:T(1,128)}, u32[]{:S(2)}) copy-start(f32[1,1,16]{2,1,0:T(1,128)} %param.23) | copy-start | bytes 196
  0.7 57.6 %copy-start.1 = (f32[1,1,16]{2,1,0:T(1,128)S(1)}, f32[1,1,16]{2,1,0:T(1,128)}, u32[]{:S(2)}) copy-start(f32[1,1,16]{2,1,0:T(1,128)} %param.24) | copy-start | bytes 196
  0.7 45.7 %copy-start = (f32[4,1,128,128]{3,2,1,0:T(8,128)S(1)}, f32[4,1,128,128]{3,2,1,0:T(8,128)}, u32[]{:S(2)}) copy-start(f32[4,1,128,128]{3,2,1,0:T(8,128)} %param.25) | copy-start | bytes 786436
  2.4 5.4 %collective-permute-start.1 = (bf16[1028,64]{1,0:T(8,128)(2,1)S(1)}, bf16[1028,64]{1,0:T(8,128)(2,1)S(1)}, u32[]{:S(2)}, u32[]{:S(2)}) collective-permute-start(bf16[1028,64]{1,0:T(8,128)(2,1)S(1)} %get-tuple-element.40), channel_id=1, source_target_pairs={{0,1},{1,0},{2,3},{3,2},{16,17},{17,16},{18,19},{19,18},{32,33},{3... | collective-permute-start | bytes 394760 | tf_op jit(solution)/shard_map/ppermute | solution.py:42
  6.1 5.5 %collective-permute-start = (bf16[464,128]{1,0:T(8,128)(2,1)}, bf16[464,128]{1,0:T(8,128)(2,1)S(1)}, u32[]{:S(2)}, u32[]{:S(2)}) collective-permute-start(bf16[464,128]{1,0:T(8,128)(2,1)} %shard_map.148), channel_id=1, source_target_pairs={{0,2},{1,3},{2,0},{3,1},{16,18},{17,19},{18,16},{19,17},{32,34},{3... | collective-permute-start | bytes 356360 | tf_op jit(solution)/shard_map/ppermute | solution.py:42
  8.0 4.5 %collective-permute-start.2 = (bf16[1040,128]{1,0:T(8,128)(2,1)S(1)}, bf16[1040,128]{1,0:T(8,128)(2,1)S(1)}, u32[]{:S(2)}, u32[]{:S(2)}) collective-permute-start(bf16[1040,128]{1,0:T(8,128)(2,1)S(1)} %fusion.3), channel_id=1, source_target_pairs={{0,0},{1,1},{2,16},{3,17},{16,2},{17,3},{18,18},{19,19},{32,36},{3... | collective-permute-start | bytes 798728 | tf_op jit(solution)/shard_map/ppermute | solution.py:42
  12.5 19.1 %collective-permute-start.7 = (bf16[2,464,128]{2,1,0:T(8,128)(2,1)S(1)}, bf16[2,464,128]{2,1,0:T(8,128)(2,1)S(1)}, u32[]{:S(2)}, u32[]{:S(2)}) collective-permute-start(bf16[2,464,128]{2,1,0:T(8,128)(2,1)S(1)} %pad_maximum_fusion.3), channel_id=1, source_target_pairs={{0,4},{1,5},{2,6},{3,7},{16,20},{17,21},{18,22},{19,23},{32,36},{3... | collective-permute-start | bytes 712712 | tf_op jit(solution)/shard_map/ppermute | solution.py:42
  21.3 16.3 %collective-permute-start.8 = (bf16[2,464,128]{2,1,0:T(8,128)(2,1)S(1)}, bf16[2,464,128]{2,1,0:T(8,128)(2,1)S(1)}, u32[]{:S(2)}, u32[]{:S(2)}) collective-permute-start(bf16[2,464,128]{2,1,0:T(8,128)(2,1)S(1)} %pad_maximum_fusion.3), channel_id=1, source_target_pairs={{0,8},{1,9},{2,10},{3,11},{16,24},{17,25},{18,26},{19,27},{32,40},... | collective-permute-start | bytes 712712 | tf_op jit(solution)/shard_map/ppermute | solution.py:42
  27.6 10.0 %collective-permute-start.9 = (bf16[2,464,128]{2,1,0:T(8,128)(2,1)S(1)}, bf16[2,464,128]{2,1,0:T(8,128)(2,1)S(1)}, u32[]{:S(2)}, u32[]{:S(2)}) collective-permute-start(bf16[2,464,128]{2,1,0:T(8,128)(2,1)S(1)} %pad_maximum_fusion.3), channel_id=1, source_target_pairs={{0,12},{1,13},{2,14},{3,15},{16,28},{17,29},{18,30},{19,31},{32,44... | collective-permute-start | bytes 712712 | tf_op jit(solution)/shard_map/ppermute | solution.py:42
  29.1 10.6 %collective-permute-start.3 = (bf16[1040,128]{1,0:T(8,128)(2,1)S(1)}, bf16[1040,128]{1,0:T(8,128)(2,1)S(1)}, u32[]{:S(2)}, u32[]{:S(2)}) collective-permute-start(bf16[1040,128]{1,0:T(8,128)(2,1)S(1)} %collective-permute-done.2), channel_id=1, source_target_pairs={{0,16},{1,17},{2,18},{3,19},{16,0},{17,1},{18,2},{19,3},{32,48},{3... | collective-permute-start | bytes 798728 | tf_op jit(solution)/shard_map/ppermute | solution.py:42
  37.7 20.7 %collective-permute-start.10 = (bf16[4,2,464,128]{3,2,1,0:T(8,128)(2,1)S(1)}, bf16[4,2,464,128]{3,2,1,0:T(8,128)(2,1)S(1)}, u32[]{:S(2)}, u32[]{:S(2)}) collective-permute-start(bf16[4,2,464,128]{3,2,1,0:T(8,128)(2,1)S(1)} %pad_maximum_fusion.refs_4_), channel_id=1, source_target_pairs={{0,1},{1,0},{2,3},{3,2},{16,17},{17,16},{18,19},{19,18},{32,33},{3... | collective-permute-start | bytes 2850824 | tf_op jit(solution)/shard_map/ppermute | solution.py:42
  39.8 11.8 %collective-permute-start.11 = (bf16[528,256]{1,0:T(8,128)(2,1)S(1)}, bf16[528,256]{1,0:T(8,128)(2,1)S(1)}, u32[]{:S(2)}, u32[]{:S(2)}) collective-permute-start(bf16[528,256]{1,0:T(8,128)(2,1)S(1)} %slice.39.refs_0_), channel_id=1, source_target_pairs={{0,32},{1,33},{2,34},{3,35},{16,48},{17,49},{18,50},{19,51},{32,64... | collective-permute-start | bytes 811016 | tf_op jit(solution)/shard_map/ppermute | solution.py:42
  39.9 18.4 %collective-permute-start.12 = (bf16[528,256]{1,0:T(8,128)(2,1)S(1)}, bf16[528,256]{1,0:T(8,128)(2,1)S(1)}, u32[]{:S(2)}, u32[]{:S(2)}) collective-permute-start(bf16[528,256]{1,0:T(8,128)(2,1)S(1)} %slice.39.refs_0_), channel_id=1, source_target_pairs={{0,64},{1,65},{2,66},{3,67},{16,80},{17,81},{18,82},{19,83},{32,96... | collective-permute-start | bytes 811016 | tf_op jit(solution)/shard_map/ppermute | solution.py:42
  46.4 12.0 %collective-permute-start.13 = (bf16[528,256]{1,0:T(8,128)(2,1)S(1)}, bf16[528,256]{1,0:T(8,128)(2,1)S(1)}, u32[]{:S(2)}, u32[]{:S(2)}) collective-permute-start(bf16[528,256]{1,0:T(8,128)(2,1)S(1)} %slice.39.refs_0_), channel_id=1, source_target_pairs={{0,96},{1,97},{2,98},{3,99},{16,112},{17,113},{18,114},{19,115},{3... | collective-permute-start | bytes 811016 | tf_op jit(solution)/shard_map/ppermute | solution.py:42
  46.5 23.1 %collective-permute-start.4 = (bf16[512,256]{1,0:T(8,128)(2,1)S(1)}, bf16[512,256]{1,0:T(8,128)(2,1)S(1)}, u32[]{:S(2)}, u32[]{:S(2)}) collective-permute-start(bf16[512,256]{1,0:T(8,128)(2,1)S(1)} %slice.36.refs_0_), channel_id=1, source_target_pairs={{0,32},{1,33},{2,34},{3,35},{16,48},{17,49},{18,50},{19,51},{32,64... | collective-permute-start | bytes 786440 | tf_op jit(solution)/shard_map/ppermute | solution.py:42
  51.6 18.0 %collective-permute-start.5 = (bf16[512,256]{1,0:T(8,128)(2,1)S(1)}, bf16[512,256]{1,0:T(8,128)(2,1)S(1)}, u32[]{:S(2)}, u32[]{:S(2)}) collective-permute-start(bf16[512,256]{1,0:T(8,128)(2,1)S(1)} %slice.36.refs_0_), channel_id=1, source_target_pairs={{0,64},{1,65},{2,66},{3,67},{16,80},{17,81},{18,82},{19,83},{32,96... | collective-permute-start | bytes 786440 | tf_op jit(solution)/shard_map/ppermute | solution.py:42
  58.3 11.4 %collective-permute-start.6 = (bf16[512,256]{1,0:T(8,128)(2,1)S(1)}, bf16[512,256]{1,0:T(8,128)(2,1)S(1)}, u32[]{:S(2)}, u32[]{:S(2)}) collective-permute-start(bf16[512,256]{1,0:T(8,128)(2,1)S(1)} %slice.36.refs_0_), channel_id=1, source_target_pairs={{0,96},{1,97},{2,98},{3,99},{16,112},{17,113},{18,114},{19,115},{3... | collective-permute-start | bytes 786440 | tf_op jit(solution)/shard_map/ppermute | solution.py:42

commit v4 on v3

--- a/solution.py
+++ b/solution.py
@@ -64,7 +64,8 @@
     return lax.rsqrt(jnp.sum(wide * wide, axis=-1, keepdims=True) + EPSILON)
 
 
-HALF = PCH // 2
+HALF = 576
+REST = PCH - HALF
 EXTRA = PADDED - PCH
 STATE = 3 * MCH
 MARK = STATE + 2 * HD
@@ -102,14 +103,14 @@
 
 
 def prefill(
-    first, projected, persist_key, persist_value, memory, momentum, rates, out_ref, out_at
+    first, count, projected, persist_key, persist_value, memory, momentum, rates, out_ref, out_at
 ):
     forget_ref, keep_ref, learn_ref = rates
     blank = jnp.zeros((HD - MCH - PERS, HD), BF16)
     row_at = lax.broadcasted_iota(jnp.int32, (MCH, HD), 0)
     column_at = lax.broadcasted_iota(jnp.int32, (MCH, HD), 1)
     visible = (column_at <= row_at) | ((column_at >= MCH) & (column_at < MCH + PERS))
-    for step in range(HALF // MCH):
+    for step in range(count):
         block = first + step
         here = slice(step * MCH, step * MCH + MCH)
         query = projected[here, 0:HD]
@@ -138,7 +139,7 @@
 
 
 def decode(
-    whole_ref, projected, persist_key, persist_value, decode_memory_ref, cache, score, arrival
+    whole_ref, projected, persist_key, persist_value, decode_memory_ref, cache, score
 ):
     query = projected[HALF : HALF + EXTRA, 0:HD]
     key = projected[HALF : HALF + EXTRA, HD : 2 * HD]
@@ -146,7 +147,6 @@
     row = lax.broadcasted_iota(jnp.int32, (EXTRA, 1), 0)
     length = jnp.zeros((EXTRA, 1), jnp.int32)
     for request in range(DEC_DEV):
-        pltpu.make_async_copy(cache.at[request], cache.at[request], arrival.at[request]).wait()
         length = jnp.where(row == request, whole_ref[DEC_DEV * PAGES + request], length)
     for place in range(PAGES):
         span = slice(place * 2 * PAGE, place * 2 * PAGE + 2 * PAGE)
@@ -197,27 +197,20 @@
 
 def first_kernel(*refs):
     token_refs, packet_refs = refs[0:4], refs[4:6]
-    whole_ref, rates_ref, persist_ref, decode_memory_ref, page_ref = refs[6:11]
+    whole_ref, rates_ref, persist_ref, decode_memory_ref, cache = refs[6:11]
     out_ref, tail_ref, memory_ref, momentum_ref = refs[11:15]
-    projected, cache, score, arrival = refs[15:]
-    for request in range(DEC_DEV):
-        for place in range(PAGES):
-            pltpu.make_async_copy(
-                page_ref.at[whole_ref[request * PAGES + place]],
-                cache.at[request, pl.ds(place * 2 * PAGE, 2 * PAGE)],
-                arrival.at[request],
-            ).start()
+    projected, score = refs[15:]
     projected[...] = project(token_refs, *packet_refs)
     memory, momentum = own_states(lax.axis_index("col").astype(F32), packet_refs)
     persist_key, persist_value = persist_ref[0:PERS, :], persist_ref[PERS:, :]
     rates = [Rate(rates_ref, kind) for kind in range(3)]
     memory, momentum = prefill(
-        0, projected, persist_key, persist_value, memory, momentum, rates, out_ref, 0
+        0, HALF // MCH, projected, persist_key, persist_value, memory, momentum, rates, out_ref, 0
     )
     memory_ref[...] = memory
     momentum_ref[...] = momentum
     tail_ref[...] = decode(
-        whole_ref, projected, persist_key, persist_value, decode_memory_ref, cache, score, arrival
+        whole_ref, projected, persist_key, persist_value, decode_memory_ref, cache, score
     )
 
 
@@ -228,6 +221,7 @@
     projected[...] = project(token_refs, *packet_refs)
     memory, momentum = prefill(
         HALF // MCH,
+        REST // MCH,
         projected,
         persist_ref[0:PERS, :],
         persist_ref[PERS:, :],
@@ -250,7 +244,31 @@
 IN_HBM = pl.BlockSpec(memory_space=pltpu.HBM)
 
 
-def first_part(whole, rates, chunks, packets, persist, decode_memory, pages):
+def page_kernel(whole_ref, page_ref, cache_ref, arrival):
+    for request in range(DEC_DEV):
+        for place in range(PAGES):
+            pltpu.make_async_copy(
+                page_ref.at[whole_ref[request * PAGES + place]],
+                cache_ref.at[request, pl.ds(place * 2 * PAGE, 2 * PAGE)],
+                arrival.at[request],
+            ).start()
+    for request in range(DEC_DEV):
+        whole = cache_ref.at[request]
+        pltpu.make_async_copy(whole, whole, arrival.at[request]).wait()
+
+
+def order_pages(whole, pages):
+    return pl.pallas_call(
+        page_kernel,
+        out_shape=jax.ShapeDtypeStruct((DEC_DEV, 2 * CACHE, HD), BF16),
+        in_specs=[IN_SMEM, IN_HBM],
+        out_specs=IN_VMEM,
+        scratch_shapes=[pltpu.SemaphoreType.DMA((DEC_DEV,))],
+        compiler_params=pltpu.CompilerParams(vmem_limit_bytes=42 * 2**20),
+    )(whole, pages.reshape(DEC_DEV * PAGES, 2 * PAGE, HD))
+
+
+def first_part(whole, rates, chunks, packets, persist, decode_memory, cache):
     return pl.pallas_call(
         first_kernel,
         out_shape=(
@@ -259,15 +277,13 @@
             jax.ShapeDtypeStruct((HD, HD), F32),
             jax.ShapeDtypeStruct((HD, HD), F32),
         ),
-        in_specs=[IN_VMEM] * 6 + [IN_SMEM] * 2 + [IN_VMEM] * 2 + [IN_HBM],
+        in_specs=[IN_VMEM] * 6 + [IN_SMEM] * 2 + [IN_VMEM] * 3,
         out_specs=(IN_VMEM,) * 4,
         scratch_shapes=[
             pltpu.VMEM((HALF + EXTRA, 3 * HD), BF16),
-            pltpu.VMEM((DEC_DEV, 2 * CACHE, HD), BF16),
             pltpu.VMEM((EXTRA, 2 * CACHE), F32),
-            pltpu.SemaphoreType.DMA((DEC_DEV,)),
         ],
-        compiler_params=pltpu.CompilerParams(vmem_limit_bytes=46 * 2**20),
+        compiler_params=pltpu.CompilerParams(vmem_limit_bytes=16 * 2**20),
     )(
         *chunks,
         *packets,
@@ -275,7 +291,7 @@
         rates,
         persist,
         decode_memory,
-        pages.reshape(DEC_DEV * PAGES, 2 * PAGE, HD),
+        cache,
     )
 
 
@@ -289,7 +305,7 @@
         ),
         in_specs=[IN_VMEM] * 6 + [IN_SMEM] + [IN_VMEM] * 5,
         out_specs=(IN_VMEM,) * 3,
-        scratch_shapes=[pltpu.VMEM((HALF, 3 * HD), BF16)],
+        scratch_shapes=[pltpu.VMEM((REST, 3 * HD), BF16)],
         compiler_params=pltpu.CompilerParams(vmem_limit_bytes=16 * 2**20),
     )(*chunks, *packets, rates, persist, memory, momentum, first, tail)
 
@@ -328,11 +344,11 @@
     )(destination, weight, memory_in.reshape(HD, HD), momentum_in.reshape(HD, HD))
 
 
-def gather_packets(packet, turned):
+def gather_packets(packet, turned, cache):
     same = lax.axis_index("row") % 2 == lax.axis_index("col") // 2 % 2
     other = permute(packet, lambda x, y, z_hi, z_lo, core: (x, y, z_hi, 1 - z_lo, core))
+    other, turned, cache = lax.optimization_barrier((other, turned, cache))
     pair = jnp.stack([jnp.where(same, packet, other), jnp.where(same, other, packet)], axis=0)
-    pair, turned = lax.optimization_barrier((pair, turned))
     near = [pair]
     for step in (1, 2, 3):
         near.append(
@@ -343,7 +359,7 @@
         )
     near = jnp.stack(near, axis=0)
     far = permute(near, lambda x, y, z_hi, z_lo, core: (x, y, z_hi, z_lo, 1 - core))
-    return (near, far), turned
+    return (near, far), turned, cache
 
 
 def shards(
@@ -396,16 +412,16 @@
         jnp.concatenate(parts, axis=0),
         lambda x, y, z_hi, z_lo, core: (y, (x + y) % 4, z_lo, z_hi, core),
     )
-    packets, turned = gather_packets(
-        make_packet(qkv_weight, memory_in, momentum_in, destination), turned
-    )
+    whole = jnp.concatenate([page_table.reshape(-1), cache_len], axis=0)
+    cache = order_pages(whole, cache_pages)
+    packet = make_packet(qkv_weight, memory_in, momentum_in, destination)
+    packets, turned, cache = gather_packets(packet, turned, cache)
     pair = pair_up(turned)
     pairs = [pair[: HALF + EXTRA], pair[HALF + EXTRA :]]
     chunks = [spread_rows(pair) for pair in pairs]
     rates = jnp.concatenate(
         [rate.reshape(-1) for rate in (forget_rate, keep_rate, learn_rate)], axis=0
     )
-    whole = jnp.concatenate([page_table.reshape(-1), cache_len], axis=0)
     persist = jnp.concatenate([persistent[:, 0], persistent[:, 1]], axis=0)
     decode_memory = decode_memory.reshape(DEC_DEV, HD, HD)
     high = decode_memory.astype(BF16)
@@ -419,7 +435,7 @@
         packets,
         persist,
         decode_parts,
-        cache_pages,
+        cache,
     )
     heads_out, memory, momentum = second_part(
         rates, chunks[1], packets, persist, memory, momentum, first, tail

time: 75.8 us -> 72.2 us (0.953); the launches traced: 74.3 us -> 71.7 us
  waiting for transfers between devices: 19.9 us -> 16.1 us
  Pallas kernels: 17.4 us -> 18.2 us
    pallas_call x0 -> x1, Pallas kernels: none -> 4.03 us  [order_pages(): pl.pallas_call(page_kernel, out_shape=jax.ShapeDtypeStruct((DEC_DEV, 2 *...]
    ppermute x14, waiting for transfers between devices: 19.9 us -> 16.1 us  [permute(): return lax.ppermute(values, ('row', 'col'), moves(target))]
    pallas_call x1, Pallas kernels: 11.2 us -> 8.27 us  [first_part(): pl.pallas_call(first_kernel, out_shape=(jax.ShapeDtypeStruct((HALF, HD),...]
    another operation x2 -> x1, other arithmetic: 0.95 us -> 0.03 us  [gather_packets(): jnp.stack([jnp.where(same, packet, other), jnp.where(same, other, packet)...]
  transfers between devices with their start and end apart: 14 -> 14, of which waited for: 5 -> 6; matrix products, arithmetic and copies ran while one was open for 4% -> 4% of each run, Pallas kernels for 17% -> 19%
where the time goes in v4:
time: 72.2 us; the launch traced here: 71.7 us
  starting transfers between devices  31.4 us (43%)
  Pallas kernels  18.2 us (25%)
  waiting for transfers between devices  16.1 us (22%)
  local copies, waits for them, and re-layouts  3.12 us (4%)
  between operations  1.52 us (2%)
  other arithmetic  1.32 us (2%)
    ppermute x14, starting transfers between devices, permute(): return lax.ppermute(values, ('row', 'col'), moves(target))  31.4 us
    ppermute x14, waiting for transfers between devices, permute(): return lax.ppermute(values, ('row', 'col'), moves(target))  16.1 us
    pallas_call x1, Pallas kernels, first_part(): pl.pallas_call(first_kernel, out_shape=(jax.ShapeDtypeStruct((HALF, HD),...  8.27 us
    pallas_call x1, Pallas kernels, second_part(): pl.pallas_call(second_kernel, out_shape=(jax.ShapeDtypeStruct((ROWS, HD),...  4.36 us
    pallas_call x1, Pallas kernels, order_pages(): pl.pallas_call(page_kernel, out_shape=jax.ShapeDtypeStruct((DEC_DEV, 2 *...  4.03 us
    pallas_call x1, Pallas kernels, make_packet(): pl.pallas_call(packet_kernel, out_shape=jax.ShapeDtypeStruct((PACKET, HD)...  1.56 us
  transfers between devices with their start and end apart: 14, of which 6 were waited for; matrix products, arithmetic and copies ran while one was open for 4% of the time, Pallas kernels for 19%

profile of v4, /device:TPU:1, one launch (start us, length us, event | category | flops | bytes accessed | tf_op | source)
XLA Modules:
  0.0 71.7 jit_solution(15946016760637930880)
XLA Ops:
  0.6 1.1 %fusion.6 = (bf16[1028,64]{0,1:T(8,128)(2,1)S(1)}, bf16[1028,64]{0,1:T(8,128)(2,1)S(1)}) fusion(bf16[2056,64]{0,1:T(8,128)(2,1)} %param.13), kind=kLoop, calls=%fused_computation.25 | loop fusion | bytes 526336 | tf_op jit(solution)/shard_map/slice | solution.py:381
  2.2 1.5 %collective-permute-start.1 = (bf16[1028,64]{1,0:T(8,128)(2,1)S(1)}, bf16[1028,64]{1,0:T(8,128)(2,1)S(1)}, u32[]{:S(2)}, u32[]{:S(2)}) collective-permute-start(bf16[1028,64]{1,0:T(8,128)(2,1)S(1)} %get-tuple-element.42), channel_id=1, source_target_pairs={{0,1},{1,0},{2,3},{3,2},{16,17},{17,16},{18,19},{19,18},{32,33},{3... | collective-permute-start | bytes 394760 | tf_op jit(solution)/shard_map/ppermute | solution.py:42
  3.7 1.2 %collective-permute-done.1 = bf16[1028,64]{1,0:T(8,128)(2,1)S(1)} collective-permute-done((bf16[1028,64]{1,0:T(8,128)(2,1)S(1)}, bf16[1028,64]{1,0:T(8,128)(2,1)S(1)}, u32[]{:S(2)}, u32[]{:S(2)}) %collective-permute-start.1) | collective-permute-done | bytes 131616 | tf_op jit(solution)/shard_map/ppermute | solution.py:42
  5.1 0.7 collective-permute-start.2
  6.5 1.6 %shard_map.148 = bf16[464,128]{1,0:T(8,128)(2,1)} custom-call(s32[1]{0:T(128)S(6)} %copy.23.destination_ref, bf16[64,384]{1,0:T(8,128)(2,1)} %weight_ref.1, f32[128,128]{1,0:T(8,128)} %bitcast.31, f32[128,128]{1,0:T(8,128)} %bitcast.32), custom_call_target="tpu_custom_call" | custom-call | tf_op jit(solution)/shard_map/pallas_call | solution.py:339
  8.0 4.6 %collective-permute-start = (bf16[464,128]{1,0:T(8,128)(2,1)}, bf16[464,128]{1,0:T(8,128)(2,1)S(1)}, u32[]{:S(2)}, u32[]{:S(2)}) collective-permute-start(bf16[464,128]{1,0:T(8,128)(2,1)} %shard_map.148), channel_id=1, source_target_pairs={{0,2},{1,3},{2,0},{3,1},{16,18},{17,19},{18,16},{19,17},{32,34},{3... | collective-permute-start | bytes 356360 | tf_op jit(solution)/shard_map/ppermute | solution.py:42
  12.6 0.8 %reshape.32 = s32[64]{0:T(128)S(1)} reshape(s32[4,16]{1,0:T(4,128)} %param.17) | data formatting | bytes 512 | tf_op jit(solution)/shard_map/reshape | solution.py:415
  13.4 0.7 copy.18
  14.1 0.7 %pad_add_fusion.whole_ref.refs_6_ = s32[68]{0:T(128)S(1)} fusion(s32[4]{0:T(128)} %param.18, s32[64]{0:T(128)S(1)} %reshape.32), kind=kLoop, calls=%fused_computation.22 | loop fusion | flops 68 | bytes 544 | tf_op jit(solution)/shard_map/concatenate | solution.py:415
  14.8 4.0 %shard_map.149.refs_10_ = bf16[4,8192,128]{2,1,0:T(8,128)(2,1)S(1)} custom-call(s32[68]{0:T(128)S(1)} %pad_add_fusion.whole_ref.refs_6_, bf16[64,512,128]{2,1,0:T(8,128)(2,1)} %bitcast.27), custom_call_target="tpu_custom_call" | custom-call | tf_op jit(solution)/shard_map/pallas_call | solution.py:261
  19.0 2.3 %collective-permute-start.7 = (bf16[2,464,128]{2,1,0:T(8,128)(2,1)S(1)}, bf16[2,464,128]{2,1,0:T(8,128)(2,1)S(1)}, u32[]{:S(2)}, u32[]{:S(2)}) collective-permute-start(bf16[2,464,128]{2,1,0:T(8,128)(2,1)S(1)} %get-tuple-element.46), channel_id=1, source_target_pairs={{0,4},{1,5},{2,6},{3,7},{16,20},{17,21},{18,22},{19,23},{32,36},{3... | collective-permute-start | bytes 712712 | tf_op jit(solution)/shard_map/ppermute | solution.py:42
  21.2 3.8 %collective-permute-start.8 = (bf16[2,464,128]{2,1,0:T(8,128)(2,1)S(1)}, bf16[2,464,128]{2,1,0:T(8,128)(2,1)S(1)}, u32[]{:S(2)}, u32[]{:S(2)}) collective-permute-start(bf16[2,464,128]{2,1,0:T(8,128)(2,1)S(1)} %get-tuple-element.46), channel_id=1, source_target_pairs={{0,8},{1,9},{2,10},{3,11},{16,24},{17,25},{18,26},{19,27},{32,40},... | collective-permute-start | bytes 712712 | tf_op jit(solution)/shard_map/ppermute | solution.py:42
  25.1 1.4 %collective-permute-start.9 = (bf16[2,464,128]{2,1,0:T(8,128)(2,1)S(1)}, bf16[2,464,128]{2,1,0:T(8,128)(2,1)S(1)}, u32[]{:S(2)}, u32[]{:S(2)}) collective-permute-start(bf16[2,464,128]{2,1,0:T(8,128)(2,1)S(1)} %get-tuple-element.46), channel_id=1, source_target_pairs={{0,12},{1,13},{2,14},{3,15},{16,28},{17,29},{18,30},{19,31},{32,44... | collective-permute-start | bytes 712712 | tf_op jit(solution)/shard_map/ppermute | solution.py:42
  26.5 2.0 %collective-permute-start.3 = (bf16[1040,128]{1,0:T(8,128)(2,1)S(1)}, bf16[1040,128]{1,0:T(8,128)(2,1)S(1)}, u32[]{:S(2)}, u32[]{:S(2)}) collective-permute-start(bf16[1040,128]{1,0:T(8,128)(2,1)S(1)} %collective-permute-done.2), channel_id=1, source_target_pairs={{0,16},{1,17},{2,18},{3,19},{16,0},{17,1},{18,2},{19,3},{32,48},{3... | collective-permute-start | bytes 798728 | tf_op jit(solution)/shard_map/ppermute | solution.py:42
  29.1 5.9 %collective-permute-done.8 = bf16[2,464,128]{2,1,0:T(8,128)(2,1)S(1)} collective-permute-done((bf16[2,464,128]{2,1,0:T(8,128)(2,1)S(1)}, bf16[2,464,128]{2,1,0:T(8,128)(2,1)S(1)}, u32[]{:S(2)}, u32[]{:S(2)}) %collective-permute-start.8) | collective-permute-done | bytes 237600 | tf_op jit(solution)/shard_map/ppermute | solution.py:42
  35.2 1.9 %collective-permute-start.10 = (bf16[4,2,464,128]{3,2,1,0:T(8,128)(2,1)S(1)}, bf16[4,2,464,128]{3,2,1,0:T(8,128)(2,1)S(1)}, u32[]{:S(2)}, u32[]{:S(2)}) collective-permute-start(bf16[4,2,464,128]{3,2,1,0:T(8,128)(2,1)S(1)} %pad_maximum_fusion.refs_4_), channel_id=1, source_target_pairs={{0,1},{1,0},{2,3},{3,2},{16,17},{17,16},{18,19},{19,18},{32,33},{3... | collective-permute-start | bytes 2850824 | tf_op jit(solution)/shard_map/ppermute | solution.py:42
  37.4 6.3 %collective-permute-start.12 = (bf16[592,256]{1,0:T(8,128)(2,1)S(1)}, bf16[592,256]{1,0:T(8,128)(2,1)S(1)}, u32[]{:S(2)}, u32[]{:S(2)}) collective-permute-start(bf16[592,256]{1,0:T(8,128)(2,1)S(1)} %slice.39.refs_0_), channel_id=1, source_target_pairs={{0,64},{1,65},{2,66},{3,67},{16,80},{17,81},{18,82},{19,83},{32,96... | collective-permute-start | bytes 909320 | tf_op jit(solution)/shard_map/ppermute | solution.py:42
  43.7 1.5 %collective-permute-start.4 = (bf16[448,256]{1,0:T(8,128)(2,1)S(1)}, bf16[448,256]{1,0:T(8,128)(2,1)S(1)}, u32[]{:S(2)}, u32[]{:S(2)}) collective-permute-start(bf16[448,256]{1,0:T(8,128)(2,1)S(1)} %slice.36.refs_0_), channel_id=1, source_target_pairs={{0,32},{1,33},{2,34},{3,35},{16,48},{17,49},{18,50},{19,51},{32,64... | collective-permute-start | bytes 688136 | tf_op jit(solution)/shard_map/ppermute | solution.py:42
  45.2 4.8 %collective-permute-done.11.refs_1_ = bf16[592,256]{1,0:T(8,128)(2,1)S(1)} collective-permute-done((bf16[592,256]{1,0:T(8,128)(2,1)S(1)}, bf16[592,256]{1,0:T(8,128)(2,1)S(1)}, u32[]{:S(2)}, u32[]{:S(2)}) %collective-permute-start.11) | collective-permute-done | bytes 303136 | tf_op jit(solution)/shard_map/ppermute | solution.py:42
  50.0 5.3 %collective-permute-start.5 = (bf16[448,256]{1,0:T(8,128)(2,1)S(1)}, bf16[448,256]{1,0:T(8,128)(2,1)S(1)}, u32[]{:S(2)}, u32[]{:S(2)}) collective-permute-start(bf16[448,256]{1,0:T(8,128)(2,1)S(1)} %slice.36.refs_0_), channel_id=1, source_target_pairs={{0,64},{1,65},{2,66},{3,67},{16,80},{17,81},{18,82},{19,83},{32,96... | collective-permute-start | bytes 688136 | tf_op jit(solution)/shard_map/ppermute | solution.py:42
  55.3 2.2 %collective-permute-done.12.refs_2_ = bf16[592,256]{1,0:T(8,128)(2,1)S(1)} collective-permute-done((bf16[592,256]{1,0:T(8,128)(2,1)S(1)}, bf16[592,256]{1,0:T(8,128)(2,1)S(1)}, u32[]{:S(2)}, u32[]{:S(2)}) %collective-permute-start.12) | collective-permute-done | bytes 303136 | tf_op jit(solution)/shard_map/ppermute | solution.py:42
  57.6 8.3 %shard_map.150 = (bf16[576,128]{1,0:T(8,128)(2,1)S(1)}, bf16[16,128]{1,0:T(8,128)(2,1)S(1)}, f32[128,128]{1,0:T(8,128)S(1)}, f32[128,128]{1,0:T(8,128)S(1)}) custom-call(bf16[592,256]{1,0:T(8,128)(2,1)S(1)} %slice.39.refs_0_, bf16[592,256]{1,0:T(8,128)(2,1)S(1)} %collective-permute-done.11.refs_1_, bf16[592,256]{1,0:T(8,128)(2,1)S(1)} %collective-permute-done.12.refs_2_, ...), custom_call_target="tpu_custom_call" | custom-call | tf_op jit(solution)/shard_map/pallas_call | solution.py:272
  65.9 1.4 %collective-permute-done.5.refs_2_ = bf16[448,256]{1,0:T(8,128)(2,1)S(1)} collective-permute-done((bf16[448,256]{1,0:T(8,128)(2,1)S(1)}, bf16[448,256]{1,0:T(8,128)(2,1)S(1)}, u32[]{:S(2)}, u32[]{:S(2)}) %collective-permute-start.5) | collective-permute-done | bytes 229408 | tf_op jit(solution)/shard_map/ppermute | solution.py:42
  67.3 4.4 %shard_map.151 = (bf16[1028,128]{1,0:T(8,128)(2,1)}, f32[128,128]{1,0:T(8,128)}, f32[128,128]{1,0:T(8,128)}) custom-call(bf16[448,256]{1,0:T(8,128)(2,1)S(1)} %slice.36.refs_0_, bf16[448,256]{1,0:T(8,128)(2,1)S(1)} %collective-permute-done.4.refs_1_, bf16[448,256]{1,0:T(8,128)(2,1)S(1)} %collective-permute-done.5.refs_2_, ...), custom_call_target="tpu_custom_call" | custom-call | tf_op jit(solution)/shard_map/pallas_call | solution.py:299
  (42 shorter events, 1.9 us)
Async XLA Ops:
  2.2 2.7 %collective-permute-start.1 = (bf16[1028,64]{1,0:T(8,128)(2,1)S(1)}, bf16[1028,64]{1,0:T(8,128)(2,1)S(1)}, u32[]{:S(2)}, u32[]{:S(2)}) collective-permute-start(bf16[1028,64]{1,0:T(8,128)(2,1)S(1)} %get-tuple-element.42), channel_id=1, source_target_pairs={{0,1},{1,0},{2,3},{3,2},{16,17},{17,16},{18,19},{19,18},{32,33},{3... | collective-permute-start | bytes 394760 | tf_op jit(solution)/shard_map/ppermute | solution.py:42
  5.1 13.8 %collective-permute-start.2 = (bf16[1040,128]{1,0:T(8,128)(2,1)S(1)}, bf16[1040,128]{1,0:T(8,128)(2,1)S(1)}, u32[]{:S(2)}, u32[]{:S(2)}) collective-permute-start(bf16[1040,128]{1,0:T(8,128)(2,1)S(1)} %fusion.3), channel_id=1, source_target_pairs={{0,0},{1,1},{2,16},{3,17},{16,2},{17,3},{18,18},{19,19},{32,36},{3... | collective-permute-start | bytes 798728 | tf_op jit(solution)/shard_map/ppermute | solution.py:42
  8.0 10.8 %collective-permute-start = (bf16[464,128]{1,0:T(8,128)(2,1)}, bf16[464,128]{1,0:T(8,128)(2,1)S(1)}, u32[]{:S(2)}, u32[]{:S(2)}) collective-permute-start(bf16[464,128]{1,0:T(8,128)(2,1)} %shard_map.148), channel_id=1, source_target_pairs={{0,2},{1,3},{2,0},{3,1},{16,18},{17,19},{18,16},{19,17},{32,34},{3... | collective-permute-start | bytes 356360 | tf_op jit(solution)/shard_map/ppermute | solution.py:42
  14.8 4.1 %copy-start = (bf16[464,128]{1,0:T(8,128)(2,1)S(1)}, bf16[464,128]{1,0:T(8,128)(2,1)}, u32[]{:S(2)}) copy-start(bf16[464,128]{1,0:T(8,128)(2,1)} %shard_map.148) | copy-start | bytes 356356
  14.8 11.6 %copy-start.1 = (f32[4,1,128,128]{3,2,1,0:T(8,128)S(1)}, f32[4,1,128,128]{3,2,1,0:T(8,128)}, u32[]{:S(2)}) copy-start(f32[4,1,128,128]{3,2,1,0:T(8,128)} %param.25) | copy-start | bytes 786436
  14.8 42.7 %copy-start.2 = (f32[1,1,16]{2,1,0:T(1,128)S(1)}, f32[1,1,16]{2,1,0:T(1,128)}, u32[]{:S(2)}) copy-start(f32[1,1,16]{2,1,0:T(1,128)} %param.24) | copy-start | bytes 196
  14.8 42.7 %copy-start.3 = (f32[1,1,16]{2,1,0:T(1,128)S(1)}, f32[1,1,16]{2,1,0:T(1,128)}, u32[]{:S(2)}) copy-start(f32[1,1,16]{2,1,0:T(1,128)} %param.23) | copy-start | bytes 196
  14.8 42.7 %copy-start.4 = (f32[1,1,16]{2,1,0:T(1,128)S(1)}, f32[1,1,16]{2,1,0:T(1,128)}, u32[]{:S(2)}) copy-start(f32[1,1,16]{2,1,0:T(1,128)} %param.22) | copy-start | bytes 196
  19.0 10.1 %collective-permute-start.7 = (bf16[2,464,128]{2,1,0:T(8,128)(2,1)S(1)}, bf16[2,464,128]{2,1,0:T(8,128)(2,1)S(1)}, u32[]{:S(2)}, u32[]{:S(2)}) collective-permute-start(bf16[2,464,128]{2,1,0:T(8,128)(2,1)S(1)} %get-tuple-element.46), channel_id=1, source_target_pairs={{0,4},{1,5},{2,6},{3,7},{16,20},{17,21},{18,22},{19,23},{32,36},{3... | collective-permute-start | bytes 712712 | tf_op jit(solution)/shard_map/ppermute | solution.py:42
  21.2 13.8 %collective-permute-start.8 = (bf16[2,464,128]{2,1,0:T(8,128)(2,1)S(1)}, bf16[2,464,128]{2,1,0:T(8,128)(2,1)S(1)}, u32[]{:S(2)}, u32[]{:S(2)}) collective-permute-start(bf16[2,464,128]{2,1,0:T(8,128)(2,1)S(1)} %get-tuple-element.46), channel_id=1, source_target_pairs={{0,8},{1,9},{2,10},{3,11},{16,24},{17,25},{18,26},{19,27},{32,40},... | collective-permute-start | bytes 712712 | tf_op jit(solution)/shard_map/ppermute | solution.py:42
  25.1 10.0 %collective-permute-start.9 = (bf16[2,464,128]{2,1,0:T(8,128)(2,1)S(1)}, bf16[2,464,128]{2,1,0:T(8,128)(2,1)S(1)}, u32[]{:S(2)}, u32[]{:S(2)}) collective-permute-start(bf16[2,464,128]{2,1,0:T(8,128)(2,1)S(1)} %get-tuple-element.46), channel_id=1, source_target_pairs={{0,12},{1,13},{2,14},{3,15},{16,28},{17,29},{18,30},{19,31},{32,44... | collective-permute-start | bytes 712712 | tf_op jit(solution)/shard_map/ppermute | solution.py:42
  26.5 10.7 %collective-permute-start.3 = (bf16[1040,128]{1,0:T(8,128)(2,1)S(1)}, bf16[1040,128]{1,0:T(8,128)(2,1)S(1)}, u32[]{:S(2)}, u32[]{:S(2)}) collective-permute-start(bf16[1040,128]{1,0:T(8,128)(2,1)S(1)} %collective-permute-done.2), channel_id=1, source_target_pairs={{0,16},{1,17},{2,18},{3,19},{16,0},{17,1},{18,2},{19,3},{32,48},{3... | collective-permute-start | bytes 798728 | tf_op jit(solution)/shard_map/ppermute | solution.py:42
  35.2 22.5 %collective-permute-start.10 = (bf16[4,2,464,128]{3,2,1,0:T(8,128)(2,1)S(1)}, bf16[4,2,464,128]{3,2,1,0:T(8,128)(2,1)S(1)}, u32[]{:S(2)}, u32[]{:S(2)}) collective-permute-start(bf16[4,2,464,128]{3,2,1,0:T(8,128)(2,1)S(1)} %pad_maximum_fusion.refs_4_), channel_id=1, source_target_pairs={{0,1},{1,0},{2,3},{3,2},{16,17},{17,16},{18,19},{19,18},{32,33},{3... | collective-permute-start | bytes 2850824 | tf_op jit(solution)/shard_map/ppermute | solution.py:42
  37.3 12.7 %collective-permute-start.11 = (bf16[592,256]{1,0:T(8,128)(2,1)S(1)}, bf16[592,256]{1,0:T(8,128)(2,1)S(1)}, u32[]{:S(2)}, u32[]{:S(2)}) collective-permute-start(bf16[592,256]{1,0:T(8,128)(2,1)S(1)} %slice.39.refs_0_), channel_id=1, source_target_pairs={{0,32},{1,33},{2,34},{3,35},{16,48},{17,49},{18,50},{19,51},{32,64... | collective-permute-start | bytes 909320 | tf_op jit(solution)/shard_map/ppermute | solution.py:42
  37.4 20.1 %collective-permute-start.12 = (bf16[592,256]{1,0:T(8,128)(2,1)S(1)}, bf16[592,256]{1,0:T(8,128)(2,1)S(1)}, u32[]{:S(2)}, u32[]{:S(2)}) collective-permute-start(bf16[592,256]{1,0:T(8,128)(2,1)S(1)} %slice.39.refs_0_), channel_id=1, source_target_pairs={{0,64},{1,65},{2,66},{3,67},{16,80},{17,81},{18,82},{19,83},{32,96... | collective-permute-start | bytes 909320 | tf_op jit(solution)/shard_map/ppermute | solution.py:42
  43.6 14.0 %collective-permute-start.13 = (bf16[592,256]{1,0:T(8,128)(2,1)S(1)}, bf16[592,256]{1,0:T(8,128)(2,1)S(1)}, u32[]{:S(2)}, u32[]{:S(2)}) collective-permute-start(bf16[592,256]{1,0:T(8,128)(2,1)S(1)} %slice.39.refs_0_), channel_id=1, source_target_pairs={{0,96},{1,97},{2,98},{3,99},{16,112},{17,113},{18,114},{19,115},{3... | collective-permute-start | bytes 909320 | tf_op jit(solution)/shard_map/ppermute | solution.py:42
  43.7 22.3 %collective-permute-start.4 = (bf16[448,256]{1,0:T(8,128)(2,1)S(1)}, bf16[448,256]{1,0:T(8,128)(2,1)S(1)}, u32[]{:S(2)}, u32[]{:S(2)}) collective-permute-start(bf16[448,256]{1,0:T(8,128)(2,1)S(1)} %slice.36.refs_0_), channel_id=1, source_target_pairs={{0,32},{1,33},{2,34},{3,35},{16,48},{17,49},{18,50},{19,51},{32,64... | collective-permute-start | bytes 688136 | tf_op jit(solution)/shard_map/ppermute | solution.py:42
  50.0 17.3 %collective-permute-start.5 = (bf16[448,256]{1,0:T(8,128)(2,1)S(1)}, bf16[448,256]{1,0:T(8,128)(2,1)S(1)}, u32[]{:S(2)}, u32[]{:S(2)}) collective-permute-start(bf16[448,256]{1,0:T(8,128)(2,1)S(1)} %slice.36.refs_0_), channel_id=1, source_target_pairs={{0,64},{1,65},{2,66},{3,67},{16,80},{17,81},{18,82},{19,83},{32,96... | collective-permute-start | bytes 688136 | tf_op jit(solution)/shard_map/ppermute | solution.py:42
  57.5 9.8 %collective-permute-start.6 = (bf16[448,256]{1,0:T(8,128)(2,1)S(1)}, bf16[448,256]{1,0:T(8,128)(2,1)S(1)}, u32[]{:S(2)}, u32[]{:S(2)}) collective-permute-start(bf16[448,256]{1,0:T(8,128)(2,1)S(1)} %slice.36.refs_0_), channel_id=1, source_target_pairs={{0,96},{1,97},{2,98},{3,99},{16,112},{17,113},{18,114},{19,115},{3... | collective-permute-start | bytes 688136 | tf_op jit(solution)/shard_map/ppermute | solution.py:42

commit v5 on v4

--- a/solution.py
+++ b/solution.py
@@ -64,7 +64,7 @@
     return lax.rsqrt(jnp.sum(wide * wide, axis=-1, keepdims=True) + EPSILON)
 
 
-HALF = 576
+HALF = 640
 REST = PCH - HALF
 EXTRA = PADDED - PCH
 STATE = 3 * MCH
@@ -357,9 +357,14 @@
                 lambda x, y, z_hi, z_lo, core, step=step: ((x + step) % 4, y, z_hi, z_lo, core),
             )
         )
+    return near, turned, cache
+
+
+def exchange_packets(near, after):
+    near[3], _ = lax.optimization_barrier((near[3], after))
     near = jnp.stack(near, axis=0)
     far = permute(near, lambda x, y, z_hi, z_lo, core: (x, y, z_hi, z_lo, 1 - core))
-    return (near, far), turned, cache
+    return near, far
 
 
 def shards(
@@ -419,6 +424,7 @@
     pair = pair_up(turned)
     pairs = [pair[: HALF + EXTRA], pair[HALF + EXTRA :]]
     chunks = [spread_rows(pair) for pair in pairs]
+    packets = exchange_packets(packets, [chunks[0][1], chunks[0][2], chunks[0][3]])
     rates = jnp.concatenate(
         [rate.reshape(-1) for rate in (forget_rate, keep_rate, learn_rate)], axis=0
     )

time: 72.2 us -> 71.2 us (0.986)
  starting transfers between devices: 31.4 us -> 34.5 us
  waiting for transfers between devices: 16.1 us -> 13.3 us
    ppermute x14, starting transfers between devices: 31.4 us -> 34.5 us  [permute(): return lax.ppermute(values, ('row', 'col'), moves(target))]
    ppermute x14, waiting for transfers between devices: 16.1 us -> 13.3 us  [permute(): return lax.ppermute(values, ('row', 'col'), moves(target))]
  transfers between devices with their start and end apart: 14 -> 14, of which waited for: 6 -> 5; matrix products, arithmetic and copies ran while one was open for 4% -> 3% of each run, Pallas kernels for 19% -> 20%
where the time goes in v5:
time: 71.2 us; the launch traced here: 71 us
  starting transfers between devices  34.5 us (48%)
  Pallas kernels  17.9 us (25%)
  waiting for transfers between devices  13.3 us (19%)
  local copies, waits for them, and re-layouts  2.44 us (3%)
  between operations  1.53 us (2%)
  other arithmetic  1.33 us (2%)
    ppermute x14, starting transfers between devices, permute(): return lax.ppermute(values, ('row', 'col'), moves(target))  34.5 us
    ppermute x14, waiting for transfers between devices, permute(): return lax.ppermute(values, ('row', 'col'), moves(target))  13.3 us
    pallas_call x1, Pallas kernels, first_part(): pl.pallas_call(first_kernel, out_shape=(jax.ShapeDtypeStruct((HALF, HD),...  8.48 us
    pallas_call x1, Pallas kernels, order_pages(): pl.pallas_call(page_kernel, out_shape=jax.ShapeDtypeStruct((DEC_DEV, 2 *...  4.03 us
    pallas_call x1, Pallas kernels, second_part(): pl.pallas_call(second_kernel, out_shape=(jax.ShapeDtypeStruct((ROWS, HD),...  3.85 us
    pallas_call x1, Pallas kernels, make_packet(): pl.pallas_call(packet_kernel, out_shape=jax.ShapeDtypeStruct((PACKET, HD)...  1.56 us
  transfers between devices with their start and end apart: 14, of which 5 were waited for; matrix products, arithmetic and copies ran while one was open for 3% of the time, Pallas kernels for 20%

profile of v5, /device:TPU:1, one launch (start us, length us, event | category | flops | bytes accessed | tf_op | source)
XLA Modules:
  0.0 71.0 jit_solution(17208980058073396795)
XLA Ops:
  0.6 1.1 %fusion.6 = (bf16[1028,64]{0,1:T(8,128)(2,1)S(1)}, bf16[1028,64]{0,1:T(8,128)(2,1)S(1)}) fusion(bf16[2056,64]{0,1:T(8,128)(2,1)} %param.13), kind=kLoop, calls=%fused_computation.25 | loop fusion | bytes 526336 | tf_op jit(solution)/shard_map/slice | solution.py:386
  1.9 0.2 copy.21
  2.2 1.5 %collective-permute-start.1 = (bf16[1028,64]{1,0:T(8,128)(2,1)S(1)}, bf16[1028,64]{1,0:T(8,128)(2,1)S(1)}, u32[]{:S(2)}, u32[]{:S(2)}) collective-permute-start(bf16[1028,64]{1,0:T(8,128)(2,1)S(1)} %get-tuple-element.44), channel_id=1, source_target_pairs={{0,1},{1,0},{2,3},{3,2},{16,17},{17,16},{18,19},{19,18},{32,33},{3... | collective-permute-start | bytes 394760 | tf_op jit(solution)/shard_map/ppermute | solution.py:42
  3.7 1.2 %collective-permute-done.1 = bf16[1028,64]{1,0:T(8,128)(2,1)S(1)} collective-permute-done((bf16[1028,64]{1,0:T(8,128)(2,1)S(1)}, bf16[1028,64]{1,0:T(8,128)(2,1)S(1)}, u32[]{:S(2)}, u32[]{:S(2)}) %collective-permute-start.1) | collective-permute-done | bytes 131616 | tf_op jit(solution)/shard_map/ppermute | solution.py:42
  5.1 0.7 collective-permute-start.2
  6.5 1.6 %shard_map.148 = bf16[464,128]{1,0:T(8,128)(2,1)} custom-call(s32[1]{0:T(128)S(6)} %copy.23.destination_ref, bf16[64,384]{1,0:T(8,128)(2,1)} %weight_ref.1, f32[128,128]{1,0:T(8,128)} %bitcast.31, f32[128,128]{1,0:T(8,128)} %bitcast.32), custom_call_target="tpu_custom_call" | custom-call | tf_op jit(solution)/shard_map/pallas_call | solution.py:339
  8.0 4.6 %collective-permute-start = (bf16[464,128]{1,0:T(8,128)(2,1)}, bf16[464,128]{1,0:T(8,128)(2,1)S(1)}, u32[]{:S(2)}, u32[]{:S(2)}) collective-permute-start(bf16[464,128]{1,0:T(8,128)(2,1)} %shard_map.148), channel_id=1, source_target_pairs={{0,2},{1,3},{2,0},{3,1},{16,18},{17,19},{18,16},{19,17},{32,34},{3... | collective-permute-start | bytes 356360 | tf_op jit(solution)/shard_map/ppermute | solution.py:42
  12.6 0.8 %reshape.32 = s32[64]{0:T(128)S(1)} reshape(s32[4,16]{1,0:T(4,128)} %param.17) | data formatting | bytes 512 | tf_op jit(solution)/shard_map/reshape | solution.py:420
  13.4 0.7 %pad_add_fusion.whole_ref.refs_6_ = s32[68]{0:T(128)S(1)} fusion(s32[4]{0:T(128)} %param.18, s32[64]{0:T(128)S(1)} %reshape.32), kind=kLoop, calls=%fused_computation.22 | loop fusion | flops 68 | bytes 544 | tf_op jit(solution)/shard_map/concatenate | solution.py:420
  14.2 4.0 %shard_map.149.refs_10_ = bf16[4,8192,128]{2,1,0:T(8,128)(2,1)S(1)} custom-call(s32[68]{0:T(128)S(1)} %pad_add_fusion.whole_ref.refs_6_, bf16[64,512,128]{2,1,0:T(8,128)(2,1)} %bitcast.27), custom_call_target="tpu_custom_call" | custom-call | tf_op jit(solution)/shard_map/pallas_call | solution.py:261
  18.2 0.5 collective-permute-start.3
  18.8 8.1 %collective-permute-start.9 = (bf16[2,464,128]{2,1,0:T(8,128)(2,1)S(1)}, bf16[2,464,128]{2,1,0:T(8,128)(2,1)S(1)}, u32[]{:S(2)}, u32[]{:S(2)}) collective-permute-start(bf16[2,464,128]{2,1,0:T(8,128)(2,1)S(1)} %get-tuple-element.48), channel_id=1, source_target_pairs={{0,12},{1,13},{2,14},{3,15},{16,28},{17,29},{18,30},{19,31},{32,44... | collective-permute-start | bytes 712712 | tf_op jit(solution)/shard_map/ppermute | solution.py:42
  27.1 0.4 collective-permute-start.10
  27.5 10.9 %collective-permute-start.11 = (bf16[656,256]{1,0:T(8,128)(2,1)S(1)}, bf16[656,256]{1,0:T(8,128)(2,1)S(1)}, u32[]{:S(2)}, u32[]{:S(2)}) collective-permute-start(bf16[656,256]{1,0:T(8,128)(2,1)S(1)} %slice.37.refs_0_), channel_id=1, source_target_pairs={{0,64},{1,65},{2,66},{3,67},{16,80},{17,81},{18,82},{19,83},{32,96... | collective-permute-start | bytes 1007624 | tf_op jit(solution)/shard_map/ppermute | solution.py:42
  38.4 1.0 %collective-permute-start.7 = (bf16[2,464,128]{2,1,0:T(8,128)(2,1)S(1)}, bf16[2,464,128]{2,1,0:T(8,128)(2,1)S(1)}, u32[]{:S(2)}, u32[]{:S(2)}) collective-permute-start(bf16[2,464,128]{2,1,0:T(8,128)(2,1)S(1)} %get-tuple-element.48), channel_id=1, source_target_pairs={{0,4},{1,5},{2,6},{3,7},{16,20},{17,21},{18,22},{19,23},{32,36},{3... | collective-permute-start | bytes 712712 | tf_op jit(solution)/shard_map/ppermute | solution.py:42
  39.4 1.6 %collective-permute-start.8 = (bf16[2,464,128]{2,1,0:T(8,128)(2,1)S(1)}, bf16[2,464,128]{2,1,0:T(8,128)(2,1)S(1)}, u32[]{:S(2)}, u32[]{:S(2)}) collective-permute-start(bf16[2,464,128]{2,1,0:T(8,128)(2,1)S(1)} %get-tuple-element.48), channel_id=1, source_target_pairs={{0,8},{1,9},{2,10},{3,11},{16,24},{17,25},{18,26},{19,27},{32,40},... | collective-permute-start | bytes 712712 | tf_op jit(solution)/shard_map/ppermute | solution.py:42
  40.9 3.0 %collective-permute-done.10.refs_1_ = bf16[656,256]{1,0:T(8,128)(2,1)S(1)} collective-permute-done((bf16[656,256]{1,0:T(8,128)(2,1)S(1)}, bf16[656,256]{1,0:T(8,128)(2,1)S(1)}, u32[]{:S(2)}, u32[]{:S(2)}) %collective-permute-start.10) | collective-permute-done | bytes 335904 | tf_op jit(solution)/shard_map/ppermute | solution.py:42
  43.9 8.1 %collective-permute-done.11.refs_2_ = bf16[656,256]{1,0:T(8,128)(2,1)S(1)} collective-permute-done((bf16[656,256]{1,0:T(8,128)(2,1)S(1)}, bf16[656,256]{1,0:T(8,128)(2,1)S(1)}, u32[]{:S(2)}, u32[]{:S(2)}) %collective-permute-start.11) | collective-permute-done | bytes 335904 | tf_op jit(solution)/shard_map/ppermute | solution.py:42
  52.0 0.4 collective-permute-done.12.refs_3_
  52.5 2.1 %collective-permute-start.13 = (bf16[4,2,464,128]{3,2,1,0:T(8,128)(2,1)S(1)}, bf16[4,2,464,128]{3,2,1,0:T(8,128)(2,1)S(1)}, u32[]{:S(2)}, u32[]{:S(2)}) collective-permute-start(bf16[4,2,464,128]{3,2,1,0:T(8,128)(2,1)S(1)} %pad_maximum_fusion.refs_4_), channel_id=1, source_target_pairs={{0,1},{1,0},{2,3},{3,2},{16,17},{17,16},{18,19},{19,18},{32,33},{3... | collective-permute-start | bytes 2850824 | tf_op jit(solution)/shard_map/ppermute | solution.py:42
  54.9 3.0 %collective-permute-start.5 = (bf16[384,256]{1,0:T(8,128)(2,1)S(1)}, bf16[384,256]{1,0:T(8,128)(2,1)S(1)}, u32[]{:S(2)}, u32[]{:S(2)}) collective-permute-start(bf16[384,256]{1,0:T(8,128)(2,1)S(1)} %slice.36.refs_0_), channel_id=1, source_target_pairs={{0,64},{1,65},{2,66},{3,67},{16,80},{17,81},{18,82},{19,83},{32,96... | collective-permute-start | bytes 589832 | tf_op jit(solution)/shard_map/ppermute | solution.py:42
  58.0 8.5 %shard_map.150 = (bf16[640,128]{1,0:T(8,128)(2,1)S(1)}, bf16[16,128]{1,0:T(8,128)(2,1)S(1)}, f32[128,128]{1,0:T(8,128)S(1)}, f32[128,128]{1,0:T(8,128)S(1)}) custom-call(bf16[656,256]{1,0:T(8,128)(2,1)S(1)} %slice.37.refs_0_, bf16[656,256]{1,0:T(8,128)(2,1)S(1)} %collective-permute-done.10.refs_1_, bf16[656,256]{1,0:T(8,128)(2,1)S(1)} %collective-permute-done.11.refs_2_, ...), custom_call_target="tpu_custom_call" | custom-call | tf_op jit(solution)/shard_map/pallas_call | solution.py:272
  66.5 0.6 collective-permute-done.5.refs_2_
  67.1 3.9 %shard_map.151 = (bf16[1028,128]{1,0:T(8,128)(2,1)}, f32[128,128]{1,0:T(8,128)}, f32[128,128]{1,0:T(8,128)}) custom-call(bf16[384,256]{1,0:T(8,128)(2,1)S(1)} %slice.36.refs_0_, bf16[384,256]{1,0:T(8,128)(2,1)S(1)} %collective-permute-done.4.refs_1_, bf16[384,256]{1,0:T(8,128)(2,1)S(1)} %collective-permute-done.5.refs_2_, ...), custom_call_target="tpu_custom_call" | custom-call | tf_op jit(solution)/shard_map/pallas_call | solution.py:299
  (44 shorter events, 1.2 us)
Async XLA Ops:
  2.2 2.7 %collective-permute-start.1 = (bf16[1028,64]{1,0:T(8,128)(2,1)S(1)}, bf16[1028,64]{1,0:T(8,128)(2,1)S(1)}, u32[]{:S(2)}, u32[]{:S(2)}) collective-permute-start(bf16[1028,64]{1,0:T(8,128)(2,1)S(1)} %get-tuple-element.44), channel_id=1, source_target_pairs={{0,1},{1,0},{2,3},{3,2},{16,17},{17,16},{18,19},{19,18},{32,33},{3... | collective-permute-start | bytes 394760 | tf_op jit(solution)/shard_map/ppermute | solution.py:42
  5.1 13.1 %collective-permute-start.2 = (bf16[1040,128]{1,0:T(8,128)(2,1)S(1)}, bf16[1040,128]{1,0:T(8,128)(2,1)S(1)}, u32[]{:S(2)}, u32[]{:S(2)}) collective-permute-start(bf16[1040,128]{1,0:T(8,128)(2,1)S(1)} %fusion.3), channel_id=1, source_target_pairs={{0,0},{1,1},{2,16},{3,17},{16,2},{17,3},{18,18},{19,19},{32,36},{3... | collective-permute-start | bytes 798728 | tf_op jit(solution)/shard_map/ppermute | solution.py:42
  8.0 10.2 %collective-permute-start = (bf16[464,128]{1,0:T(8,128)(2,1)}, bf16[464,128]{1,0:T(8,128)(2,1)S(1)}, u32[]{:S(2)}, u32[]{:S(2)}) collective-permute-start(bf16[464,128]{1,0:T(8,128)(2,1)} %shard_map.148), channel_id=1, source_target_pairs={{0,2},{1,3},{2,0},{3,1},{16,18},{17,19},{18,16},{19,17},{32,34},{3... | collective-permute-start | bytes 356360 | tf_op jit(solution)/shard_map/ppermute | solution.py:42
  14.1 4.6 %copy-start = (bf16[464,128]{1,0:T(8,128)(2,1)S(1)}, bf16[464,128]{1,0:T(8,128)(2,1)}, u32[]{:S(2)}) copy-start(bf16[464,128]{1,0:T(8,128)(2,1)} %shard_map.148) | copy-start | bytes 356356
  14.1 40.5 %copy-start.2 = (bf16[16,2,128]{2,1,0:T(2,128)(2,1)S(1)}, bf16[16,2,128]{2,1,0:T(2,128)(2,1)}, u32[]{:S(2)}) copy-start(bf16[16,2,128]{2,1,0:T(2,128)(2,1)} %param.15) | copy-start | bytes 24580
  14.1 40.6 %copy-start.1 = (f32[4,1,128,128]{3,2,1,0:T(8,128)S(1)}, f32[4,1,128,128]{3,2,1,0:T(8,128)}, u32[]{:S(2)}) copy-start(f32[4,1,128,128]{3,2,1,0:T(8,128)} %param.25) | copy-start | bytes 786436
  14.1 43.8 %copy-start.3 = (f32[1,1,16]{2,1,0:T(1,128)S(1)}, f32[1,1,16]{2,1,0:T(1,128)}, u32[]{:S(2)}) copy-start(f32[1,1,16]{2,1,0:T(1,128)} %param.24) | copy-start | bytes 196
  14.1 43.8 %copy-start.4 = (f32[1,1,16]{2,1,0:T(1,128)S(1)}, f32[1,1,16]{2,1,0:T(1,128)}, u32[]{:S(2)}) copy-start(f32[1,1,16]{2,1,0:T(1,128)} %param.23) | copy-start | bytes 196
  14.1 43.8 %copy-start.5 = (f32[1,1,16]{2,1,0:T(1,128)S(1)}, f32[1,1,16]{2,1,0:T(1,128)}, u32[]{:S(2)}) copy-start(f32[1,1,16]{2,1,0:T(1,128)} %param.22) | copy-start | bytes 196
  18.2 8.7 %collective-permute-start.3 = (bf16[1040,128]{1,0:T(8,128)(2,1)S(1)}, bf16[1040,128]{1,0:T(8,128)(2,1)S(1)}, u32[]{:S(2)}, u32[]{:S(2)}) collective-permute-start(bf16[1040,128]{1,0:T(8,128)(2,1)S(1)} %collective-permute-done.2), channel_id=1, source_target_pairs={{0,16},{1,17},{2,18},{3,19},{16,0},{17,1},{18,2},{19,3},{32,48},{3... | collective-permute-start | bytes 798728 | tf_op jit(solution)/shard_map/ppermute | solution.py:42
  18.8 20.6 %collective-permute-start.9 = (bf16[2,464,128]{2,1,0:T(8,128)(2,1)S(1)}, bf16[2,464,128]{2,1,0:T(8,128)(2,1)S(1)}, u32[]{:S(2)}, u32[]{:S(2)}) collective-permute-start(bf16[2,464,128]{2,1,0:T(8,128)(2,1)S(1)} %get-tuple-element.48), channel_id=1, source_target_pairs={{0,12},{1,13},{2,14},{3,15},{16,28},{17,29},{18,30},{19,31},{32,44... | collective-permute-start | bytes 712712 | tf_op jit(solution)/shard_map/ppermute | solution.py:42
  27.1 16.8 %collective-permute-start.10 = (bf16[656,256]{1,0:T(8,128)(2,1)S(1)}, bf16[656,256]{1,0:T(8,128)(2,1)S(1)}, u32[]{:S(2)}, u32[]{:S(2)}) collective-permute-start(bf16[656,256]{1,0:T(8,128)(2,1)S(1)} %slice.37.refs_0_), channel_id=1, source_target_pairs={{0,32},{1,33},{2,34},{3,35},{16,48},{17,49},{18,50},{19,51},{32,64... | collective-permute-start | bytes 1007624 | tf_op jit(solution)/shard_map/ppermute | solution.py:42
  27.5 24.5 %collective-permute-start.11 = (bf16[656,256]{1,0:T(8,128)(2,1)S(1)}, bf16[656,256]{1,0:T(8,128)(2,1)S(1)}, u32[]{:S(2)}, u32[]{:S(2)}) collective-permute-start(bf16[656,256]{1,0:T(8,128)(2,1)S(1)} %slice.37.refs_0_), channel_id=1, source_target_pairs={{0,64},{1,65},{2,66},{3,67},{16,80},{17,81},{18,82},{19,83},{32,96... | collective-permute-start | bytes 1007624 | tf_op jit(solution)/shard_map/ppermute | solution.py:42
  38.4 14.0 %collective-permute-start.12 = (bf16[656,256]{1,0:T(8,128)(2,1)S(1)}, bf16[656,256]{1,0:T(8,128)(2,1)S(1)}, u32[]{:S(2)}, u32[]{:S(2)}) collective-permute-start(bf16[656,256]{1,0:T(8,128)(2,1)S(1)} %slice.37.refs_0_), channel_id=1, source_target_pairs={{0,96},{1,97},{2,98},{3,99},{16,112},{17,113},{18,114},{19,115},{3... | collective-permute-start | bytes 1007624 | tf_op jit(solution)/shard_map/ppermute | solution.py:42
  38.4 14.0 %collective-permute-start.7 = (bf16[2,464,128]{2,1,0:T(8,128)(2,1)S(1)}, bf16[2,464,128]{2,1,0:T(8,128)(2,1)S(1)}, u32[]{:S(2)}, u32[]{:S(2)}) collective-permute-start(bf16[2,464,128]{2,1,0:T(8,128)(2,1)S(1)} %get-tuple-element.48), channel_id=1, source_target_pairs={{0,4},{1,5},{2,6},{3,7},{16,20},{17,21},{18,22},{19,23},{32,36},{3... | collective-permute-start | bytes 712712 | tf_op jit(solution)/shard_map/ppermute | solution.py:42
  39.4 13.1 %collective-permute-start.8 = (bf16[2,464,128]{2,1,0:T(8,128)(2,1)S(1)}, bf16[2,464,128]{2,1,0:T(8,128)(2,1)S(1)}, u32[]{:S(2)}, u32[]{:S(2)}) collective-permute-start(bf16[2,464,128]{2,1,0:T(8,128)(2,1)S(1)} %get-tuple-element.48), channel_id=1, source_target_pairs={{0,8},{1,9},{2,10},{3,11},{16,24},{17,25},{18,26},{19,27},{32,40},... | collective-permute-start | bytes 712712 | tf_op jit(solution)/shard_map/ppermute | solution.py:42
  52.5 5.5 %collective-permute-start.13 = (bf16[4,2,464,128]{3,2,1,0:T(8,128)(2,1)S(1)}, bf16[4,2,464,128]{3,2,1,0:T(8,128)(2,1)S(1)}, u32[]{:S(2)}, u32[]{:S(2)}) collective-permute-start(bf16[4,2,464,128]{3,2,1,0:T(8,128)(2,1)S(1)} %pad_maximum_fusion.refs_4_), channel_id=1, source_target_pairs={{0,1},{1,0},{2,3},{3,2},{16,17},{17,16},{18,19},{19,18},{32,33},{3... | collective-permute-start | bytes 2850824 | tf_op jit(solution)/shard_map/ppermute | solution.py:42
  54.8 11.7 %collective-permute-start.4 = (bf16[384,256]{1,0:T(8,128)(2,1)S(1)}, bf16[384,256]{1,0:T(8,128)(2,1)S(1)}, u32[]{:S(2)}, u32[]{:S(2)}) collective-permute-start(bf16[384,256]{1,0:T(8,128)(2,1)S(1)} %slice.36.refs_0_), channel_id=1, source_target_pairs={{0,32},{1,33},{2,34},{3,35},{16,48},{17,49},{18,50},{19,51},{32,64... | collective-permute-start | bytes 589832 | tf_op jit(solution)/shard_map/ppermute | solution.py:42
  54.9 12.2 %collective-permute-start.5 = (bf16[384,256]{1,0:T(8,128)(2,1)S(1)}, bf16[384,256]{1,0:T(8,128)(2,1)S(1)}, u32[]{:S(2)}, u32[]{:S(2)}) collective-permute-start(bf16[384,256]{1,0:T(8,128)(2,1)S(1)} %slice.36.refs_0_), channel_id=1, source_target_pairs={{0,64},{1,65},{2,66},{3,67},{16,80},{17,81},{18,82},{19,83},{32,96... | collective-permute-start | bytes 589832 | tf_op jit(solution)/shard_map/ppermute | solution.py:42
  57.9 9.2 %collective-permute-start.6 = (bf16[384,256]{1,0:T(8,128)(2,1)S(1)}, bf16[384,256]{1,0:T(8,128)(2,1)S(1)}, u32[]{:S(2)}, u32[]{:S(2)}) collective-permute-start(bf16[384,256]{1,0:T(8,128)(2,1)S(1)} %slice.36.refs_0_), channel_id=1, source_target_pairs={{0,96},{1,97},{2,98},{3,99},{16,112},{17,113},{18,114},{19,115},{3... | collective-permute-start | bytes 589832 | tf_op jit(solution)/shard_map/ppermute | solution.py:42

commit v6 on v5

--- a/solution.py
+++ b/solution.py
@@ -64,7 +64,7 @@
     return lax.rsqrt(jnp.sum(wide * wide, axis=-1, keepdims=True) + EPSILON)
 
 
-HALF = 640
+HALF = 704
 REST = PCH - HALF
 EXTRA = PADDED - PCH
 STATE = 3 * MCH

time: 71.2 us -> 72.3 us (1.015)
  waiting for transfers between devices: 13.3 us -> 14.1 us
    ppermute x14, waiting for transfers between devices: 13.3 us -> 14.1 us  [permute(): return lax.ppermute(values, ('row', 'col'), moves(target))]
  transfers between devices with their start and end apart: 14 -> 14, of which waited for: 5 -> 4; matrix products, arithmetic and copies ran while one was open for 3% -> 3% of each run, Pallas kernels for 20% -> 20%
where the time goes in v6:
time: 72.3 us; the launch traced here: 72.1 us
  starting transfers between devices  34.5 us (48%)
  Pallas kernels  18.3 us (25%)
  waiting for transfers between devices  14.1 us (20%)
  local copies, waits for them, and re-layouts  2.44 us (3%)
  between operations  1.55 us (2%)
  other arithmetic  1.33 us (2%)
    ppermute x14, starting transfers between devices, permute(): return lax.ppermute(values, ('row', 'col'), moves(target))  34.5 us
    ppermute x14, waiting for transfers between devices, permute(): return lax.ppermute(values, ('row', 'col'), moves(target))  14.1 us
    pallas_call x1, Pallas kernels, first_part(): pl.pallas_call(first_kernel, out_shape=(jax.ShapeDtypeStruct((HALF, HD),...  9.06 us
    pallas_call x1, Pallas kernels, order_pages(): pl.pallas_call(page_kernel, out_shape=jax.ShapeDtypeStruct((DEC_DEV, 2 *...  4.03 us
    pallas_call x1, Pallas kernels, second_part(): pl.pallas_call(second_kernel, out_shape=(jax.ShapeDtypeStruct((ROWS, HD),...  3.6 us
    pallas_call x1, Pallas kernels, make_packet(): pl.pallas_call(packet_kernel, out_shape=jax.ShapeDtypeStruct((PACKET, HD)...  1.56 us
  transfers between devices with their start and end apart: 14, of which 4 were waited for; matrix products, arithmetic and copies ran while one was open for 3% of the time, Pallas kernels for 20%

profile of v6, /device:TPU:1, one launch (start us, length us, event | category | flops | bytes accessed | tf_op | source)
XLA Modules:
  0.0 72.1 jit_solution(12920545140844649845)
XLA Ops:
  0.6 1.1 %fusion.6 = (bf16[1028,64]{0,1:T(8,128)(2,1)S(1)}, bf16[1028,64]{0,1:T(8,128)(2,1)S(1)}) fusion(bf16[2056,64]{0,1:T(8,128)(2,1)} %param.13), kind=kLoop, calls=%fused_computation.25 | loop fusion | bytes 526336 | tf_op jit(solution)/shard_map/slice | solution.py:386
  1.7 0.2 copy.20
  1.9 0.2 copy.21
  2.2 1.5 %collective-permute-start.1 = (bf16[1028,64]{1,0:T(8,128)(2,1)S(1)}, bf16[1028,64]{1,0:T(8,128)(2,1)S(1)}, u32[]{:S(2)}, u32[]{:S(2)}) collective-permute-start(bf16[1028,64]{1,0:T(8,128)(2,1)S(1)} %get-tuple-element.44), channel_id=1, source_target_pairs={{0,1},{1,0},{2,3},{3,2},{16,17},{17,16},{18,19},{19,18},{32,33},{3... | collective-permute-start | bytes 394760 | tf_op jit(solution)/shard_map/ppermute | solution.py:42
  3.7 1.2 %collective-permute-done.1 = bf16[1028,64]{1,0:T(8,128)(2,1)S(1)} collective-permute-done((bf16[1028,64]{1,0:T(8,128)(2,1)S(1)}, bf16[1028,64]{1,0:T(8,128)(2,1)S(1)}, u32[]{:S(2)}, u32[]{:S(2)}) %collective-permute-start.1) | collective-permute-done | bytes 131616 | tf_op jit(solution)/shard_map/ppermute | solution.py:42
  5.1 0.7 collective-permute-start.2
  6.5 1.6 %shard_map.148 = bf16[464,128]{1,0:T(8,128)(2,1)} custom-call(s32[1]{0:T(128)S(6)} %copy.23.destination_ref, bf16[64,384]{1,0:T(8,128)(2,1)} %weight_ref.1, f32[128,128]{1,0:T(8,128)} %bitcast.31, f32[128,128]{1,0:T(8,128)} %bitcast.32), custom_call_target="tpu_custom_call" | custom-call | tf_op jit(solution)/shard_map/pallas_call | solution.py:339
  8.0 4.6 %collective-permute-start = (bf16[464,128]{1,0:T(8,128)(2,1)}, bf16[464,128]{1,0:T(8,128)(2,1)S(1)}, u32[]{:S(2)}, u32[]{:S(2)}) collective-permute-start(bf16[464,128]{1,0:T(8,128)(2,1)} %shard_map.148), channel_id=1, source_target_pairs={{0,2},{1,3},{2,0},{3,1},{16,18},{17,19},{18,16},{19,17},{32,34},{3... | collective-permute-start | bytes 356360 | tf_op jit(solution)/shard_map/ppermute | solution.py:42
  12.6 0.8 %reshape.32 = s32[64]{0:T(128)S(1)} reshape(s32[4,16]{1,0:T(4,128)} %param.17) | data formatting | bytes 512 | tf_op jit(solution)/shard_map/reshape | solution.py:420
  13.4 0.7 %pad_add_fusion.whole_ref.refs_6_ = s32[68]{0:T(128)S(1)} fusion(s32[4]{0:T(128)} %param.18, s32[64]{0:T(128)S(1)} %reshape.32), kind=kLoop, calls=%fused_computation.22 | loop fusion | flops 68 | bytes 544 | tf_op jit(solution)/shard_map/concatenate | solution.py:420
  14.2 4.0 %shard_map.149.refs_10_ = bf16[4,8192,128]{2,1,0:T(8,128)(2,1)S(1)} custom-call(s32[68]{0:T(128)S(1)} %pad_add_fusion.whole_ref.refs_6_, bf16[64,512,128]{2,1,0:T(8,128)(2,1)} %bitcast.27), custom_call_target="tpu_custom_call" | custom-call | tf_op jit(solution)/shard_map/pallas_call | solution.py:261
  18.2 0.5 collective-permute-start.3
  18.8 8.1 %collective-permute-start.9 = (bf16[2,464,128]{2,1,0:T(8,128)(2,1)S(1)}, bf16[2,464,128]{2,1,0:T(8,128)(2,1)S(1)}, u32[]{:S(2)}, u32[]{:S(2)}) collective-permute-start(bf16[2,464,128]{2,1,0:T(8,128)(2,1)S(1)} %get-tuple-element.48), channel_id=1, source_target_pairs={{0,12},{1,13},{2,14},{3,15},{16,28},{17,29},{18,30},{19,31},{32,44... | collective-permute-start | bytes 712712 | tf_op jit(solution)/shard_map/ppermute | solution.py:42
  27.1 0.4 collective-permute-start.10
  27.5 10.9 %collective-permute-start.11 = (bf16[720,256]{1,0:T(8,128)(2,1)S(1)}, bf16[720,256]{1,0:T(8,128)(2,1)S(1)}, u32[]{:S(2)}, u32[]{:S(2)}) collective-permute-start(bf16[720,256]{1,0:T(8,128)(2,1)S(1)} %slice.37.refs_0_), channel_id=1, source_target_pairs={{0,64},{1,65},{2,66},{3,67},{16,80},{17,81},{18,82},{19,83},{32,96... | collective-permute-start | bytes 1105928 | tf_op jit(solution)/shard_map/ppermute | solution.py:42
  38.4 1.0 %collective-permute-start.7 = (bf16[2,464,128]{2,1,0:T(8,128)(2,1)S(1)}, bf16[2,464,128]{2,1,0:T(8,128)(2,1)S(1)}, u32[]{:S(2)}, u32[]{:S(2)}) collective-permute-start(bf16[2,464,128]{2,1,0:T(8,128)(2,1)S(1)} %get-tuple-element.48), channel_id=1, source_target_pairs={{0,4},{1,5},{2,6},{3,7},{16,20},{17,21},{18,22},{19,23},{32,36},{3... | collective-permute-start | bytes 712712 | tf_op jit(solution)/shard_map/ppermute | solution.py:42
  39.4 1.6 %collective-permute-start.8 = (bf16[2,464,128]{2,1,0:T(8,128)(2,1)S(1)}, bf16[2,464,128]{2,1,0:T(8,128)(2,1)S(1)}, u32[]{:S(2)}, u32[]{:S(2)}) collective-permute-start(bf16[2,464,128]{2,1,0:T(8,128)(2,1)S(1)} %get-tuple-element.48), channel_id=1, source_target_pairs={{0,8},{1,9},{2,10},{3,11},{16,24},{17,25},{18,26},{19,27},{32,40},... | collective-permute-start | bytes 712712 | tf_op jit(solution)/shard_map/ppermute | solution.py:42
  40.9 3.7 %collective-permute-done.10.refs_1_ = bf16[720,256]{1,0:T(8,128)(2,1)S(1)} collective-permute-done((bf16[720,256]{1,0:T(8,128)(2,1)S(1)}, bf16[720,256]{1,0:T(8,128)(2,1)S(1)}, u32[]{:S(2)}, u32[]{:S(2)}) %collective-permute-start.10) | collective-permute-done | bytes 368672 | tf_op jit(solution)/shard_map/ppermute | solution.py:42
  44.6 8.8 %collective-permute-done.11.refs_2_ = bf16[720,256]{1,0:T(8,128)(2,1)S(1)} collective-permute-done((bf16[720,256]{1,0:T(8,128)(2,1)S(1)}, bf16[720,256]{1,0:T(8,128)(2,1)S(1)}, u32[]{:S(2)}, u32[]{:S(2)}) %collective-permute-start.11) | collective-permute-done | bytes 368672 | tf_op jit(solution)/shard_map/ppermute | solution.py:42
  53.4 0.4 collective-permute-done.12.refs_3_
  53.9 2.1 %collective-permute-start.13 = (bf16[4,2,464,128]{3,2,1,0:T(8,128)(2,1)S(1)}, bf16[4,2,464,128]{3,2,1,0:T(8,128)(2,1)S(1)}, u32[]{:S(2)}, u32[]{:S(2)}) collective-permute-start(bf16[4,2,464,128]{3,2,1,0:T(8,128)(2,1)S(1)} %pad_maximum_fusion.refs_4_), channel_id=1, source_target_pairs={{0,1},{1,0},{2,3},{3,2},{16,17},{17,16},{18,19},{19,18},{32,33},{3... | collective-permute-start | bytes 2850824 | tf_op jit(solution)/shard_map/ppermute | solution.py:42
  56.2 3.0 %collective-permute-start.5 = (bf16[320,256]{1,0:T(8,128)(2,1)S(1)}, bf16[320,256]{1,0:T(8,128)(2,1)S(1)}, u32[]{:S(2)}, u32[]{:S(2)}) collective-permute-start(bf16[320,256]{1,0:T(8,128)(2,1)S(1)} %slice.36.refs_0_), channel_id=1, source_target_pairs={{0,64},{1,65},{2,66},{3,67},{16,80},{17,81},{18,82},{19,83},{32,96... | collective-permute-start | bytes 491528 | tf_op jit(solution)/shard_map/ppermute | solution.py:42
  59.4 9.1 %shard_map.150 = (bf16[704,128]{1,0:T(8,128)(2,1)S(1)}, bf16[16,128]{1,0:T(8,128)(2,1)S(1)}, f32[128,128]{1,0:T(8,128)S(1)}, f32[128,128]{1,0:T(8,128)S(1)}) custom-call(bf16[720,256]{1,0:T(8,128)(2,1)S(1)} %slice.37.refs_0_, bf16[720,256]{1,0:T(8,128)(2,1)S(1)} %collective-permute-done.10.refs_1_, bf16[720,256]{1,0:T(8,128)(2,1)S(1)} %collective-permute-done.11.refs_2_, ...), custom_call_target="tpu_custom_call" | custom-call | tf_op jit(solution)/shard_map/pallas_call | solution.py:272
  68.5 3.6 %shard_map.151 = (bf16[1028,128]{1,0:T(8,128)(2,1)}, f32[128,128]{1,0:T(8,128)}, f32[128,128]{1,0:T(8,128)}) custom-call(bf16[320,256]{1,0:T(8,128)(2,1)S(1)} %slice.36.refs_0_, bf16[320,256]{1,0:T(8,128)(2,1)S(1)} %collective-permute-done.4.refs_1_, bf16[320,256]{1,0:T(8,128)(2,1)S(1)} %collective-permute-done.5.refs_2_, ...), custom_call_target="tpu_custom_call" | custom-call | tf_op jit(solution)/shard_map/pallas_call | solution.py:299
  (44 shorter events, 0.9 us)
Async XLA Ops:
  2.2 2.7 %collective-permute-start.1 = (bf16[1028,64]{1,0:T(8,128)(2,1)S(1)}, bf16[1028,64]{1,0:T(8,128)(2,1)S(1)}, u32[]{:S(2)}, u32[]{:S(2)}) collective-permute-start(bf16[1028,64]{1,0:T(8,128)(2,1)S(1)} %get-tuple-element.44), channel_id=1, source_target_pairs={{0,1},{1,0},{2,3},{3,2},{16,17},{17,16},{18,19},{19,18},{32,33},{3... | collective-permute-start | bytes 394760 | tf_op jit(solution)/shard_map/ppermute | solution.py:42
  5.1 13.1 %collective-permute-start.2 = (bf16[1040,128]{1,0:T(8,128)(2,1)S(1)}, bf16[1040,128]{1,0:T(8,128)(2,1)S(1)}, u32[]{:S(2)}, u32[]{:S(2)}) collective-permute-start(bf16[1040,128]{1,0:T(8,128)(2,1)S(1)} %fusion.3), channel_id=1, source_target_pairs={{0,0},{1,1},{2,16},{3,17},{16,2},{17,3},{18,18},{19,19},{32,36},{3... | collective-permute-start | bytes 798728 | tf_op jit(solution)/shard_map/ppermute | solution.py:42
  8.0 10.2 %collective-permute-start = (bf16[464,128]{1,0:T(8,128)(2,1)}, bf16[464,128]{1,0:T(8,128)(2,1)S(1)}, u32[]{:S(2)}, u32[]{:S(2)}) collective-permute-start(bf16[464,128]{1,0:T(8,128)(2,1)} %shard_map.148), channel_id=1, source_target_pairs={{0,2},{1,3},{2,0},{3,1},{16,18},{17,19},{18,16},{19,17},{32,34},{3... | collective-permute-start | bytes 356360 | tf_op jit(solution)/shard_map/ppermute | solution.py:42
  14.1 4.6 %copy-start = (bf16[464,128]{1,0:T(8,128)(2,1)S(1)}, bf16[464,128]{1,0:T(8,128)(2,1)}, u32[]{:S(2)}) copy-start(bf16[464,128]{1,0:T(8,128)(2,1)} %shard_map.148) | copy-start | bytes 356356
  14.1 41.9 %copy-start.2 = (bf16[16,2,128]{2,1,0:T(2,128)(2,1)S(1)}, bf16[16,2,128]{2,1,0:T(2,128)(2,1)}, u32[]{:S(2)}) copy-start(bf16[16,2,128]{2,1,0:T(2,128)(2,1)} %param.15) | copy-start | bytes 24580
  14.1 42.0 %copy-start.1 = (f32[4,1,128,128]{3,2,1,0:T(8,128)S(1)}, f32[4,1,128,128]{3,2,1,0:T(8,128)}, u32[]{:S(2)}) copy-start(f32[4,1,128,128]{3,2,1,0:T(8,128)} %param.25) | copy-start | bytes 786436
  14.1 45.2 %copy-start.3 = (f32[1,1,16]{2,1,0:T(1,128)S(1)}, f32[1,1,16]{2,1,0:T(1,128)}, u32[]{:S(2)}) copy-start(f32[1,1,16]{2,1,0:T(1,128)} %param.24) | copy-start | bytes 196
  14.1 45.2 %copy-start.4 = (f32[1,1,16]{2,1,0:T(1,128)S(1)}, f32[1,1,16]{2,1,0:T(1,128)}, u32[]{:S(2)}) copy-start(f32[1,1,16]{2,1,0:T(1,128)} %param.23) | copy-start | bytes 196
  14.1 45.2 %copy-start.5 = (f32[1,1,16]{2,1,0:T(1,128)S(1)}, f32[1,1,16]{2,1,0:T(1,128)}, u32[]{:S(2)}) copy-start(f32[1,1,16]{2,1,0:T(1,128)} %param.22) | copy-start | bytes 196
  18.2 8.7 %collective-permute-start.3 = (bf16[1040,128]{1,0:T(8,128)(2,1)S(1)}, bf16[1040,128]{1,0:T(8,128)(2,1)S(1)}, u32[]{:S(2)}, u32[]{:S(2)}) collective-permute-start(bf16[1040,128]{1,0:T(8,128)(2,1)S(1)} %collective-permute-done.2), channel_id=1, source_target_pairs={{0,16},{1,17},{2,18},{3,19},{16,0},{17,1},{18,2},{19,3},{32,48},{3... | collective-permute-start | bytes 798728 | tf_op jit(solution)/shard_map/ppermute | solution.py:42
  18.8 20.6 %collective-permute-start.9 = (bf16[2,464,128]{2,1,0:T(8,128)(2,1)S(1)}, bf16[2,464,128]{2,1,0:T(8,128)(2,1)S(1)}, u32[]{:S(2)}, u32[]{:S(2)}) collective-permute-start(bf16[2,464,128]{2,1,0:T(8,128)(2,1)S(1)} %get-tuple-element.48), channel_id=1, source_target_pairs={{0,12},{1,13},{2,14},{3,15},{16,28},{17,29},{18,30},{19,31},{32,44... | collective-permute-start | bytes 712712 | tf_op jit(solution)/shard_map/ppermute | solution.py:42
  27.1 17.5 %collective-permute-start.10 = (bf16[720,256]{1,0:T(8,128)(2,1)S(1)}, bf16[720,256]{1,0:T(8,128)(2,1)S(1)}, u32[]{:S(2)}, u32[]{:S(2)}) collective-permute-start(bf16[720,256]{1,0:T(8,128)(2,1)S(1)} %slice.37.refs_0_), channel_id=1, source_target_pairs={{0,32},{1,33},{2,34},{3,35},{16,48},{17,49},{18,50},{19,51},{32,64... | collective-permute-start | bytes 1105928 | tf_op jit(solution)/shard_map/ppermute | solution.py:42
  27.5 25.9 %collective-permute-start.11 = (bf16[720,256]{1,0:T(8,128)(2,1)S(1)}, bf16[720,256]{1,0:T(8,128)(2,1)S(1)}, u32[]{:S(2)}, u32[]{:S(2)}) collective-permute-start(bf16[720,256]{1,0:T(8,128)(2,1)S(1)} %slice.37.refs_0_), channel_id=1, source_target_pairs={{0,64},{1,65},{2,66},{3,67},{16,80},{17,81},{18,82},{19,83},{32,96... | collective-permute-start | bytes 1105928 | tf_op jit(solution)/shard_map/ppermute | solution.py:42
  38.4 15.4 %collective-permute-start.12 = (bf16[720,256]{1,0:T(8,128)(2,1)S(1)}, bf16[720,256]{1,0:T(8,128)(2,1)S(1)}, u32[]{:S(2)}, u32[]{:S(2)}) collective-permute-start(bf16[720,256]{1,0:T(8,128)(2,1)S(1)} %slice.37.refs_0_), channel_id=1, source_target_pairs={{0,96},{1,97},{2,98},{3,99},{16,112},{17,113},{18,114},{19,115},{3... | collective-permute-start | bytes 1105928 | tf_op jit(solution)/shard_map/ppermute | solution.py:42
  38.4 15.4 %collective-permute-start.7 = (bf16[2,464,128]{2,1,0:T(8,128)(2,1)S(1)}, bf16[2,464,128]{2,1,0:T(8,128)(2,1)S(1)}, u32[]{:S(2)}, u32[]{:S(2)}) collective-permute-start(bf16[2,464,128]{2,1,0:T(8,128)(2,1)S(1)} %get-tuple-element.48), channel_id=1, source_target_pairs={{0,4},{1,5},{2,6},{3,7},{16,20},{17,21},{18,22},{19,23},{32,36},{3... | collective-permute-start | bytes 712712 | tf_op jit(solution)/shard_map/ppermute | solution.py:42
  39.4 14.5 %collective-permute-start.8 = (bf16[2,464,128]{2,1,0:T(8,128)(2,1)S(1)}, bf16[2,464,128]{2,1,0:T(8,128)(2,1)S(1)}, u32[]{:S(2)}, u32[]{:S(2)}) collective-permute-start(bf16[2,464,128]{2,1,0:T(8,128)(2,1)S(1)} %get-tuple-element.48), channel_id=1, source_target_pairs={{0,8},{1,9},{2,10},{3,11},{16,24},{17,25},{18,26},{19,27},{32,40},... | collective-permute-start | bytes 712712 | tf_op jit(solution)/shard_map/ppermute | solution.py:42
  53.9 5.5 %collective-permute-start.13 = (bf16[4,2,464,128]{3,2,1,0:T(8,128)(2,1)S(1)}, bf16[4,2,464,128]{3,2,1,0:T(8,128)(2,1)S(1)}, u32[]{:S(2)}, u32[]{:S(2)}) collective-permute-start(bf16[4,2,464,128]{3,2,1,0:T(8,128)(2,1)S(1)} %pad_maximum_fusion.refs_4_), channel_id=1, source_target_pairs={{0,1},{1,0},{2,3},{3,2},{16,17},{17,16},{18,19},{19,18},{32,33},{3... | collective-permute-start | bytes 2850824 | tf_op jit(solution)/shard_map/ppermute | solution.py:42
  56.2 12.3 %collective-permute-start.4 = (bf16[320,256]{1,0:T(8,128)(2,1)S(1)}, bf16[320,256]{1,0:T(8,128)(2,1)S(1)}, u32[]{:S(2)}, u32[]{:S(2)}) collective-permute-start(bf16[320,256]{1,0:T(8,128)(2,1)S(1)} %slice.36.refs_0_), channel_id=1, source_target_pairs={{0,32},{1,33},{2,34},{3,35},{16,48},{17,49},{18,50},{19,51},{32,64... | collective-permute-start | bytes 491528 | tf_op jit(solution)/shard_map/ppermute | solution.py:42
  56.2 12.3 %collective-permute-start.5 = (bf16[320,256]{1,0:T(8,128)(2,1)S(1)}, bf16[320,256]{1,0:T(8,128)(2,1)S(1)}, u32[]{:S(2)}, u32[]{:S(2)}) collective-permute-start(bf16[320,256]{1,0:T(8,128)(2,1)S(1)} %slice.36.refs_0_), channel_id=1, source_target_pairs={{0,64},{1,65},{2,66},{3,67},{16,80},{17,81},{18,82},{19,83},{32,96... | collective-permute-start | bytes 491528 | tf_op jit(solution)/shard_map/ppermute | solution.py:42
  59.3 9.2 %collective-permute-start.6 = (bf16[320,256]{1,0:T(8,128)(2,1)S(1)}, bf16[320,256]{1,0:T(8,128)(2,1)S(1)}, u32[]{:S(2)}, u32[]{:S(2)}) collective-permute-start(bf16[320,256]{1,0:T(8,128)(2,1)S(1)} %slice.36.refs_0_), channel_id=1, source_target_pairs={{0,96},{1,97},{2,98},{3,99},{16,112},{17,113},{18,114},{19,115},{3... | collective-permute-start | bytes 491528 | tf_op jit(solution)/shard_map/ppermute | solution.py:42
